TPU v7x, 512 devices: a whole 4x8x8 slice. The times are simulated.
512 devices in a mesh: segment: 4 (over z_lo), dp: 128 (over z_hi, y, x, core).
Axes of the slice: x: 4, y: 8, z: 8 (z_hi: 2, z_lo: 4; z = z_hi * 4 + z_lo), core: 2. Of those that a mesh axis runs over, the one named last changes fastest.
Arguments:
- hidden: bfloat16 [4, 256, 7168], P('segment', 'dp')
- head_weight: bfloat16 [65536, 7168], P(('segment', 'dp')), as said below
- target_ids: int32 [4, 256], P('segment', 'dp'), may hold values from 0 to 65535
- policy_logp: float32 [4, 256], P('segment', 'dp'), may hold values from -20 to -10
Outputs:
- ref_logp: float32 [4, 256], P('segment', 'dp')
- kl_term: float32 [4, 256], P('segment', 'dp')
Inputs may be any that keep to these rules, and one draw needn't show every extreme that they name: `head_weight`: each vocabulary row of the head is drawn on its own.
All inputs are finite; a program needn't handle non-finite values.
Results may differ from a plain program's by a relative error of at most 0.0006.
Values may be sent and summed in bfloat16 or wider, within the bound.
No kernel may reach another device: no remote copies, remote signals or barrier semaphores. Data moves between devices by JAX's collectives and lax.ppermute only.
A program may use at most 128 MiB of HBM per device.

v0:
```python
import jax
import jax.numpy as jnp
from jax import lax
from jax.sharding import PartitionSpec as P


def shifted(block, axis, distance):
    devices = range(lax.axis_size(axis))
    route = [((i - distance) % len(devices), i) for i in devices]
    return lax.ppermute(block, axis, route)


def local_stats(logits, columns, row_ids):
    maxima = jnp.max(logits, axis=-1)
    totals = jnp.sum(jnp.exp(logits - maxima[..., None]), axis=-1)
    picked = jnp.sum(jnp.where(row_ids[..., None] == columns, logits, 0.0), axis=-1)
    return (maxima, totals, picked)


def across_all(maxima, totals, picked):
    highest = lax.pmax(maxima, ("segment", "dp"))
    summed, gathered_pick = lax.psum(
        (totals * jnp.exp(maxima - highest), picked), ("segment", "dp")
    )
    merged = (highest, summed, gathered_pick)
    return merged


def finish(highest, totals, picked, policy_logp):
    ref_logp = picked - (highest + jnp.log(totals))
    log_ratio = ref_logp - policy_logp
    kl_term = jnp.minimum(jnp.exp(log_ratio) - log_ratio - 1.0, 10.0)
    return (ref_logp, kl_term)


def per_device(hidden, head_weight, target_ids, policy_logp):
    segment_count = lax.axis_size("segment")
    group_count = lax.axis_size("dp")
    segment_index = lax.axis_index("segment")
    group_index = lax.axis_index("dp")
    batches = hidden.shape[0]
    row_dev = hidden.shape[1]
    voc_dev = head_weight.shape[0]
    columns = (segment_index * group_count + group_index) * voc_dev + jnp.arange(
        voc_dev, dtype=jnp.int32
    )
    block, block_ids = (hidden, target_ids)
    shape_all = (batches * segment_count, row_dev * group_count)
    maxima = jnp.zeros(shape_all, jnp.float32)
    totals = jnp.zeros(shape_all, jnp.float32)
    picked = jnp.zeros(shape_all, jnp.float32)
    for offset in range(segment_count):
        if offset > 0:
            block, block_ids = shifted((block, block_ids), "segment", 1)
        gathered, gathered_ids = (
            lax.all_gather(block, "dp", axis=1, tiled=True),
            lax.all_gather(block_ids, "dp", axis=1, tiled=True),
        )
        logits = jnp.einsum(
            "grd,vd->grv", gathered, head_weight, preferred_element_type=jnp.float32
        )
        partial_value = local_stats(logits, columns, gathered_ids)
        anchor = (segment_index - offset) % segment_count * batches
        maxima = lax.dynamic_update_slice_in_dim(maxima, partial_value[0], anchor, 0)
        totals = lax.dynamic_update_slice_in_dim(totals, partial_value[1], anchor, 0)
        picked = lax.dynamic_update_slice_in_dim(picked, partial_value[2], anchor, 0)
    merged = across_all(maxima, totals, picked)
    first_batch = segment_index * batches
    merged = tuple((lax.dynamic_slice_in_dim(member, first_batch, batches, 0) for member in merged))
    first_row = group_index * row_dev
    highest, summed, chosen = tuple(
        (lax.dynamic_slice_in_dim(member, first_row, row_dev, 1) for member in merged)
    )
    return finish(highest, summed, chosen, policy_logp)


def solution(mesh):
    return jax.shard_map(
        per_device,
        mesh=mesh,
        in_specs=(
            P("segment", "dp", None),
            P(("segment", "dp"), None),
            P("segment", "dp"),
            P("segment", "dp"),
        ),
        out_specs=(P("segment", "dp"), P("segment", "dp")),
        check_vma=False,
    )
```

profile of v0, /device:TPU:1, one launch (start us, length us, event | category | flops | bytes accessed | tf_op | source)
XLA Modules:
  0.0 830.2 jit_solution(3139782764414474931)
XLA Ops:
  7.2 0.0 copy-start
  7.2 0.0 all-gather.5.cloned.1.call-start
  7.2 1.5 copy.8
  8.8 0.0 all-gather.5.cloned.1.call-update
  8.8 0.0 all-gather.7.cloned.1.call-start
  8.8 4.8 collective-permute-start.1
  13.7 5.4 collective-permute-done.1
  19.0 0.0 copy-start.1
  19.1 0.6 copy-done.1
  19.7 0.0 all-gather.7.cloned.1.call-update
  19.7 0.0 all-gather.9.cloned.1.call-start
  19.7 1.9 collective-permute-start.3
  21.7 5.0 collective-permute-done.3
  26.7 0.0 copy-start.2
  26.7 0.6 copy-done.2
  27.3 0.0 all-gather.9.cloned.1.call-update
  27.3 0.0 all-gather.11.cloned.1.call-start
  27.4 1.9 collective-permute-start.5
  29.3 5.0 collective-permute-done.5
  34.3 0.0 copy-start.3
  34.3 0.6 copy-done.3
  34.9 0.0 all-gather.11.cloned.1.call-update
  34.9 1.9 collective-permute-start
  36.9 1.3 dynamic-slice
  38.9 0.8 bitcast_dynamic-update-slice_fusion.3
  39.7 1.9 collective-permute-done
  41.5 1.9 collective-permute-start.2
  43.5 0.1 bitcast_dynamic-update-slice_fusion.2
  43.6 4.0 collective-permute-done.2
  47.6 1.9 collective-permute-start.4
  49.6 0.1 bitcast_dynamic-update-slice_fusion.1
  49.7 4.0 collective-permute-done.4
  53.7 0.1 bitcast_dynamic-update-slice_fusion
  53.8 32.7 %all-reduce.4 = (s32[256]{0:T(256)S(1)}, s32[256]{0:T(256)S(1)}, s32[256]{0:T(256)S(1)}, s32[256]{0:T(256)S(1)}) all-reduce(s32[256]{0:T(256)S(1)} %bitcast_dynamic-update-slice_fusion, s32[256]{0:T(256)S(1)} %bitcast_dynamic-update-slice_fusion.2, ...), channel_id=1, replica_groups=mesh['segment'=4,'dp'=128] {'dp'}, use_global_device_ids=true, to_apply=%add.3 | all-reduce | flops 1024 | bytes 8192
  86.5 85.5 %all-gather.5.cloned.1.call-done = bf16[1,256,7168]{2,0,1:T(2,128)(2,1)} async-done(((bf16[1,2,7168]{2,0,1:T(2,128)(2,1)}), bf16[1,256,7168]{2,0,1:T(2,128)(2,1)}) %all-gather.5.cloned.1.call-update) | async-done | bytes 3670032 | tf_op jit(solution)/shard_map/all_gather | solution.py:56
  172.1 0.0 copy-done
  172.1 4.6 fusion.17
  176.7 147.4 %all-gather.7.cloned.1.call-done = bf16[1,256,7168]{2,0,1:T(2,128)(2,1)} async-done(((bf16[1,2,7168]{2,0,1:T(2,128)(2,1)}), bf16[1,256,7168]{2,0,1:T(2,128)(2,1)}) %all-gather.7.cloned.1.call-update) | async-done | bytes 3670032 | tf_op jit(solution)/shard_map/all_gather | solution.py:56
  324.1 4.6 fusion.15
  328.8 147.4 %all-gather.9.cloned.1.call-done = bf16[1,256,7168]{2,0,1:T(2,128)(2,1)} async-done(((bf16[1,2,7168]{2,0,1:T(2,128)(2,1)}), bf16[1,256,7168]{2,0,1:T(2,128)(2,1)}) %all-gather.9.cloned.1.call-update) | async-done | bytes 3670032 | tf_op jit(solution)/shard_map/all_gather | solution.py:56
  476.2 4.6 fusion.16
  480.8 0.0 copy-start.4
  480.9 147.3 %all-gather.11.cloned.1.call-done = bf16[1,256,7168]{2,0,1:T(2,128)(2,1)} async-done(((bf16[1,2,7168]{2,0,1:T(2,128)(2,1)}), bf16[1,256,7168]{2,0,1:T(2,128)(2,1)}) %all-gather.11.cloned.1.call-update) | async-done | bytes 3670032 | tf_op jit(solution)/shard_map/all_gather | solution.py:56
  628.1 4.6 fusion.14
  632.8 96.2 %pmax.7 = f32[4,256]{1,0:T(4,128)S(1)} all-reduce(f32[4,256]{1,0:T(4,128)S(1)} %dynamic_update_slice.43), channel_id=1, replica_groups=mesh['segment'=4,'dp'=128] {'segment','dp'}, use_global_device_ids=true, to_apply=%region_9.10 | all-reduce | flops 1024 | bytes 8192 | tf_op jit(solution)/shard_map/pmax | solution.py:21
  729.0 0.2 select_reduce_fusion
  729.5 93.6 %all-reduce.5 = (f32[4,256]{1,0:T(4,128)S(1)}, f32[4,256]{1,0:T(4,128)S(1)}) all-reduce(f32[4,256]{1,0:T(4,128)S(1)} %exponential_multiply_fusion, f32[4,256]{1,0:T(4,128)S(1)} %dynamic_update_slice.39), channel_id=1, replica_groups=mesh['segment'=4,'dp'=128] {'segment','dp'}, use_global_device_ids=true, to_apply=%region_14.15 | all-reduce | flops 2048 | bytes 16384 | tf_op jit(solution)/shard_map/psum | solution.py:22
  823.1 0.0 copy-done.4
  823.1 0.6 fusion.13
  (21 shorter events, 0.5 us)
Async XLA Ops:
  7.2 164.9 %copy-start = (bf16[128,7168]{1,0:T(8,128)(2,1)S(1)}, bf16[128,7168]{1,0:T(8,128)(2,1)}, u32[]{:S(2)}) copy-start(bf16[128,7168]{1,0:T(8,128)(2,1)} %param.5) | copy-start | bytes 5505028
  7.2 164.9 %all-gather.5.cloned.1.call-start = ((), (), s32[]{:S(2)}) async-start(), calls=%async_computation | async-start | bytes 7397376 | tf_op jit(solution)/shard_map/all_gather | solution.py:56
  8.8 315.4 %all-gather.7.cloned.1.call-start = ((), (), s32[]{:S(2)}) async-start(), calls=%async_computation.1 | async-start | bytes 7397376 | tf_op jit(solution)/shard_map/all_gather | solution.py:56
  8.8 10.2 %collective-permute-start.1 = (bf16[1,2,7168]{2,0,1:T(2,128)(2,1)}, bf16[1,2,7168]{2,0,1:T(2,128)(2,1)S(1)}, u32[]{:S(2)}, u32[]{:S(2)}) collective-permute-start(bf16[1,2,7168]{2,0,1:T(2,128)(2,1)} %copy.8), channel_id=1, source_target_pairs={{384,0},{0,128},{128,256},{256,384},{385,1},{1,129},{129,257},{257... | collective-permute-start | bytes 86024 | tf_op jit(solution)/shard_map/ppermute | solution.py:10
  19.0 0.6 copy-start.1
  19.7 456.5 %all-gather.9.cloned.1.call-start = ((), (), s32[]{:S(2)}) async-start(), calls=%async_computation.2 | async-start | bytes 7397376 | tf_op jit(solution)/shard_map/all_gather | solution.py:56
  19.7 6.9 collective-permute-start.3
  26.7 0.6 copy-start.2
  27.3 600.8 %all-gather.11.cloned.1.call-start = ((), (), s32[]{:S(2)}) async-start(), calls=%async_computation.3 | async-start | bytes 7397376 | tf_op jit(solution)/shard_map/all_gather | solution.py:56
  27.4 6.9 collective-permute-start.5
  34.3 0.6 copy-start.3
  34.9 6.6 collective-permute-start
  41.5 6.1 collective-permute-start.2
  47.6 6.1 collective-permute-start.4
  480.8 342.3 %copy-start.4 = (f32[1,2]{1,0:T(1,128)S(1)}, f32[1,2]{1,0:T(1,128)}, u32[]{:S(2)}) copy-start(f32[1,2]{1,0:T(1,128)} %param.7) | copy-start | bytes 28
Sparse Core Ops, SparseCore 0:
  12.6 159.4 all-gather.4
  176.6 147.4 all-gather.6
  328.7 147.4 all-gather.8
  480.7 147.4 all-gather.10
where the time goes:
time: 831 us; the launch traced here: 830 us
  waiting for transfers between devices  553 us (67%)
  blocking collectives  223 us (27%)
  matrix products  18.3 us (2%)
  between operations  14.7 us (2%)
  starting transfers between devices  14.6 us (2%)
    all_gather x4, waiting for transfers between devices, per_device(): lax.all_gather(block, 'dp', axis=1, tiled=True)  528 us
    pmax x1, blocking collectives, across_all(): highest = lax.pmax(maxima, ('segment', 'dp'))  96.2 us
    psum x1, blocking collectives, across_all(): lax.psum((totals * jnp.exp(maxima - highest), picked), ('segment', 'dp'))  93.6 us
    unnamed x1, blocking collectives  32.7 us
    ppermute x6, waiting for transfers between devices, shifted(): return lax.ppermute(block, axis, route)  25.4 us
    dot_general x4, matrix products, per_device(): jnp.einsum('grd,vd->grv', gathered, head_weight, preferred_element_type=j...  18.3 us
  transfers between devices with their start and end apart: 10, of which 10 were waited for; matrix products, arithmetic and copies ran while one was open for 2% of the time, Pallas kernels for 0%

commit v1 on v0

v1 whole, which is shorter than its diff:
```python
import functools
import jax
import jax.numpy as jnp
import numpy as np
from jax import lax
from jax.experimental import pallas as pl
from jax.experimental.pallas import tpu as pltpu
from jax.sharding import Mesh, PartitionSpec as P

NAMES = ("s1", "s0", "zh", "y1", "y0", "x", "core")
SIZES = (2, 2, 2, 4, 2, 4, 2)
SEG = ("s1", "s0")
DP = ("zh", "y1", "y0", "x", "core")
KG = ("s0", "y0")
GA = ("s1", "zh", "y1")
GB = ("x",)
IDS = 128


def size_of(axes):
    return int(np.prod([SIZES[NAMES.index(a)] for a in axes]))


def matmul_kernel(h_ref, own_ref, other_ref, out_ref):
    depth = own_ref.shape[1]
    half = own_ref.shape[0]
    rows = h_ref[:, 0, :, :depth].reshape(-1, depth)
    dims = (((1,), (1,)), ((), ()))
    out_ref[0, :, :half] = lax.dot_general(
        rows, own_ref[...], dims, preferred_element_type=jnp.float32
    )
    out_ref[0, :, half:] = lax.dot_general(
        rows, other_ref[...], dims, preferred_element_type=jnp.float32
    )


def partial_logits(gathered, own, other):
    nb, nk, rows, width = gathered.shape
    voc, depth = own.shape
    return pl.pallas_call(
        matmul_kernel,
        grid=(nk,),
        in_specs=[
            pl.BlockSpec((nb, 1, rows, width), lambda k: (0, k, 0, 0)),
            pl.BlockSpec((voc, depth), lambda k: (0, 0)),
            pl.BlockSpec((voc, depth), lambda k: (0, 0)),
        ],
        out_specs=pl.BlockSpec((1, nb * rows, 2 * voc), lambda k: (k, 0, 0)),
        out_shape=jax.ShapeDtypeStruct((nk, nb * rows, 2 * voc), jnp.float32),
        compiler_params=pltpu.CompilerParams(vmem_limit_bytes=48 * 1024 * 1024),
    )(gathered, own, other)


def stats_kernel(parts_ref, ids_ref, columns_ref, out_ref):
    nk = parts_ref.shape[0]
    logits = parts_ref[0]
    for k in range(1, nk):
        logits = logits + parts_ref[k]
    top = jnp.max(logits, axis=1, keepdims=True)
    total = jnp.sum(jnp.exp(logits - top), axis=1, keepdims=True)
    hit = ids_ref[...] == columns_ref[...]
    picked = jnp.sum(jnp.where(hit, logits, 0.0), axis=1, keepdims=True)
    lane = lax.broadcasted_iota(jnp.int32, out_ref.shape, 1)
    out_ref[...] = jnp.where(lane == 0, top, jnp.where(lane == 1, total, picked))


def local_stats(parts, ids, columns):
    return pl.pallas_call(
        stats_kernel,
        out_shape=jax.ShapeDtypeStruct((parts.shape[1], 128), jnp.float32),
        compiler_params=pltpu.CompilerParams(vmem_limit_bytes=32 * 1024 * 1024),
    )(parts, ids, columns)


def per_device(hidden, head_weight, target_ids, policy_logp):
    nk, na, nb = size_of(KG), size_of(GA), size_of(GB)
    rows, width = hidden.shape[1:]
    voc = head_weight.shape[0]
    depth = width // nk
    k_index = lax.axis_index(KG)
    core = lax.axis_index("core")

    slices = hidden.reshape(rows, nk, depth).transpose(1, 0, 2)
    ids = target_ids.reshape(rows, 1)
    lane = lax.broadcasted_iota(jnp.int32, (rows, IDS), 1)
    code = jnp.where(lane == 0, ids // 256, ids % 256).astype(hidden.dtype)
    code = jnp.broadcast_to(code[None], (nk, rows, IDS))
    message = jnp.concatenate([slices, code], axis=2)
    message = jnp.broadcast_to(message[:, None], (nk, na, rows, depth + IDS))
    message = message.reshape(nk * na, rows, depth + IDS)
    column = lax.all_to_all(message, KG + GA, 0, 0, tiled=True)
    column = column.reshape(nk * na * rows, depth + IDS)
    gathered = lax.all_gather(column, GB, axis=0, tiled=True)
    gathered = gathered.reshape(nb, nk, na * rows, depth + IDS)

    pieces = head_weight.reshape(voc, nk, depth).transpose(1, 0, 2)
    own = lax.all_to_all(pieces, KG, 0, 0, tiled=True).reshape(nk * voc, depth)
    other = lax.ppermute(own, "core", [(0, 1), (1, 0)])

    parts = partial_logits(gathered, own, other)
    parts = lax.all_to_all(parts, KG, 0, 0, tiled=True)

    def device(c, k0, k1):
        at = {a: lax.axis_index(a) for a in NAMES}
        at.update({"core": c, KG[0]: k0, KG[1]: k1})
        flat = 0
        for a, n in zip(NAMES, SIZES):
            flat = flat * n + at[a]
        return flat

    cell = jnp.arange(2 * nk, dtype=jnp.int32)
    n1 = size_of(KG[1:])
    first = device(
        jnp.where(cell < nk, core, 1 - core), (cell % nk) // n1, cell % n1
    )
    columns = (first[:, None] * voc + jnp.arange(voc, dtype=jnp.int32)).reshape(1, -1)
    mine = lax.dynamic_slice_in_dim(gathered, k_index, 1, 1)[:, 0, :, depth : depth + 2]
    mine = mine.astype(jnp.int32).reshape(nb * na * rows, 2)
    mine = mine[:, :1] * 256 + mine[:, 1:]

    stats = local_stats(parts, mine, columns)[:, :8]
    stats = stats.reshape(nb * na, rows, 8)
    stats = lax.all_to_all(stats, GB + GA, 0, 0, tiled=True)
    tops, totals, picks = stats[..., 0], stats[..., 1], stats[..., 2]
    highest = jnp.max(tops, axis=0)
    total = jnp.sum(totals * jnp.exp(tops - highest), axis=0)
    picked = jnp.sum(picks, axis=0)
    ref_logp = (picked - (highest + jnp.log(total))).reshape(1, rows)
    log_ratio = ref_logp - policy_logp
    kl_term = jnp.minimum(jnp.exp(log_ratio) - log_ratio - 1.0, 10.0)
    return (ref_logp, kl_term)


def solution(mesh):
    fine = Mesh(mesh.devices.reshape(SIZES), NAMES)
    return jax.shard_map(
        per_device,
        mesh=fine,
        in_specs=(P(SEG, DP, None), P(SEG + DP, None), P(SEG, DP), P(SEG, DP)),
        out_specs=(P(SEG, DP), P(SEG, DP)),
        check_vma=False,
    )
```

time: 831 us -> 158 us (0.19)
  waiting for transfers between devices: 553 us -> 68.6 us
  blocking collectives: 223 us -> 27.4 us
  matrix products: 18.3 us -> 0 us
  starting transfers between devices: 14.6 us -> 27.7 us
    all_gather x4 -> x1, waiting for transfers between devices: 528 us -> 11.2 us  [per_device(): gathered = lax.all_gather(column, GB, axis=0, tiled=True)]
    pmax x1 -> x0, blocking collectives: 96.2 us -> none  [across_all(): highest = lax.pmax(maxima, ('segment', 'dp'))]
    psum x1 -> x0, blocking collectives: 93.6 us -> none  [across_all(): lax.psum((totals * jnp.exp(maxima - highest), picked), ('segment', 'dp'))]
    all_to_all x0 -> x3, waiting for transfers between devices: none -> 57.4 us  [the longest x1 23.3 us: per_device(): parts = lax.all_to_all(parts, KG, 0, 0, tiled=True)]
    unnamed x1 -> x0, blocking collectives: 32.7 us -> none
    all_to_all x0 -> x1, blocking collectives: none -> 27.4 us  [per_device(): stats = lax.all_to_all(stats, GB + GA, 0, 0, tiled=True)]
    ppermute x6 -> x1, waiting for transfers between devices: 25.4 us -> 0.01 us  [per_device(): other = lax.ppermute(own, 'core', [(0, 1), (1, 0)])]
    all_to_all x0 -> x3, starting transfers between devices: none -> 24.3 us  [the longest x1 17.1 us: per_device(): column = lax.all_to_all(message, KG + GA, 0, 0, tiled=True)]
  transfers between devices with their start and end apart: 10 -> 5, of which waited for: 10 -> 4; matrix products, arithmetic and copies ran while one was open for 2% -> 3% of each run, Pallas kernels for 0% -> 0%
where the time goes in v1:
time: 158 us; the launch traced here: 156 us
  waiting for transfers between devices  68.6 us (43%)
  starting transfers between devices  27.7 us (18%)
  blocking collectives  27.4 us (17%)
  between operations  14.1 us (9%)
  local copies, waits for them, and re-layouts  8.16 us (5%)
  Pallas kernels  8.05 us (5%)
  other arithmetic  2.05 us (1%)
    all_to_all x1, blocking collectives, per_device(): stats = lax.all_to_all(stats, GB + GA, 0, 0, tiled=True)  27.4 us
    all_to_all x1, waiting for transfers between devices, per_device(): parts = lax.all_to_all(parts, KG, 0, 0, tiled=True)  23.3 us
    all_to_all x1, waiting for transfers between devices, per_device(): own = lax.all_to_all(pieces, KG, 0, 0, tiled=True).reshape(nk * voc, depth)  20.5 us
    all_to_all x1, starting transfers between devices, per_device(): column = lax.all_to_all(message, KG + GA, 0, 0, tiled=True)  17.1 us
    all_to_all x1, waiting for transfers between devices, per_device(): column = lax.all_to_all(message, KG + GA, 0, 0, tiled=True)  13.6 us
    all_gather x1, waiting for transfers between devices, per_device(): gathered = lax.all_gather(column, GB, axis=0, tiled=True)  11.2 us
    pallas_call x1, Pallas kernels, partial_logits(): pl.pallas_call(matmul_kernel, grid=(nk,), in_specs=[pl.BlockSpec((nb, 1,...  7.71 us
    all_to_all x1, starting transfers between devices, per_device(): parts = lax.all_to_all(parts, KG, 0, 0, tiled=True)  3.61 us
  transfers between devices with their start and end apart: 5, of which 4 were waited for; matrix products, arithmetic and copies ran while one was open for 3% of the time, Pallas kernels for 0%

profile of v1, /device:TPU:1, one launch (start us, length us, event | category | flops | bytes accessed | tf_op | source)
XLA Modules:
  0.0 156.1 jit_solution(6649412154338456110)
XLA Ops:
  7.2 0.7 and_select_fusion.4
  7.8 0.8 reshape.255
  8.6 0.1 select_convert_fusion
  8.8 1.0 broadcast_in_dim.42
  9.8 17.1 %all-to-all-start = ((bf16[64,2,1920]{2,1,0:T(2,128)(2,1)}), bf16[64,2,1920]{2,1,0:T(2,128)(2,1)S(1)}, u32[]{:S(2)}, u32[]{:S(2)}) async-start(bf16[64,2,1920]{2,1,0:T(2,128)(2,1)} %bitcast.2), calls=%async_computation | async-start | bytes 983040 | tf_op jit(solution)/shard_map/all_to_all | solution.py:91
  26.9 2.9 %copy.20 = bf16[16,4,8,1792]{3,2,0,1:T(8,128)(2,1)} copy(bf16[16,4,8,1792]{3,2,1,0:T(8,128)(2,1)} %bitcast.52) | data formatting | bytes 3670016 | tf_op jit(solution)/shard_map/reshape | solution.py:96
  29.8 13.6 %all-to-all-done = bf16[64,2,1920]{2,1,0:T(2,128)(2,1)S(1)} async-done(((bf16[64,2,1920]{2,1,0:T(2,128)(2,1)}), bf16[64,2,1920]{2,1,0:T(2,128)(2,1)S(1)}, u32[]{:S(2)}, u32[]{:S(2)}) %all-to-all-start) | async-done | bytes 491552 | tf_op jit(solution)/shard_map/all_to_all | solution.py:91
  43.4 3.6 %all-to-all-start.1 = ((bf16[4,128,1792]{2,1,0:T(8,128)(2,1)}), bf16[4,128,1792]{2,1,0:T(8,128)(2,1)S(1)}, u32[]{:S(2)}, u32[]{:S(2)}) async-start(bf16[4,128,1792]{2,1,0:T(8,128)(2,1)} %bitcast.51), calls=%async_computation.1 | async-start | bytes 3670016 | tf_op jit(solution)/shard_map/all_to_all | solution.py:97
  47.0 0.0 all-gather.2.cloned.1.call-start
  47.0 1.0 reshape.258
  48.0 0.0 all-gather.2.cloned.1.call-update
  48.0 20.5 %all-to-all-done.1 = bf16[4,128,1792]{2,1,0:T(8,128)(2,1)S(1)} async-done(((bf16[4,128,1792]{2,1,0:T(8,128)(2,1)}), bf16[4,128,1792]{2,1,0:T(8,128)(2,1)S(1)}, u32[]{:S(2)}, u32[]{:S(2)}) %all-to-all-start.1) | async-done | bytes 1835040 | tf_op jit(solution)/shard_map/all_to_all | solution.py:97
  68.5 3.3 %collective-permute-start = (bf16[512,1792]{1,0:T(8,128)(2,1)S(1)}, bf16[512,1792]{1,0:T(8,128)(2,1)}, u32[]{:S(2)}, u32[]{:S(2)}) collective-permute-start(bf16[512,1792]{1,0:T(8,128)(2,1)S(1)} %bitcast.45), channel_id=1, source_target_pairs={{0,1},{1,0},{2,3},{3,2},{4,5},{5,4},{6,7},{7,6},{8,9},{9,8},{10,11... | collective-permute-start | bytes 5505032 | tf_op jit(solution)/shard_map/ppermute | solution.py:98
  71.9 11.2 %all-gather.2.cloned.1.call-done = bf16[512,1920]{1,0:T(8,128)(2,1)} async-done(((bf16[128,1920]{1,0:T(8,128)(2,1)}), bf16[512,1920]{1,0:T(8,128)(2,1)}) %all-gather.2.cloned.1.call-update) | async-done | bytes 1966096 | tf_op jit(solution)/shard_map/all_gather | solution.py:93
  83.0 0.0 collective-permute-done.other_ref
  83.0 0.0 copy-start
  83.0 1.5 copy-done
  84.6 7.7 %shard_map.59 = f32[4,128,1024]{2,1,0:T(8,128)} custom-call(bf16[4,4,32,1920]{3,2,1,0:T(8,128)(2,1)S(1)} %bitcast.48, bf16[512,1792]{1,0:T(8,128)(2,1)S(1)} %bitcast.46, bf16[512,1792]{1,0:T(8,128)(2,1)} %collective-permute-done.other_ref), custom_call_target="tpu_custom_call" | custom-call | tf_op jit(solution)/shard_map/pallas_call | solution.py:40
  92.3 3.6 %all-to-all-start.2 = ((f32[4,128,1024]{2,1,0:T(8,128)}), f32[4,128,1024]{2,1,0:T(8,128)S(1)}, u32[]{:S(2)}, u32[]{:S(2)}) async-start(f32[4,128,1024]{2,1,0:T(8,128)} %shard_map.59), calls=%async_computation.2 | async-start | bytes 4194304 | tf_op jit(solution)/shard_map/all_to_all | solution.py:101
  95.9 0.0 copy-start.1
  96.0 0.1 iota_add_fusion
  96.0 0.8 constant_dynamic-slice_fusion
  96.8 0.1 slice_add_fusion.ids_ref
  96.9 23.3 %all-to-all-done.2.parts_ref = f32[4,128,1024]{2,1,0:T(8,128)S(1)} async-done(((f32[4,128,1024]{2,1,0:T(8,128)}), f32[4,128,1024]{2,1,0:T(8,128)S(1)}, u32[]{:S(2)}, u32[]{:S(2)}) %all-to-all-start.2) | async-done | bytes 2097184 | tf_op jit(solution)/shard_map/all_to_all | solution.py:101
  120.2 0.3 shard_map.60
  120.5 27.4 %all_to_all.20 = f32[64,2,8]{2,1,0:T(2,128)S(1)} all-to-all(f32[64,2,8]{2,1,0:T(2,128)S(1)} %bitcast.49), channel_id=1, replica_groups=mesh['s1'=2,'s0'=2,'zh'=2,'y1'=4,'y0'=2,'x'=4,'core'=2] {'x','s1','zh','..., dimensions={0} | all-to-all | bytes 8192 | tf_op jit(solution)/shard_map/all_to_all | solution.py:123
  147.9 0.4 fusion.8
  148.3 0.1 copy.17
  148.4 0.1 copy.16
  148.5 0.2 fusion.2
  148.7 0.0 copy-done.1
  148.7 0.5 fusion.5
  (6 shorter events, 0.1 us)
Async XLA Ops:
  9.8 33.6 %all-to-all-start = ((bf16[64,2,1920]{2,1,0:T(2,128)(2,1)}), bf16[64,2,1920]{2,1,0:T(2,128)(2,1)S(1)}, u32[]{:S(2)}, u32[]{:S(2)}) async-start(bf16[64,2,1920]{2,1,0:T(2,128)(2,1)} %bitcast.2), calls=%async_computation | async-start | bytes 983040 | tf_op jit(solution)/shard_map/all_to_all | solution.py:91
  43.4 25.2 %all-to-all-start.1 = ((bf16[4,128,1792]{2,1,0:T(8,128)(2,1)}), bf16[4,128,1792]{2,1,0:T(8,128)(2,1)S(1)}, u32[]{:S(2)}, u32[]{:S(2)}) async-start(bf16[4,128,1792]{2,1,0:T(8,128)(2,1)} %bitcast.51), calls=%async_computation.1 | async-start | bytes 3670016 | tf_op jit(solution)/shard_map/all_to_all | solution.py:97
  47.0 36.1 %all-gather.2.cloned.1.call-start = ((), (), s32[]{:S(2)}) async-start(), calls=%async_computation.4 | async-start | bytes 2457600 | tf_op jit(solution)/shard_map/all_gather | solution.py:93
  68.5 14.5 %collective-permute-start = (bf16[512,1792]{1,0:T(8,128)(2,1)S(1)}, bf16[512,1792]{1,0:T(8,128)(2,1)}, u32[]{:S(2)}, u32[]{:S(2)}) collective-permute-start(bf16[512,1792]{1,0:T(8,128)(2,1)S(1)} %bitcast.45), channel_id=1, source_target_pairs={{0,1},{1,0},{2,3},{3,2},{4,5},{5,4},{6,7},{7,6},{8,9},{9,8},{10,11... | collective-permute-start | bytes 5505032 | tf_op jit(solution)/shard_map/ppermute | solution.py:98
  83.0 1.5 copy-start
  92.3 27.9 %all-to-all-start.2 = ((f32[4,128,1024]{2,1,0:T(8,128)}), f32[4,128,1024]{2,1,0:T(8,128)S(1)}, u32[]{:S(2)}, u32[]{:S(2)}) async-start(f32[4,128,1024]{2,1,0:T(8,128)} %shard_map.59), calls=%async_computation.2 | async-start | bytes 4194304 | tf_op jit(solution)/shard_map/all_to_all | solution.py:101
  95.9 52.8 %copy-start.1 = (f32[1,2]{1,0:T(1,128)S(1)}, f32[1,2]{1,0:T(1,128)}, u32[]{:S(2)}) copy-start(f32[1,2]{1,0:T(1,128)} %param.7) | copy-start | bytes 28
Sparse Core Ops, SparseCore 0:
  49.9 33.0 all-gather.1

commit v2 on v1

v2 whole, which is shorter than its diff:
```python
import jax
import jax.numpy as jnp
import numpy as np
from jax import lax
from jax.experimental import pallas as pl
from jax.experimental.pallas import tpu as pltpu
from jax.sharding import Mesh, PartitionSpec as P

NAMES = ("s1", "s0", "zh", "y1", "y0", "x", "core")
SIZES = (2, 2, 2, 4, 2, 4, 2)
SEG = ("s1", "s0")
DP = ("zh", "y1", "y0", "x", "core")
GA = ("s1", "zh", "y1")
GB = ("x",)
IDS = 128
SWAP = [(0, 1), (1, 0)]


def size_of(axes):
    return int(np.prod([SIZES[NAMES.index(a)] for a in axes]))


def matmul_kernel(s0_ref, h_ref, *refs):
    pieces, (keep_ref, send_ref, id_ref) = refs[:-3], refs[-3:]
    voc, depth = pieces[0].shape
    mine = s0_ref[0]
    wide = h_ref.shape[-1]
    kept = h_ref[:, mine].reshape(-1, wide)
    sent = h_ref[:, 1 - mine].reshape(-1, wide)
    rows = jnp.concatenate([kept[:, :depth], sent[:, :depth]], axis=0)
    half = kept.shape[0]
    code = kept[:, depth:].astype(jnp.float32).T
    id_ref[...] = (code[0:1] * 256.0 + code[1:2]).astype(jnp.int32)
    for j, piece in enumerate(pieces):
        out = lax.dot_general(
            piece[...], rows, (((1,), (1,)), ((), ())),
            preferred_element_type=jnp.float32,
        )
        keep_ref[j] = out[:, :half]
        send_ref[j ^ 1] = out[:, half:]


def partial_logits(s0, gathered, pieces):
    nb, _, rows, _ = gathered.shape
    voc = pieces[0].shape[0]
    block = jax.ShapeDtypeStruct((len(pieces), voc, nb * rows), jnp.float32)
    vmem = pl.BlockSpec(memory_space=pltpu.VMEM)
    return pl.pallas_call(
        matmul_kernel,
        in_specs=[pl.BlockSpec(memory_space=pltpu.SMEM)] + [vmem] * (1 + len(pieces)),
        out_specs=[vmem] * 3,
        out_shape=[block, block, jax.ShapeDtypeStruct((1, nb * rows), jnp.int32)],
        compiler_params=pltpu.CompilerParams(vmem_limit_bytes=48 * 1024 * 1024),
    )(s0, gathered, *pieces)


def stats_kernel(first_ref, mine_ref, theirs_ref, ids_ref, out_ref):
    pieces, voc, rows = mine_ref.shape
    logits = mine_ref[...] + theirs_ref[...]
    top = jnp.max(jnp.max(logits, axis=0), axis=0, keepdims=True)
    total = jnp.sum(jnp.sum(jnp.exp(logits - top[None]), axis=0), axis=0, keepdims=True)
    ids = ids_ref[...]
    entry = lax.broadcasted_iota(jnp.int32, (voc, rows), 0)
    picked = jnp.zeros((voc, rows), jnp.float32)
    for j in range(pieces):
        picked += jnp.where(entry + first_ref[j] == ids, logits[j], 0.0)
    picked = jnp.sum(picked, axis=0, keepdims=True)
    line = lax.broadcasted_iota(jnp.int32, (128, rows), 0)
    out_ref[...] = jnp.where(line == 0, top, jnp.where(line == 1, total, picked)).T


def local_stats(first, mine, theirs, ids):
    vmem = pl.BlockSpec(memory_space=pltpu.VMEM)
    return pl.pallas_call(
        stats_kernel,
        in_specs=[pl.BlockSpec(memory_space=pltpu.SMEM)] + [vmem] * 3,
        out_specs=vmem,
        out_shape=jax.ShapeDtypeStruct((mine.shape[2], 128), jnp.float32),
        compiler_params=pltpu.CompilerParams(vmem_limit_bytes=32 * 1024 * 1024),
    )(first, mine, theirs, ids)


def per_device(hidden, head_weight, target_ids, policy_logp):
    na, nb = size_of(GA), size_of(GB)
    rows, width = hidden.shape[1:]
    voc = head_weight.shape[0]
    depth = width // 2
    at = {a: lax.axis_index(a) for a in NAMES}
    s0 = at["s0"]

    kept = lax.dynamic_slice_in_dim(head_weight, s0 * depth, depth, 1)
    given = lax.dynamic_slice_in_dim(head_weight, (1 - s0) * depth, depth, 1)
    pieces = [
        kept,
        lax.ppermute(given, "s0", SWAP),
        lax.ppermute(kept, "y0", SWAP),
        lax.ppermute(given, ("s0", "y0"), [(i, i ^ 3) for i in range(4)]),
    ]

    ids = target_ids.reshape(rows, 1)
    lane = lax.broadcasted_iota(jnp.int32, (rows, IDS), 1)
    code = jnp.where(lane == 0, ids >> 8, ids & 255).astype(hidden.dtype)
    halves = [
        jnp.concatenate([hidden[0, :, k * depth : (k + 1) * depth], code], axis=1)
        for k in range(2)
    ]
    message = jnp.broadcast_to(jnp.stack(halves)[:, None], (2, na, rows, depth + IDS))
    message = message.reshape(2 * na, rows, depth + IDS)
    column = lax.all_to_all(message, ("s0",) + GA, 0, 0, tiled=True)
    column = column.reshape(2 * na * rows, depth + IDS)
    copies = jnp.broadcast_to(column[None], (nb,) + column.shape)
    gathered = lax.all_to_all(copies, GB, 0, 0, tiled=True)
    gathered = gathered.reshape(nb, 2, na * rows, depth + IDS)

    pieces += [lax.ppermute(piece, "core", SWAP) for piece in pieces]

    mine, send, ids = partial_logits(s0.reshape(1), gathered, pieces)
    theirs = lax.ppermute(send, "s0", SWAP)

    firsts = []
    for j in range(len(pieces)):
        place = dict(at)
        place["s0"] = at["s0"] ^ (j & 1)
        place["y0"] = at["y0"] ^ ((j >> 1) & 1)
        place["core"] = at["core"] ^ (j >> 2)
        flat = 0
        for a, n in zip(NAMES, SIZES):
            flat = flat * n + place[a]
        firsts.append(flat * voc)
    stats = local_stats(jnp.stack(firsts), mine, theirs, ids)[:, :8]
    stats = stats.reshape(nb * na, rows, 8)
    stats = lax.all_to_all(stats, GB + GA, 0, 0, tiled=True)
    tops, totals, picks = stats[..., 0], stats[..., 1], stats[..., 2]
    highest = jnp.max(tops, axis=0)
    total = jnp.sum(totals * jnp.exp(tops - highest), axis=0)
    picked = jnp.sum(picks, axis=0)
    ref_logp = (picked - (highest + jnp.log(total))).reshape(1, rows)
    log_ratio = ref_logp - policy_logp
    kl_term = jnp.minimum(jnp.exp(log_ratio) - log_ratio - 1.0, 10.0)
    return (ref_logp, kl_term)


def solution(mesh):
    fine = Mesh(mesh.devices.reshape(SIZES), NAMES)
    return jax.shard_map(
        per_device,
        mesh=fine,
        in_specs=(P(SEG, DP, None), P(SEG + DP, None), P(SEG, DP), P(SEG, DP)),
        out_specs=(P(SEG, DP), P(SEG, DP)),
        check_vma=False,
    )
```

time: 158 us -> 134 us (0.85)
  waiting for transfers between devices: 68.6 us -> 39.5 us
  starting transfers between devices: 27.7 us -> 46 us
  between operations: 14.1 us -> 0.84 us
  blocking collectives: 27.4 us -> 24.4 us
  local copies, waits for them, and re-layouts: 8.16 us -> 11.1 us
    all_to_all x3 -> x2, waiting for transfers between devices: 57.4 us -> 9.2 us  [the longest x1 9.2 us: per_device(): column = lax.all_to_all(message, ('s0',) + GA, 0, 0, tiled=True)]
    ppermute x1 -> x8, waiting for transfers between devices: 0.01 us -> 30.3 us  [the longest x1 15.6 us: per_device(): lax.ppermute(given, 's0', SWAP)]
    ppermute x1 -> x8, starting transfers between devices: 3.3 us -> 24.9 us  [the longest x4 14.1 us: per_device(): pieces += [lax.ppermute(piece, 'core', SWAP) for piece in pieces]]
    all_gather x1 -> x0, waiting for transfers between devices: 11.2 us -> none  [per_device(): gathered = lax.all_gather(column, GB, axis=0, tiled=True)]
    reshape x3 -> x0, local copies, waits for them, and re-layouts: 4.61 us -> none  [the longest x1 2.87 us: per_device(): pieces = head_weight.reshape(voc, nk, depth).transpose(1, 0, 2)]
    all_to_all x3 -> x2, starting transfers between devices: 24.3 us -> 21 us  [the longest x1 16.6 us: per_device(): column = lax.all_to_all(message, ('s0',) + GA, 0, 0, tiled=True)]
    all_to_all x1, blocking collectives: 27.4 us -> 24.4 us  [per_device(): stats = lax.all_to_all(stats, GB + GA, 0, 0, tiled=True)]
    broadcast_in_dim x2 -> x3, local copies, waits for them, and re-layouts: 1.04 us -> 3.58 us  [the longest x2 2.57 us: per_device(): copies = jnp.broadcast_to(column[None], (nb,) + column.shape)]
  transfers between devices with their start and end apart: 5 -> 10, of which waited for: 4 -> 4; matrix products, arithmetic and copies ran while one was open for 3% -> 4% of each run, Pallas kernels for 0% -> 0%
where the time goes in v2:
time: 134 us; the launch traced here: 133 us
  starting transfers between devices  46 us (34%)
  waiting for transfers between devices  39.5 us (29%)
  blocking collectives  24.4 us (18%)
  local copies, waits for them, and re-layouts  11.1 us (8%)
  Pallas kernels  9.06 us (7%)
  other arithmetic  1.91 us (1%)
    all_to_all x1, blocking collectives, per_device(): stats = lax.all_to_all(stats, GB + GA, 0, 0, tiled=True)  24.4 us
    all_to_all x1, starting transfers between devices, per_device(): column = lax.all_to_all(message, ('s0',) + GA, 0, 0, tiled=True)  16.6 us
    ppermute x1, waiting for transfers between devices, per_device(): lax.ppermute(given, 's0', SWAP)  15.6 us
    ppermute x4, starting transfers between devices, per_device(): pieces += [lax.ppermute(piece, 'core', SWAP) for piece in pieces]  14.1 us
    ppermute x1, waiting for transfers between devices, per_device(): theirs = lax.ppermute(send, 's0', SWAP)  12.5 us
    all_to_all x1, waiting for transfers between devices, per_device(): column = lax.all_to_all(message, ('s0',) + GA, 0, 0, tiled=True)  9.2 us
    pallas_call x1, Pallas kernels, partial_logits(): pl.pallas_call(matmul_kernel, in_specs=[pl.BlockSpec(memory_space=pltpu.S...  8.17 us
    all_to_all x1, starting transfers between devices, per_device(): gathered = lax.all_to_all(copies, GB, 0, 0, tiled=True)  4.41 us
  transfers between devices with their start and end apart: 10, of which 4 were waited for; matrix products, arithmetic and copies ran while one was open for 4% of the time, Pallas kernels for 0%

profile of v2, /device:TPU:1, one launch (start us, length us, event | category | flops | bytes accessed | tf_op | source)
XLA Modules:
  0.0 132.9 jit_solution(6800218069110644096)
XLA Ops:
  0.6 0.7 shift-right-arithmetic_bitcast_fusion
  1.3 0.8 slice_bitcast_fusion.1
  2.1 0.1 select_convert_fusion
  2.2 1.0 broadcast_in_dim.32
  3.2 16.6 %all-to-all-start = ((bf16[32,2,3712]{2,1,0:T(2,128)(2,1)}), bf16[32,2,3712]{2,1,0:T(2,128)(2,1)}, u32[]{:S(2)}, u32[]{:S(2)}) async-start(bf16[32,2,3712]{2,1,0:T(2,128)(2,1)} %bitcast.15), calls=%async_computation | async-start | bytes 950272 | tf_op jit(solution)/shard_map/all_to_all | solution.py:109
  19.9 2.5 %constant_dynamic-slice_fusion = (bf16[128,3584]{1,0:T(8,128)(2,1)}, bf16[128,3584]{1,0:T(8,128)(2,1)S(1)}) fusion(bf16[128,7168]{1,0:T(8,128)(2,1)} %param.5, s32[]{:T(128)S(6)} %select_n.12, s32[]{:T(128)S(6)} %select_n.11), kind=kLoop, calls=%fused_computation.19 | loop fusion | bytes 3670024 | tf_op jit(solution)/shard_map/dynamic_slice | solution.py:92
  22.4 3.2 %collective-permute-start.2 = (bf16[128,3584]{1,0:T(8,128)(2,1)}, bf16[128,3584]{1,0:T(8,128)(2,1)S(1)}, u32[]{:S(2)}, u32[]{:S(2)}) collective-permute-start(bf16[128,3584]{1,0:T(8,128)(2,1)} %get-tuple-element.12), channel_id=1, source_target_pairs={{0,136},{8,128},{128,8},{136,0},{1,137},{9,129},{129,9},{137,1},{2... | collective-permute-start | bytes 2752520 | tf_op jit(solution)/shard_map/ppermute | solution.py:97
  25.6 2.2 %collective-permute-start = (bf16[128,3584]{1,0:T(8,128)(2,1)}, bf16[128,3584]{1,0:T(8,128)(2,1)S(1)}, u32[]{:S(2)}, u32[]{:S(2)}) collective-permute-start(bf16[128,3584]{1,0:T(8,128)(2,1)} %get-tuple-element.12), channel_id=1, source_target_pairs={{0,128},{128,0},{1,129},{129,1},{2,130},{130,2},{3,131},{131,3},{4... | collective-permute-start | bytes 2752520 | tf_op jit(solution)/shard_map/ppermute | solution.py:95
  27.8 3.0 %collective-permute-start.1 = (bf16[128,3584]{1,0:T(8,128)(2,1)S(1)}, bf16[128,3584]{1,0:T(8,128)(2,1)}, u32[]{:S(2)}, u32[]{:S(2)}) collective-permute-start(bf16[128,3584]{1,0:T(8,128)(2,1)S(1)} %get-tuple-element.13.refs_0_), channel_id=1, source_target_pairs={{0,8},{8,0},{1,9},{9,1},{2,10},{10,2},{3,11},{11,3},{4,12},{12,4},... | collective-permute-start | bytes 2752520 | tf_op jit(solution)/shard_map/ppermute | solution.py:96
  30.8 9.2 %all-to-all-done = bf16[32,2,3712]{2,1,0:T(2,128)(2,1)} async-done(((bf16[32,2,3712]{2,1,0:T(2,128)(2,1)}), bf16[32,2,3712]{2,1,0:T(2,128)(2,1)}, u32[]{:S(2)}, u32[]{:S(2)}) %all-to-all-start) | async-done | bytes 475168 | tf_op jit(solution)/shard_map/all_to_all | solution.py:109
  40.0 1.2 broadcast_in_dim.33
  41.2 1.4 %broadcast_in_dim.34 = bf16[4,64,3712]{2,1,0:T(8,128)(2,1)} broadcast(bf16[64,3712]{1,0:T(8,128)(2,1)S(1)} %broadcast_in_dim.33), dimensions={1,2} | broadcast | bytes 2375680 | tf_op jit(solution)/shard_map/broadcast_in_dim | solution.py:111
  42.6 4.4 %all-to-all-start.1 = ((bf16[4,64,3712]{2,1,0:T(8,128)(2,1)}), bf16[4,64,3712]{2,1,0:T(8,128)(2,1)}, u32[]{:S(2)}, u32[]{:S(2)}) async-start(bf16[4,64,3712]{2,1,0:T(8,128)(2,1)} %broadcast_in_dim.34), calls=%async_computation.1 | async-start | bytes 3801088 | tf_op jit(solution)/shard_map/all_to_all | solution.py:112
  47.0 4.5 %collective-permute-start.3 = (bf16[128,3584]{1,0:T(8,128)(2,1)S(1)}, bf16[128,3584]{1,0:T(8,128)(2,1)S(1)}, u32[]{:S(2)}, u32[]{:S(2)}) collective-permute-start(bf16[128,3584]{1,0:T(8,128)(2,1)S(1)} %get-tuple-element.13.refs_0_), channel_id=1, source_target_pairs={{0,1},{1,0},{2,3},{3,2},{4,5},{5,4},{6,7},{7,6},{8,9},{9,8},{10,11... | collective-permute-start | bytes 2752520 | tf_op jit(solution)/shard_map/ppermute | solution.py:115
  51.5 2.2 %collective-permute-done.2.refs_3_ = bf16[128,3584]{1,0:T(8,128)(2,1)S(1)} collective-permute-done((bf16[128,3584]{1,0:T(8,128)(2,1)}, bf16[128,3584]{1,0:T(8,128)(2,1)S(1)}, u32[]{:S(2)}, u32[]{:S(2)}) %collective-permute-start.2) | collective-permute-done | bytes 917536 | tf_op jit(solution)/shard_map/ppermute | solution.py:97
  53.7 5.1 %collective-permute-start.6 = (bf16[128,3584]{1,0:T(8,128)(2,1)S(1)}, bf16[128,3584]{1,0:T(8,128)(2,1)S(1)}, u32[]{:S(2)}, u32[]{:S(2)}) collective-permute-start(bf16[128,3584]{1,0:T(8,128)(2,1)S(1)} %collective-permute-done.2.refs_3_), channel_id=1, source_target_pairs={{0,1},{1,0},{2,3},{3,2},{4,5},{5,4},{6,7},{7,6},{8,9},{9,8},{10,11... | collective-permute-start | bytes 2752520 | tf_op jit(solution)/shard_map/ppermute | solution.py:115
  58.8 15.6 %collective-permute-done.refs_1_ = bf16[128,3584]{1,0:T(8,128)(2,1)S(1)} collective-permute-done((bf16[128,3584]{1,0:T(8,128)(2,1)}, bf16[128,3584]{1,0:T(8,128)(2,1)S(1)}, u32[]{:S(2)}, u32[]{:S(2)}) %collective-permute-start) | collective-permute-done | bytes 917536 | tf_op jit(solution)/shard_map/ppermute | solution.py:95
  74.5 2.5 %collective-permute-start.4 = (bf16[128,3584]{1,0:T(8,128)(2,1)S(1)}, bf16[128,3584]{1,0:T(8,128)(2,1)S(1)}, u32[]{:S(2)}, u32[]{:S(2)}) collective-permute-start(bf16[128,3584]{1,0:T(8,128)(2,1)S(1)} %collective-permute-done.refs_1_), channel_id=1, source_target_pairs={{0,1},{1,0},{2,3},{3,2},{4,5},{5,4},{6,7},{7,6},{8,9},{9,8},{10,11... | collective-permute-start | bytes 2752520 | tf_op jit(solution)/shard_map/ppermute | solution.py:115
  77.0 0.0 collective-permute-done.1.refs_2_
  77.0 1.9 %collective-permute-start.5 = (bf16[128,3584]{1,0:T(8,128)(2,1)}, bf16[128,3584]{1,0:T(8,128)(2,1)}, u32[]{:S(2)}, u32[]{:S(2)}) collective-permute-start(bf16[128,3584]{1,0:T(8,128)(2,1)} %collective-permute-done.1.refs_2_), channel_id=1, source_target_pairs={{0,1},{1,0},{2,3},{3,2},{4,5},{5,4},{6,7},{7,6},{8,9},{9,8},{10,11... | collective-permute-start | bytes 2752520 | tf_op jit(solution)/shard_map/ppermute | solution.py:115
  78.9 0.0 collective-permute-done.3.refs_4_
  78.9 0.0 copy-start
  78.9 1.0 copy-done
  79.9 0.0 collective-permute-done.6.refs_7_
  79.9 0.0 copy-start.2
  79.9 0.0 collective-permute-done.4.refs_5_
  79.9 0.9 copy-done.2
  80.8 0.0 copy-start.3
  80.8 0.9 copy-done.3
  81.8 0.0 collective-permute-done.5.refs_6_
  81.8 0.0 all-to-all-done.1
  81.8 0.0 copy-start.1
  81.8 1.2 copy-done.1
  83.0 0.0 copy-start.4
  83.0 8.2 %shard_map.59 = (f32[8,128,128]{2,1,0:T(8,128)S(1)}, f32[8,128,128]{2,1,0:T(8,128)}, s32[1,128]{1,0:T(1,128)S(1)}) custom-call(s32[1]{0:T(128)} %bitcast.8.s0_ref, bf16[4,2,32,3712]{3,2,1,0:T(8,128)(2,1)} %bitcast.16.h_ref, bf16[128,3584]{1,0:T(8,128)(2,1)S(1)} %get-tuple-element.13.refs_0_, bf16[128,3584]{1,0:T(8,128)(2,1)S(1)} %collective-permute-done.refs_1_, ...), custom_call_target="tpu_custom_call" | custom-call | tf_op jit(solution)/shard_map/pallas_call | solution.py:48
  91.1 2.5 %collective-permute-start.7 = (f32[8,128,128]{2,1,0:T(8,128)}, f32[8,128,128]{2,1,0:T(8,128)S(1)}, u32[]{:S(2)}, u32[]{:S(2)}) collective-permute-start(f32[8,128,128]{2,1,0:T(8,128)} %get-tuple-element.6), channel_id=1, source_target_pairs={{0,128},{128,0},{1,129},{129,1},{2,130},{130,2},{3,131},{131,3},{4... | collective-permute-start | bytes 1572872 | tf_op jit(solution)/shard_map/ppermute | solution.py:118
  93.7 0.1 stack.44.first_ref
  93.8 12.5 %collective-permute-done.7.theirs_ref = f32[8,128,128]{2,1,0:T(8,128)S(1)} collective-permute-done((f32[8,128,128]{2,1,0:T(8,128)}, f32[8,128,128]{2,1,0:T(8,128)S(1)}, u32[]{:S(2)}, u32[]{:S(2)}) %collective-permute-start.7) | collective-permute-done | bytes 524320 | tf_op jit(solution)/shard_map/ppermute | solution.py:118
  106.2 0.9 shard_map.60
  107.1 24.4 %all_to_all.15 = f32[64,2,8]{2,1,0:T(2,128)S(1)} all-to-all(f32[64,2,8]{2,1,0:T(2,128)S(1)} %bitcast.38), channel_id=1, replica_groups=mesh['s1'=2,'s0'=2,'zh'=2,'y1'=4,'y0'=2,'x'=4,'core'=2] {'x','s1','zh','..., dimensions={0} | all-to-all | bytes 8192 | tf_op jit(solution)/shard_map/all_to_all | solution.py:132
  131.6 0.4 fusion.7
  131.9 0.1 copy.10
  132.0 0.1 copy.11
  132.1 0.2 fusion.4
  132.3 0.0 copy-done.4
  132.3 0.5 fusion.6
  (3 shorter events, 0.1 us)
Async XLA Ops:
  3.2 36.8 %all-to-all-start = ((bf16[32,2,3712]{2,1,0:T(2,128)(2,1)}), bf16[32,2,3712]{2,1,0:T(2,128)(2,1)}, u32[]{:S(2)}, u32[]{:S(2)}) async-start(bf16[32,2,3712]{2,1,0:T(2,128)(2,1)} %bitcast.15), calls=%async_computation | async-start | bytes 950272 | tf_op jit(solution)/shard_map/all_to_all | solution.py:109
  22.4 31.3 %collective-permute-start.2 = (bf16[128,3584]{1,0:T(8,128)(2,1)}, bf16[128,3584]{1,0:T(8,128)(2,1)S(1)}, u32[]{:S(2)}, u32[]{:S(2)}) collective-permute-start(bf16[128,3584]{1,0:T(8,128)(2,1)} %get-tuple-element.12), channel_id=1, source_target_pairs={{0,136},{8,128},{128,8},{136,0},{1,137},{9,129},{129,9},{137,1},{2... | collective-permute-start | bytes 2752520 | tf_op jit(solution)/shard_map/ppermute | solution.py:97
  25.6 48.9 %collective-permute-start = (bf16[128,3584]{1,0:T(8,128)(2,1)}, bf16[128,3584]{1,0:T(8,128)(2,1)S(1)}, u32[]{:S(2)}, u32[]{:S(2)}) collective-permute-start(bf16[128,3584]{1,0:T(8,128)(2,1)} %get-tuple-element.12), channel_id=1, source_target_pairs={{0,128},{128,0},{1,129},{129,1},{2,130},{130,2},{3,131},{131,3},{4... | collective-permute-start | bytes 2752520 | tf_op jit(solution)/shard_map/ppermute | solution.py:95
  27.8 49.2 %collective-permute-start.1 = (bf16[128,3584]{1,0:T(8,128)(2,1)S(1)}, bf16[128,3584]{1,0:T(8,128)(2,1)}, u32[]{:S(2)}, u32[]{:S(2)}) collective-permute-start(bf16[128,3584]{1,0:T(8,128)(2,1)S(1)} %get-tuple-element.13.refs_0_), channel_id=1, source_target_pairs={{0,8},{8,0},{1,9},{9,1},{2,10},{10,2},{3,11},{11,3},{4,12},{12,4},... | collective-permute-start | bytes 2752520 | tf_op jit(solution)/shard_map/ppermute | solution.py:96
  42.6 39.2 %all-to-all-start.1 = ((bf16[4,64,3712]{2,1,0:T(8,128)(2,1)}), bf16[4,64,3712]{2,1,0:T(8,128)(2,1)}, u32[]{:S(2)}, u32[]{:S(2)}) async-start(bf16[4,64,3712]{2,1,0:T(8,128)(2,1)} %broadcast_in_dim.34), calls=%async_computation.1 | async-start | bytes 3801088 | tf_op jit(solution)/shard_map/all_to_all | solution.py:112
  47.0 31.9 %collective-permute-start.3 = (bf16[128,3584]{1,0:T(8,128)(2,1)S(1)}, bf16[128,3584]{1,0:T(8,128)(2,1)S(1)}, u32[]{:S(2)}, u32[]{:S(2)}) collective-permute-start(bf16[128,3584]{1,0:T(8,128)(2,1)S(1)} %get-tuple-element.13.refs_0_), channel_id=1, source_target_pairs={{0,1},{1,0},{2,3},{3,2},{4,5},{5,4},{6,7},{7,6},{8,9},{9,8},{10,11... | collective-permute-start | bytes 2752520 | tf_op jit(solution)/shard_map/ppermute | solution.py:115
  53.7 26.2 %collective-permute-start.6 = (bf16[128,3584]{1,0:T(8,128)(2,1)S(1)}, bf16[128,3584]{1,0:T(8,128)(2,1)S(1)}, u32[]{:S(2)}, u32[]{:S(2)}) collective-permute-start(bf16[128,3584]{1,0:T(8,128)(2,1)S(1)} %collective-permute-done.2.refs_3_), channel_id=1, source_target_pairs={{0,1},{1,0},{2,3},{3,2},{4,5},{5,4},{6,7},{7,6},{8,9},{9,8},{10,11... | collective-permute-start | bytes 2752520 | tf_op jit(solution)/shard_map/ppermute | solution.py:115
  74.5 5.4 %collective-permute-start.4 = (bf16[128,3584]{1,0:T(8,128)(2,1)S(1)}, bf16[128,3584]{1,0:T(8,128)(2,1)S(1)}, u32[]{:S(2)}, u32[]{:S(2)}) collective-permute-start(bf16[128,3584]{1,0:T(8,128)(2,1)S(1)} %collective-permute-done.refs_1_), channel_id=1, source_target_pairs={{0,1},{1,0},{2,3},{3,2},{4,5},{5,4},{6,7},{7,6},{8,9},{9,8},{10,11... | collective-permute-start | bytes 2752520 | tf_op jit(solution)/shard_map/ppermute | solution.py:115
  77.0 4.8 %collective-permute-start.5 = (bf16[128,3584]{1,0:T(8,128)(2,1)}, bf16[128,3584]{1,0:T(8,128)(2,1)}, u32[]{:S(2)}, u32[]{:S(2)}) collective-permute-start(bf16[128,3584]{1,0:T(8,128)(2,1)} %collective-permute-done.1.refs_2_), channel_id=1, source_target_pairs={{0,1},{1,0},{2,3},{3,2},{4,5},{5,4},{6,7},{7,6},{8,9},{9,8},{10,11... | collective-permute-start | bytes 2752520 | tf_op jit(solution)/shard_map/ppermute | solution.py:115
  78.9 1.0 copy-start
  79.9 0.9 copy-start.2
  80.8 1.0 copy-start.3
  81.8 1.2 copy-start.1
  83.0 49.4 %copy-start.4 = (f32[1,2]{1,0:T(1,128)S(1)}, f32[1,2]{1,0:T(1,128)}, u32[]{:S(2)}) copy-start(f32[1,2]{1,0:T(1,128)} %param.7) | copy-start | bytes 28
  91.1 15.1 %collective-permute-start.7 = (f32[8,128,128]{2,1,0:T(8,128)}, f32[8,128,128]{2,1,0:T(8,128)S(1)}, u32[]{:S(2)}, u32[]{:S(2)}) collective-permute-start(f32[8,128,128]{2,1,0:T(8,128)} %get-tuple-element.6), channel_id=1, source_target_pairs={{0,128},{128,0},{1,129},{129,1},{2,130},{130,2},{3,131},{131,3},{4... | collective-permute-start | bytes 1572872 | tf_op jit(solution)/shard_map/ppermute | solution.py:118

commit v3 on v2

v3 whole, which is shorter than its diff:
```python
import jax
import jax.numpy as jnp
import numpy as np
from jax import lax
from jax.experimental import pallas as pl
from jax.experimental.pallas import tpu as pltpu
from jax.sharding import Mesh, PartitionSpec as P

NAMES = ("s1", "s0", "zh", "y1", "y0", "x1", "x0", "core")
SIZES = (2, 2, 2, 4, 2, 2, 2, 2)
SEG = ("s1", "s0")
DP = ("zh", "y1", "y0", "x1", "x0", "core")
GA = ("s1", "zh", "y1")
GB = ("s0", "y0")
IDS = 128
SWAP = [(0, 1), (1, 0)]


def size_of(axes):
    return int(np.prod([SIZES[NAMES.index(a)] for a in axes]))


def halves_kernel(k_ref, weight_ref, kept_ref, given_ref, sems):
    depth = kept_ref.shape[1]
    mine = pl.multiple_of(k_ref[0] * depth, 128)
    rest = pl.multiple_of((1 - k_ref[0]) * depth, 128)
    copies = [
        pltpu.make_async_copy(weight_ref.at[:, pl.ds(mine, depth)], kept_ref, sems.at[0]),
        pltpu.make_async_copy(weight_ref.at[:, pl.ds(rest, depth)], given_ref, sems.at[1]),
    ]
    for copy in copies:
        copy.start()
    for copy in copies:
        copy.wait()


def halves_of(k, weight):
    half = jax.ShapeDtypeStruct((weight.shape[0], weight.shape[1] // 2), weight.dtype)
    anywhere = pl.BlockSpec(memory_space=pl.ANY)
    return pl.pallas_call(
        halves_kernel,
        in_specs=[pl.BlockSpec(memory_space=pltpu.SMEM), anywhere],
        out_specs=[anywhere] * 2,
        out_shape=[half, half],
        scratch_shapes=[pltpu.SemaphoreType.DMA((2,))],
        compiler_params=pltpu.CompilerParams(vmem_limit_bytes=56 * 1024 * 1024),
    )(k, weight)


def matmul_kernel(*refs):
    h_ref, pieces, (keep_ref, send_ref, id_ref) = refs[0], refs[1:9], refs[9:12]
    rows_in, held, turned, keep, send, row_sems, sems, keep_sems, send_sems = refs[12:]
    depth = pieces[0].shape[1]
    wide = h_ref.shape[-1]
    arrivals = [
        pltpu.make_async_copy(h_ref.at[b], rows_in.at[b], row_sems.at[b])
        for b in range(h_ref.shape[0])
    ]
    loads = [
        pltpu.make_async_copy(piece, held.at[j], sems.at[j])
        for j, piece in enumerate(pieces)
    ]
    for copy in arrivals + loads:
        copy.start()
    for copy in arrivals:
        copy.wait()
    kept = rows_in[:, 0].reshape(-1, wide)
    sent = rows_in[:, 1].reshape(-1, wide)
    half = kept.shape[0]
    turned[:, :half] = kept[:, :depth].T
    turned[:, half:] = sent[:, :depth].T
    code = kept[:, depth:].astype(jnp.float32).T
    id_ref[...] = (code[0:1] * 256.0 + code[1:2]).astype(jnp.int32)
    stores = []
    for j, load in enumerate(loads):
        load.wait()
        out = jnp.dot(held[j], turned[...], preferred_element_type=jnp.float32)
        send[j ^ 1] = out[:, half:]
        keep[j] = out[:, :half]
        stores += [
            pltpu.make_async_copy(send.at[j ^ 1], send_ref.at[j ^ 1], send_sems.at[j]),
            pltpu.make_async_copy(keep.at[j], keep_ref.at[j], keep_sems.at[j]),
        ]
        stores[-2].start()
        stores[-1].start()
    for copy in stores:
        copy.wait()


def partial_logits(gathered, pieces):
    nb, _, rows, _ = gathered.shape
    voc, depth = pieces[0].shape
    block = jax.ShapeDtypeStruct((len(pieces), voc, nb * rows), jnp.float32)
    anywhere = pl.BlockSpec(memory_space=pl.ANY)
    count = len(pieces)
    return pl.pallas_call(
        matmul_kernel,
        in_specs=[anywhere] * (1 + count),
        out_specs=[anywhere, anywhere, pl.BlockSpec(memory_space=pltpu.VMEM)],
        out_shape=[block, block, jax.ShapeDtypeStruct((1, nb * rows), jnp.int32)],
        scratch_shapes=[
            pltpu.VMEM(gathered.shape, gathered.dtype),
            pltpu.VMEM((count, voc, depth), gathered.dtype),
            pltpu.VMEM((depth, 2 * nb * rows), gathered.dtype),
            pltpu.VMEM(block.shape, jnp.float32),
            pltpu.VMEM(block.shape, jnp.float32),
            pltpu.SemaphoreType.DMA((nb,)),
            pltpu.SemaphoreType.DMA((count,)),
            pltpu.SemaphoreType.DMA((count,)),
            pltpu.SemaphoreType.DMA((count,)),
        ],
        compiler_params=pltpu.CompilerParams(vmem_limit_bytes=50 * 1024 * 1024),
    )(gathered, *pieces)


def stats_kernel(first_ref, mine_ref, theirs_ref, ids_ref, out_ref):
    pieces, voc, rows = mine_ref.shape
    logits = mine_ref[...] + theirs_ref[...]
    top = jnp.max(jnp.max(logits, axis=0), axis=0, keepdims=True)
    total = jnp.sum(jnp.sum(jnp.exp(logits - top[None]), axis=0), axis=0, keepdims=True)
    ids = ids_ref[...]
    entry = lax.broadcasted_iota(jnp.int32, (voc, rows), 0)
    picked = jnp.zeros((voc, rows), jnp.float32)
    for j in range(pieces):
        picked += jnp.where(entry + first_ref[j] == ids, logits[j], 0.0)
    picked = jnp.sum(picked, axis=0, keepdims=True)
    line = lax.broadcasted_iota(jnp.int32, (128, rows), 0)
    out_ref[...] = jnp.where(line == 0, top, jnp.where(line == 1, total, picked)).T


def local_stats(first, mine, theirs, ids):
    vmem = pl.BlockSpec(memory_space=pltpu.VMEM)
    return pl.pallas_call(
        stats_kernel,
        in_specs=[pl.BlockSpec(memory_space=pltpu.SMEM)] + [vmem] * 3,
        out_specs=vmem,
        out_shape=jax.ShapeDtypeStruct((mine.shape[2], 128), jnp.float32),
        compiler_params=pltpu.CompilerParams(vmem_limit_bytes=8 * 1024 * 1024),
    )(first, mine, theirs, ids)


def per_device(hidden, head_weight, target_ids, policy_logp):
    na, nb = size_of(GA), size_of(GB)
    rows, width = hidden.shape[1:]
    voc = head_weight.shape[0]
    depth = width // 2
    at = {a: lax.axis_index(a) for a in NAMES}
    k = at["x0"]

    ids = target_ids.reshape(rows, 1)
    lane = lax.broadcasted_iota(jnp.int32, (rows, IDS), 1)
    code = jnp.where(lane == 0, ids >> 8, ids & 255).astype(hidden.dtype)
    low, high = hidden[0, :, :depth], hidden[0, :, depth:]
    own = jnp.concatenate([jnp.where(k == 0, low, high), code], axis=1)
    other = jnp.concatenate([jnp.where(k == 0, high, low), code], axis=1)
    other = lax.ppermute(other, "x0", SWAP)

    kept, given = halves_of(k.reshape(1), head_weight)
    near = lax.ppermute(given, "x0", SWAP)
    back = lax.ppermute(given, ("x1", "x0"), [(i, i ^ 3) for i in range(4)])

    message = jnp.broadcast_to(jnp.stack([own, other])[None], (na, 2, rows, depth + IDS))
    column = lax.all_to_all(message, GA, 0, 0, tiled=True)
    column = column.transpose(1, 0, 2, 3).reshape(2 * na * rows, depth + IDS)
    column, near, back = lax.optimization_barrier((column, near, back))
    copies = jnp.broadcast_to(column[None], (nb,) + column.shape)
    gathered = lax.all_to_all(copies, GB, 0, 0, tiled=True)
    gathered = gathered.reshape(nb, 2, na * rows, depth + IDS)

    pieces = [kept, near, lax.ppermute(kept, "x1", SWAP), back]
    pieces += [lax.ppermute(piece, "core", SWAP) for piece in pieces]

    mine, send, ids = partial_logits(gathered, pieces)
    theirs = lax.ppermute(send, "x0", SWAP)

    firsts = []
    for j in range(len(pieces)):
        place = dict(at)
        place["x0"] = at["x0"] ^ (j & 1)
        place["x1"] = at["x1"] ^ ((j >> 1) & 1)
        place["core"] = at["core"] ^ (j >> 2)
        flat = 0
        for a, n in zip(NAMES, SIZES):
            flat = flat * n + place[a]
        firsts.append(flat * voc)
    stats = local_stats(jnp.stack(firsts), mine, theirs, ids)[:, :8]
    stats = stats.reshape(nb * na, rows, 8)
    stats = lax.all_to_all(stats, GB + GA, 0, 0, tiled=True)
    tops, totals, picks = stats[..., 0], stats[..., 1], stats[..., 2]
    highest = jnp.max(tops, axis=0)
    total = jnp.sum(totals * jnp.exp(tops - highest), axis=0)
    picked = jnp.sum(picks, axis=0)
    ref_logp = (picked - (highest + jnp.log(total))).reshape(1, rows)
    log_ratio = ref_logp - policy_logp
    kl_term = jnp.minimum(jnp.exp(log_ratio) - log_ratio - 1.0, 10.0)
    return (ref_logp, kl_term)


def solution(mesh):
    fine = Mesh(mesh.devices.reshape(SIZES), NAMES)
    return jax.shard_map(
        per_device,
        mesh=fine,
        in_specs=(P(SEG, DP, None), P(SEG + DP, None), P(SEG, DP), P(SEG, DP)),
        out_specs=(P(SEG, DP), P(SEG, DP)),
        check_vma=False,
    )
```

time: 134 us -> 188 us (1.40)
  Pallas kernels: 9.06 us -> 66 us
  blocking collectives: 24.4 us -> 51 us
  starting transfers between devices: 46 us -> 32.3 us
  waiting for transfers between devices: 39.5 us -> 28.7 us
  local copies, waits for them, and re-layouts: 11.1 us -> 5.4 us
    pallas_call x1 -> x2, Pallas kernels: 8.17 us -> 65.1 us  [the longest x1 56.7 us: halves_of(): pl.pallas_call(halves_kernel, in_specs=[pl.BlockSpec(memory_space=pltpu.S...]
    all_to_all x0 -> x1, blocking collectives: none -> 33.3 us  [per_device(): column = lax.all_to_all(message, GA, 0, 0, tiled=True)]
    all_to_all x1 -> x0, starting transfers between devices: 16.6 us -> none  [per_device(): column = lax.all_to_all(message, ('s0',) + GA, 0, 0, tiled=True)]
    all_to_all x1 -> x0, waiting for transfers between devices: 9.2 us -> none  [per_device(): column = lax.all_to_all(message, ('s0',) + GA, 0, 0, tiled=True)]
    all_to_all x1, blocking collectives: 24.4 us -> 17.7 us  [per_device(): stats = lax.all_to_all(stats, GB + GA, 0, 0, tiled=True)]
    ppermute x4 -> x5, starting transfers between devices: 10.9 us -> 14.8 us  [the longest x1 4.63 us: per_device(): back = lax.ppermute(given, ('x1', 'x0'), [(i, i ^ 3) for i in range(4)])]
    dynamic_slice x1 -> x0, local copies, waits for them, and re-layouts: 2.52 us -> none  [per_device(): given = lax.dynamic_slice_in_dim(head_weight, (1 - s0) * depth, depth, 1)]
    ppermute x4 -> x5, waiting for transfers between devices: 30.3 us -> 28 us  [the longest x1 14.6 us: per_device(): pieces = [kept, near, lax.ppermute(kept, 'x1', SWAP), back]]
  transfers between devices with their start and end apart: 10 -> 10, of which waited for: 4 -> 4; matrix products, arithmetic and copies ran while one was open for 4% -> 0% of each run, Pallas kernels for 0% -> 30%
where the time goes in v3:
time: 188 us; the launch traced here: 187 us
  Pallas kernels  66 us (35%)
  blocking collectives  51 us (27%)
  starting transfers between devices  32.3 us (17%)
  waiting for transfers between devices  28.7 us (15%)
  local copies, waits for them, and re-layouts  5.4 us (3%)
  other arithmetic  2.67 us (1%)
    pallas_call x1, Pallas kernels, halves_of(): pl.pallas_call(halves_kernel, in_specs=[pl.BlockSpec(memory_space=pltpu.S...  56.7 us
    all_to_all x1, blocking collectives, per_device(): column = lax.all_to_all(message, GA, 0, 0, tiled=True)  33.3 us
    all_to_all x1, blocking collectives, per_device(): stats = lax.all_to_all(stats, GB + GA, 0, 0, tiled=True)  17.7 us
    ppermute x1, waiting for transfers between devices, per_device(): pieces = [kept, near, lax.ppermute(kept, 'x1', SWAP), back]  14.6 us
    ppermute x1, waiting for transfers between devices, per_device(): theirs = lax.ppermute(send, 'x0', SWAP)  13.4 us
    ppermute x4, starting transfers between devices, per_device(): pieces += [lax.ppermute(piece, 'core', SWAP) for piece in pieces]  12.9 us
    pallas_call x1, Pallas kernels, partial_logits(): pl.pallas_call(matmul_kernel, in_specs=[anywhere] * (1 + count), out_spec...  8.37 us
    ppermute x1, starting transfers between devices, per_device(): back = lax.ppermute(given, ('x1', 'x0'), [(i, i ^ 3) for i in range(4)])  4.63 us
  transfers between devices with their start and end apart: 10, of which 4 were waited for; matrix products, arithmetic and copies ran while one was open for 0% of the time, Pallas kernels for 30%

profile of v3, /device:TPU:1, one launch (start us, length us, event | category | flops | bytes accessed | tf_op | source)
XLA Modules:
  0.0 187.0 jit_solution(9027201762451824746)
XLA Ops:
  0.6 0.7 shift-right-arithmetic_bitcast_fusion
  1.3 0.8 fusion.1
  2.1 0.1 select_convert_fusion
  2.2 3.9 %collective-permute-start = (bf16[2,3712]{1,0:T(2,128)(2,1)S(1)}, bf16[2,3712]{1,0:T(2,128)(2,1)S(1)}, u32[]{:S(2)}, u32[]{:S(2)}) collective-permute-start(bf16[2,3712]{1,0:T(2,128)(2,1)S(1)} %get-tuple-element.29), channel_id=1, source_target_pairs={{0,2},{2,0},{1,3},{3,1},{4,6},{6,4},{5,7},{7,5},{8,10},{10,8},{9,1... | collective-permute-start | bytes 44552 | tf_op jit(solution)/shard_map/ppermute | solution.py:156
  6.1 56.7 %shard_map.59 = (bf16[128,3584]{1,0:T(8,128)(2,1)}, bf16[128,3584]{1,0:T(8,128)(2,1)}) custom-call(s32[1]{0:T(128)} %bitcast.15.k_ref, bf16[128,7168]{1,0:T(8,128)(2,1)} %weight_ref.1), custom_call_target="tpu_custom_call" | custom-call | tf_op jit(solution)/shard_map/pallas_call | solution.py:40
  62.9 1.9 %collective-permute-start.1 = (bf16[128,3584]{1,0:T(8,128)(2,1)}, bf16[128,3584]{1,0:T(8,128)(2,1)S(1)}, u32[]{:S(2)}, u32[]{:S(2)}) collective-permute-start(bf16[128,3584]{1,0:T(8,128)(2,1)} %get-tuple-element.10), channel_id=1, source_target_pairs={{0,2},{2,0},{1,3},{3,1},{4,6},{6,4},{5,7},{7,5},{8,10},{10,8},{9,1... | collective-permute-start | bytes 2752520 | tf_op jit(solution)/shard_map/ppermute | solution.py:159
  64.8 4.6 %collective-permute-start.2 = (bf16[128,3584]{1,0:T(8,128)(2,1)}, bf16[128,3584]{1,0:T(8,128)(2,1)S(1)}, u32[]{:S(2)}, u32[]{:S(2)}) collective-permute-start(bf16[128,3584]{1,0:T(8,128)(2,1)} %get-tuple-element.10), channel_id=1, source_target_pairs={{0,6},{2,4},{4,2},{6,0},{1,7},{3,5},{5,3},{7,1},{8,14},{10,12},{12... | collective-permute-start | bytes 2752520 | tf_op jit(solution)/shard_map/ppermute | solution.py:160
  69.4 0.0 collective-permute-done
  69.5 0.2 broadcast_in_dim.31
  69.7 33.3 %all_to_all.15 = bf16[16,2,2,3712]{3,2,1,0:T(2,128)(2,1)S(1)} all-to-all(bf16[16,2,2,3712]{3,2,1,0:T(2,128)(2,1)S(1)} %broadcast_in_dim.31), channel_id=1, replica_groups=mesh['s1'=2,'s0'=2,'zh'=2,'y1'=4,'y0'=2,'x1'=2,'x0'=2,'core'=2] {'s1','z..., dimensions={0} | all-to-all | bytes 950272 | tf_op jit(solution)/shard_map/all_to_all | solution.py:163
  103.0 0.3 copy.14
  103.3 0.2 reshape.67
  103.5 0.0 collective-permute-done.1.refs_2_
  103.5 0.0 collective-permute-done.2.refs_4_
  103.5 0.0 copy-start.1
  103.6 0.9 copy-done.1
  104.5 1.4 broadcast_in_dim.32
  105.8 0.0 copy-start
  105.8 4.5 %all-to-all-start.1 = ((bf16[4,64,3712]{2,1,0:T(8,128)(2,1)}), bf16[4,64,3712]{2,1,0:T(8,128)(2,1)}, u32[]{:S(2)}, u32[]{:S(2)}) async-start(bf16[4,64,3712]{2,1,0:T(8,128)(2,1)} %broadcast_in_dim.32), calls=%async_computation.1 | async-start | bytes 3801088 | tf_op jit(solution)/shard_map/all_to_all | solution.py:167
  110.4 0.0 copy-done
  110.4 2.4 %collective-permute-start.3 = (bf16[128,3584]{1,0:T(8,128)(2,1)S(1)}, bf16[128,3584]{1,0:T(8,128)(2,1)S(1)}, u32[]{:S(2)}, u32[]{:S(2)}) collective-permute-start(bf16[128,3584]{1,0:T(8,128)(2,1)S(1)} %copy-done), channel_id=1, source_target_pairs={{0,4},{4,0},{1,5},{5,1},{2,6},{6,2},{3,7},{7,3},{8,12},{12,8},{9,1... | collective-permute-start | bytes 2752520 | tf_op jit(solution)/shard_map/ppermute | solution.py:170
  112.8 4.2 %collective-permute-start.4 = (bf16[128,3584]{1,0:T(8,128)(2,1)S(1)}, bf16[128,3584]{1,0:T(8,128)(2,1)S(1)}, u32[]{:S(2)}, u32[]{:S(2)}) collective-permute-start(bf16[128,3584]{1,0:T(8,128)(2,1)S(1)} %copy-done), channel_id=1, source_target_pairs={{0,1},{1,0},{2,3},{3,2},{4,5},{5,4},{6,7},{7,6},{8,9},{9,8},{10,11... | collective-permute-start | bytes 2752520 | tf_op jit(solution)/shard_map/ppermute | solution.py:171
  117.1 1.9 %collective-permute-start.5 = (bf16[128,3584]{1,0:T(8,128)(2,1)S(1)}, bf16[128,3584]{1,0:T(8,128)(2,1)S(1)}, u32[]{:S(2)}, u32[]{:S(2)}) collective-permute-start(bf16[128,3584]{1,0:T(8,128)(2,1)S(1)} %collective-permute-done.1.refs_2_), channel_id=1, source_target_pairs={{0,1},{1,0},{2,3},{3,2},{4,5},{5,4},{6,7},{7,6},{8,9},{9,8},{10,11... | collective-permute-start | bytes 2752520 | tf_op jit(solution)/shard_map/ppermute | solution.py:171
  119.0 14.6 %collective-permute-done.3.refs_3_ = bf16[128,3584]{1,0:T(8,128)(2,1)S(1)} collective-permute-done((bf16[128,3584]{1,0:T(8,128)(2,1)S(1)}, bf16[128,3584]{1,0:T(8,128)(2,1)S(1)}, u32[]{:S(2)}, u32[]{:S(2)}) %collective-permute-start.3) | collective-permute-done | bytes 917536 | tf_op jit(solution)/shard_map/ppermute | solution.py:170
  133.6 4.9 %collective-permute-start.6 = (bf16[128,3584]{1,0:T(8,128)(2,1)S(1)}, bf16[128,3584]{1,0:T(8,128)(2,1)S(1)}, u32[]{:S(2)}, u32[]{:S(2)}) collective-permute-start(bf16[128,3584]{1,0:T(8,128)(2,1)S(1)} %collective-permute-done.3.refs_3_), channel_id=1, source_target_pairs={{0,1},{1,0},{2,3},{3,2},{4,5},{5,4},{6,7},{7,6},{8,9},{9,8},{10,11... | collective-permute-start | bytes 2752520 | tf_op jit(solution)/shard_map/ppermute | solution.py:171
  138.5 1.9 %collective-permute-start.7 = (bf16[128,3584]{1,0:T(8,128)(2,1)}, bf16[128,3584]{1,0:T(8,128)(2,1)}, u32[]{:S(2)}, u32[]{:S(2)}) collective-permute-start(bf16[128,3584]{1,0:T(8,128)(2,1)} %copy-done.1), channel_id=1, source_target_pairs={{0,1},{1,0},{2,3},{3,2},{4,5},{5,4},{6,7},{7,6},{8,9},{9,8},{10,11... | collective-permute-start | bytes 2752520 | tf_op jit(solution)/shard_map/ppermute | solution.py:171
  140.4 0.0 collective-permute-done.4.refs_5_
  140.4 0.0 copy-start.2
  140.4 0.0 collective-permute-done.5.refs_6_
  140.4 0.0 copy-start.3
  140.4 0.1 collective-permute-done.6.refs_7_
  140.5 0.8 copy-done.2
  141.4 0.4 copy-done.3
  141.7 0.0 copy-start.4
  141.7 0.9 copy-done.4
  142.6 0.5 collective-permute-done.7.refs_8_
  143.2 0.0 all-to-all-done.1
  143.2 0.0 copy-start.5
  143.2 8.4 %shard_map.60 = (f32[8,128,128]{2,1,0:T(8,128)S(1)}, f32[8,128,128]{2,1,0:T(8,128)}, s32[1,128]{1,0:T(1,128)S(1)}) custom-call(bf16[4,2,32,3712]{3,2,1,0:T(8,128)(2,1)} %bitcast.16.refs_0_, bf16[128,3584]{1,0:T(8,128)(2,1)S(1)} %copy-done, bf16[128,3584]{1,0:T(8,128)(2,1)S(1)} %collective-permute-done.1.refs_2_, ...), custom_call_target="tpu_custom_call" | custom-call | tf_op jit(solution)/shard_map/pallas_call | solution.py:96
  151.6 1.9 %collective-permute-start.8 = (f32[8,128,128]{2,1,0:T(8,128)}, f32[8,128,128]{2,1,0:T(8,128)S(1)}, u32[]{:S(2)}, u32[]{:S(2)}) collective-permute-start(f32[8,128,128]{2,1,0:T(8,128)} %get-tuple-element.16), channel_id=1, source_target_pairs={{0,2},{2,0},{1,3},{3,1},{4,6},{6,4},{5,7},{7,5},{8,10},{10,8},{9,1... | collective-permute-start | bytes 1572872 | tf_op jit(solution)/shard_map/ppermute | solution.py:174
  153.5 0.1 stack.44.first_ref
  153.6 13.4 %collective-permute-done.8.theirs_ref = f32[8,128,128]{2,1,0:T(8,128)S(1)} collective-permute-done((f32[8,128,128]{2,1,0:T(8,128)}, f32[8,128,128]{2,1,0:T(8,128)S(1)}, u32[]{:S(2)}, u32[]{:S(2)}) %collective-permute-start.8) | collective-permute-done | bytes 524320 | tf_op jit(solution)/shard_map/ppermute | solution.py:174
  167.1 0.9 shard_map.61
  168.0 17.7 %all_to_all.16 = f32[64,2,8]{2,1,0:T(2,128)S(1)} all-to-all(f32[64,2,8]{2,1,0:T(2,128)S(1)} %bitcast.37), channel_id=1, replica_groups=mesh['s1'=2,'s0'=2,'zh'=2,'y1'=4,'y0'=2,'x1'=2,'x0'=2,'core'=2] {'s0','y..., dimensions={0} | all-to-all | bytes 8192 | tf_op jit(solution)/shard_map/all_to_all | solution.py:188
  185.7 0.4 fusion.8
  186.0 0.1 copy.16
  186.1 0.1 copy.15
  186.2 0.2 fusion.5
  186.4 0.0 copy-done.5
  186.4 0.5 fusion.7
  (3 shorter events, 0.1 us)
Async XLA Ops:
  2.2 67.2 %collective-permute-start = (bf16[2,3712]{1,0:T(2,128)(2,1)S(1)}, bf16[2,3712]{1,0:T(2,128)(2,1)S(1)}, u32[]{:S(2)}, u32[]{:S(2)}) collective-permute-start(bf16[2,3712]{1,0:T(2,128)(2,1)S(1)} %get-tuple-element.29), channel_id=1, source_target_pairs={{0,2},{2,0},{1,3},{3,1},{4,6},{6,4},{5,7},{7,5},{8,10},{10,8},{9,1... | collective-permute-start | bytes 44552 | tf_op jit(solution)/shard_map/ppermute | solution.py:156
  62.9 40.7 %collective-permute-start.1 = (bf16[128,3584]{1,0:T(8,128)(2,1)}, bf16[128,3584]{1,0:T(8,128)(2,1)S(1)}, u32[]{:S(2)}, u32[]{:S(2)}) collective-permute-start(bf16[128,3584]{1,0:T(8,128)(2,1)} %get-tuple-element.10), channel_id=1, source_target_pairs={{0,2},{2,0},{1,3},{3,1},{4,6},{6,4},{5,7},{7,5},{8,10},{10,8},{9,1... | collective-permute-start | bytes 2752520 | tf_op jit(solution)/shard_map/ppermute | solution.py:159
  64.8 38.7 %collective-permute-start.2 = (bf16[128,3584]{1,0:T(8,128)(2,1)}, bf16[128,3584]{1,0:T(8,128)(2,1)S(1)}, u32[]{:S(2)}, u32[]{:S(2)}) collective-permute-start(bf16[128,3584]{1,0:T(8,128)(2,1)} %get-tuple-element.10), channel_id=1, source_target_pairs={{0,6},{2,4},{4,2},{6,0},{1,7},{3,5},{5,3},{7,1},{8,14},{10,12},{12... | collective-permute-start | bytes 2752520 | tf_op jit(solution)/shard_map/ppermute | solution.py:160
  103.5 0.9 copy-start.1
  105.8 4.6 %copy-start = (bf16[128,3584]{1,0:T(8,128)(2,1)S(1)}, bf16[128,3584]{1,0:T(8,128)(2,1)}, u32[]{:S(2)}) copy-start(bf16[128,3584]{1,0:T(8,128)(2,1)} %get-tuple-element.12.refs_1_) | copy-start | bytes 2752516
  105.8 37.3 %all-to-all-start.1 = ((bf16[4,64,3712]{2,1,0:T(8,128)(2,1)}), bf16[4,64,3712]{2,1,0:T(8,128)(2,1)}, u32[]{:S(2)}, u32[]{:S(2)}) async-start(bf16[4,64,3712]{2,1,0:T(8,128)(2,1)} %broadcast_in_dim.32), calls=%async_computation.1 | async-start | bytes 3801088 | tf_op jit(solution)/shard_map/all_to_all | solution.py:167
  110.4 23.2 %collective-permute-start.3 = (bf16[128,3584]{1,0:T(8,128)(2,1)S(1)}, bf16[128,3584]{1,0:T(8,128)(2,1)S(1)}, u32[]{:S(2)}, u32[]{:S(2)}) collective-permute-start(bf16[128,3584]{1,0:T(8,128)(2,1)S(1)} %copy-done), channel_id=1, source_target_pairs={{0,4},{4,0},{1,5},{5,1},{2,6},{6,2},{3,7},{7,3},{8,12},{12,8},{9,1... | collective-permute-start | bytes 2752520 | tf_op jit(solution)/shard_map/ppermute | solution.py:170
  112.8 27.6 %collective-permute-start.4 = (bf16[128,3584]{1,0:T(8,128)(2,1)S(1)}, bf16[128,3584]{1,0:T(8,128)(2,1)S(1)}, u32[]{:S(2)}, u32[]{:S(2)}) collective-permute-start(bf16[128,3584]{1,0:T(8,128)(2,1)S(1)} %copy-done), channel_id=1, source_target_pairs={{0,1},{1,0},{2,3},{3,2},{4,5},{5,4},{6,7},{7,6},{8,9},{9,8},{10,11... | collective-permute-start | bytes 2752520 | tf_op jit(solution)/shard_map/ppermute | solution.py:171
  117.1 23.3 %collective-permute-start.5 = (bf16[128,3584]{1,0:T(8,128)(2,1)S(1)}, bf16[128,3584]{1,0:T(8,128)(2,1)S(1)}, u32[]{:S(2)}, u32[]{:S(2)}) collective-permute-start(bf16[128,3584]{1,0:T(8,128)(2,1)S(1)} %collective-permute-done.1.refs_2_), channel_id=1, source_target_pairs={{0,1},{1,0},{2,3},{3,2},{4,5},{5,4},{6,7},{7,6},{8,9},{9,8},{10,11... | collective-permute-start | bytes 2752520 | tf_op jit(solution)/shard_map/ppermute | solution.py:171
  133.6 7.0 %collective-permute-start.6 = (bf16[128,3584]{1,0:T(8,128)(2,1)S(1)}, bf16[128,3584]{1,0:T(8,128)(2,1)S(1)}, u32[]{:S(2)}, u32[]{:S(2)}) collective-permute-start(bf16[128,3584]{1,0:T(8,128)(2,1)S(1)} %collective-permute-done.3.refs_3_), channel_id=1, source_target_pairs={{0,1},{1,0},{2,3},{3,2},{4,5},{5,4},{6,7},{7,6},{8,9},{9,8},{10,11... | collective-permute-start | bytes 2752520 | tf_op jit(solution)/shard_map/ppermute | solution.py:171
  138.5 4.7 %collective-permute-start.7 = (bf16[128,3584]{1,0:T(8,128)(2,1)}, bf16[128,3584]{1,0:T(8,128)(2,1)}, u32[]{:S(2)}, u32[]{:S(2)}) collective-permute-start(bf16[128,3584]{1,0:T(8,128)(2,1)} %copy-done.1), channel_id=1, source_target_pairs={{0,1},{1,0},{2,3},{3,2},{4,5},{5,4},{6,7},{7,6},{8,9},{9,8},{10,11... | collective-permute-start | bytes 2752520 | tf_op jit(solution)/shard_map/ppermute | solution.py:171
  140.4 0.9 copy-start.2
  140.4 1.3 copy-start.3
  141.7 0.9 copy-start.4
  143.2 43.2 %copy-start.5 = (f32[1,2]{1,0:T(1,128)S(1)}, f32[1,2]{1,0:T(1,128)}, u32[]{:S(2)}) copy-start(f32[1,2]{1,0:T(1,128)} %param.7) | copy-start | bytes 28
  151.6 15.5 %collective-permute-start.8 = (f32[8,128,128]{2,1,0:T(8,128)}, f32[8,128,128]{2,1,0:T(8,128)S(1)}, u32[]{:S(2)}, u32[]{:S(2)}) collective-permute-start(f32[8,128,128]{2,1,0:T(8,128)} %get-tuple-element.16), channel_id=1, source_target_pairs={{0,2},{2,0},{1,3},{3,1},{4,6},{6,4},{5,7},{7,5},{8,10},{10,8},{9,1... | collective-permute-start | bytes 1572872 | tf_op jit(solution)/shard_map/ppermute | solution.py:174

commit v4 on v3

v4 whole, which is shorter than its diff:
```python
import jax
import jax.numpy as jnp
import numpy as np
from jax import lax
from jax.experimental import pallas as pl
from jax.experimental.pallas import tpu as pltpu
from jax.sharding import Mesh, PartitionSpec as P

NAMES = ("s1", "s0", "zh", "y1", "y0", "x1", "x0", "core")
SIZES = (2, 2, 2, 4, 2, 2, 2, 2)
SEG = ("s1", "s0")
DP = ("zh", "y1", "y0", "x1", "x0", "core")
GA = ("s1", "zh", "y1")
GB = ("s0", "y0")
KG = ("x1", "x0")
IDS = 128
SWAP = [(0, 1), (1, 0)]


def size_of(axes):
    return int(np.prod([SIZES[NAMES.index(a)] for a in axes]))


def matmul_kernel(x_ref, *refs):
    h_ref, pieces, (out_ref, id_ref) = refs[0], refs[1:9], refs[9:11]
    rows_in, held, turned, parts, row_sems, sems, out_sems = refs[11:]
    x = x_ref[0]
    depth = pieces[0].shape[1]
    nb, nk, _, wide = rows_in.shape
    arrivals = [
        pltpu.make_async_copy(h_ref.at[b], rows_in.at[b], row_sems.at[b])
        for b in range(nb)
    ]
    loads = [
        pltpu.make_async_copy(piece, held.at[j], sems.at[j])
        for j, piece in enumerate(pieces)
    ]
    for copy in arrivals + loads:
        copy.start()
    for copy in arrivals:
        copy.wait()
    for k in range(nk):
        rows = rows_in[:, k, :, :depth].reshape(-1, depth)
        width = rows.shape[0]
        turned[:, k * width : (k + 1) * width] = rows.T
    code = rows_in[:, x, :, depth:].reshape(-1, wide - depth).astype(jnp.float32).T
    id_ref[...] = (code[0:1] * 256.0 + code[1:2]).astype(jnp.int32)
    stores = []
    for j, load in enumerate(loads):
        load.wait()
        out = jnp.dot(held[j], turned[...], preferred_element_type=jnp.float32)
        slot = nk * (j // nk) + (x ^ (j % nk))
        for k in range(nk):
            parts[k, slot] = out[:, k * width : (k + 1) * width]
        stores.append(
            pltpu.make_async_copy(parts.at[:, slot], out_ref.at[:, slot], out_sems.at[j])
        )
        stores[-1].start()
    for copy in stores:
        copy.wait()


def partial_logits(x, gathered, pieces):
    nb, nk, rows, _ = gathered.shape
    voc, depth = pieces[0].shape
    count = len(pieces)
    block = (nk, count, voc, nb * rows)
    anywhere = pl.BlockSpec(memory_space=pl.ANY)
    return pl.pallas_call(
        matmul_kernel,
        in_specs=[pl.BlockSpec(memory_space=pltpu.SMEM)] + [anywhere] * (1 + count),
        out_specs=[anywhere, pl.BlockSpec(memory_space=pltpu.VMEM)],
        out_shape=[
            jax.ShapeDtypeStruct(block, jnp.float32),
            jax.ShapeDtypeStruct((1, nb * rows), jnp.int32),
        ],
        scratch_shapes=[
            pltpu.VMEM(gathered.shape, gathered.dtype),
            pltpu.VMEM((count, voc, depth), gathered.dtype),
            pltpu.VMEM((depth, nk * nb * rows), gathered.dtype),
            pltpu.VMEM(block, jnp.float32),
            pltpu.SemaphoreType.DMA((nb,)),
            pltpu.SemaphoreType.DMA((count,)),
            pltpu.SemaphoreType.DMA((count,)),
        ],
        compiler_params=pltpu.CompilerParams(vmem_limit_bytes=50 * 1024 * 1024),
    )(x, gathered, *pieces)


def stats_kernel(first_ref, parts_ref, ids_ref, out_ref):
    nk, pieces, voc, rows = parts_ref.shape
    logits = parts_ref[0]
    for k in range(1, nk):
        logits += parts_ref[k]
    top = jnp.max(jnp.max(logits, axis=0), axis=0, keepdims=True)
    total = jnp.sum(jnp.sum(jnp.exp(logits - top[None]), axis=0), axis=0, keepdims=True)
    ids = ids_ref[...]
    entry = lax.broadcasted_iota(jnp.int32, (voc, rows), 0)
    picked = jnp.zeros((voc, rows), jnp.float32)
    for j in range(pieces):
        picked += jnp.where(entry + first_ref[j] == ids, logits[j], 0.0)
    picked = jnp.sum(picked, axis=0, keepdims=True)
    line = lax.broadcasted_iota(jnp.int32, (128, rows), 0)
    out_ref[...] = jnp.where(line == 0, top, jnp.where(line == 1, total, picked)).T


def local_stats(first, parts, ids):
    vmem = pl.BlockSpec(memory_space=pltpu.VMEM)
    return pl.pallas_call(
        stats_kernel,
        in_specs=[pl.BlockSpec(memory_space=pltpu.SMEM), vmem, vmem],
        out_specs=vmem,
        out_shape=jax.ShapeDtypeStruct((parts.shape[3], 128), jnp.float32),
        compiler_params=pltpu.CompilerParams(vmem_limit_bytes=8 * 1024 * 1024),
    )(first, parts, ids)


def per_device(hidden, head_weight, target_ids, policy_logp):
    na, nb, nk = size_of(GA), size_of(GB), size_of(KG)
    rows, width = hidden.shape[1:]
    voc = head_weight.shape[0]
    depth = width // nk
    at = {a: lax.axis_index(a) for a in NAMES}
    x = lax.axis_index(KG)

    ids = target_ids.reshape(rows, 1)
    lane = lax.broadcasted_iota(jnp.int32, (rows, IDS), 1)
    code = jnp.where(lane == 0, ids >> 8, ids & 255).astype(hidden.dtype)
    quarters = [
        jnp.concatenate([hidden[0, :, j * depth : (j + 1) * depth], code], axis=1)
        for j in range(nk)
    ]
    quarter = lax.all_to_all(jnp.stack(quarters), KG, 0, 0, tiled=True)
    quarter = quarter.reshape(nk * rows, depth + IDS)

    def far(j):
        piece = lax.dynamic_slice_in_dim(head_weight, (x ^ j) * depth, depth, 1)
        if j == 0:
            return piece
        return lax.ppermute(piece, KG, [(i, i ^ j) for i in range(nk)])

    pieces = [far(j) for j in range(nk)]

    message = jnp.broadcast_to(quarter[None], (na,) + quarter.shape)
    column = lax.all_to_all(message, GA, 0, 0, tiled=True)
    column = column.reshape(na, nk, rows, depth + IDS).transpose(1, 0, 2, 3)
    column = column.reshape(nk * na * rows, depth + IDS)
    column, pieces[1], pieces[3] = lax.optimization_barrier((column, pieces[1], pieces[3]))
    copies = jnp.broadcast_to(column[None], (nb,) + column.shape)
    gathered = lax.all_to_all(copies, GB, 0, 0, tiled=True)
    gathered = gathered.reshape(nb, nk, na * rows, depth + IDS)

    pieces += [lax.ppermute(piece, "core", SWAP) for piece in pieces]

    parts, ids = partial_logits(x.reshape(1), gathered, pieces)
    parts = lax.all_to_all(parts, KG, 0, 0, tiled=True)

    firsts = []
    for j in range(len(pieces)):
        place = dict(at)
        place["x1"], place["x0"] = (j >> 1) & 1, j & 1
        place["core"] = at["core"] ^ (j // nk)
        flat = 0
        for a, n in zip(NAMES, SIZES):
            flat = flat * n + place[a]
        firsts.append(flat * voc)
    stats = local_stats(jnp.stack(firsts), parts, ids)[:, :8]
    stats = stats.reshape(nb * na, rows, 8)
    stats = lax.all_to_all(stats, GB + GA, 0, 0, tiled=True)
    tops, totals, picks = stats[..., 0], stats[..., 1], stats[..., 2]
    highest = jnp.max(tops, axis=0)
    total = jnp.sum(totals * jnp.exp(tops - highest), axis=0)
    picked = jnp.sum(picks, axis=0)
    ref_logp = (picked - (highest + jnp.log(total))).reshape(1, rows)
    log_ratio = ref_logp - policy_logp
    kl_term = jnp.minimum(jnp.exp(log_ratio) - log_ratio - 1.0, 10.0)
    return (ref_logp, kl_term)


def solution(mesh):
    fine = Mesh(mesh.devices.reshape(SIZES), NAMES)
    return jax.shard_map(
        per_device,
        mesh=fine,
        in_specs=(P(SEG, DP, None), P(SEG + DP, None), P(SEG, DP), P(SEG, DP)),
        out_specs=(P(SEG, DP), P(SEG, DP)),
        check_vma=False,
    )
```

time: 188 us -> 137 us (0.73)
  Pallas kernels: 66 us -> 7.85 us
  blocking collectives: 51 us -> 27.6 us
  waiting for transfers between devices: 28.7 us -> 46.8 us
  starting transfers between devices: 32.3 us -> 44.1 us
    pallas_call x2 -> x1, Pallas kernels: 65.1 us -> 6.86 us  [partial_logits(): pl.pallas_call(matmul_kernel, in_specs=[pl.BlockSpec(memory_space=pltpu.S...]
    all_to_all x0 -> x2, waiting for transfers between devices: none -> 38.8 us  [the longest x1 25.9 us: per_device(): parts = lax.all_to_all(parts, KG, 0, 0, tiled=True)]
    all_to_all x1, blocking collectives: 33.3 us -> 8.93 us  [per_device(): quarter = lax.all_to_all(jnp.stack(quarters), KG, 0, 0, tiled=True)]
    ppermute x5 -> x3, waiting for transfers between devices: 28 us -> 6.6 us  [far(): return lax.ppermute(piece, KG, [(i, i ^ j) for i in range(nk)])]
    all_to_all x0 -> x2, starting transfers between devices: none -> 19 us  [the longest x1 15.4 us: per_device(): column = lax.all_to_all(message, GA, 0, 0, tiled=True)]
    ppermute x5 -> x3, starting transfers between devices: 14.8 us -> 7.45 us  [far(): return lax.ppermute(piece, KG, [(i, i ^ j) for i in range(nk)])]
  transfers between devices with their start and end apart: 10 -> 10, of which waited for: 4 -> 4; matrix products, arithmetic and copies ran while one was open for 0% -> 1% of each run, Pallas kernels for 30% -> 0%
where the time goes in v4:
time: 137 us; the launch traced here: 136 us
  waiting for transfers between devices  46.8 us (34%)
  starting transfers between devices  44.1 us (32%)
  blocking collectives  27.6 us (20%)
  Pallas kernels  7.85 us (6%)
  local copies, waits for them, and re-layouts  6.86 us (5%)
  other arithmetic  2.05 us (1%)
    all_to_all x1, waiting for transfers between devices, per_device(): parts = lax.all_to_all(parts, KG, 0, 0, tiled=True)  25.9 us
    all_to_all x1, blocking collectives, per_device(): stats = lax.all_to_all(stats, GB + GA, 0, 0, tiled=True)  18.6 us
    all_to_all x1, starting transfers between devices, per_device(): column = lax.all_to_all(message, GA, 0, 0, tiled=True)  15.4 us
    ppermute x4, starting transfers between devices, per_device(): pieces += [lax.ppermute(piece, 'core', SWAP) for piece in pieces]  13.2 us
    all_to_all x1, waiting for transfers between devices, per_device(): column = lax.all_to_all(message, GA, 0, 0, tiled=True)  12.9 us
    all_to_all x1, blocking collectives, per_device(): quarter = lax.all_to_all(jnp.stack(quarters), KG, 0, 0, tiled=True)  8.93 us
    ppermute x3, starting transfers between devices, far(): return lax.ppermute(piece, KG, [(i, i ^ j) for i in range(nk)])  7.45 us
    pallas_call x1, Pallas kernels, partial_logits(): pl.pallas_call(matmul_kernel, in_specs=[pl.BlockSpec(memory_space=pltpu.S...  6.86 us
  transfers between devices with their start and end apart: 10, of which 4 were waited for; matrix products, arithmetic and copies ran while one was open for 1% of the time, Pallas kernels for 0%

profile of v4, /device:TPU:1, one launch (start us, length us, event | category | flops | bytes accessed | tf_op | source)
XLA Modules:
  0.0 136.1 jit_solution(938439938524109001)
XLA Ops:
  0.6 0.0 copy-start.2
  0.7 0.8 shift-right-arithmetic_bitcast_fusion
  1.4 0.8 slice_bitcast_fusion.3
  2.2 0.1 select_convert_fusion
  2.3 0.1 pad_maximum_fusion
  2.4 8.9 %all_to_all.25 = bf16[4,2,1920]{2,1,0:T(2,128)(2,1)S(1)} all-to-all(bf16[4,2,1920]{2,1,0:T(2,128)(2,1)S(1)} %pad_maximum_fusion), channel_id=1, replica_groups=mesh['s1'=2,'s0'=2,'zh'=2,'y1'=4,'y0'=2,'x1'=2,'x0'=2,'core'=2] {'x1','x0'}, dimensions={0} | all-to-all | bytes 61440 | tf_op jit(solution)/shard_map/all_to_all | solution.py:133
  11.3 0.8 broadcast_in_dim.33
  12.2 15.4 %all-to-all-start.1 = ((bf16[16,8,1920]{2,1,0:T(8,128)(2,1)}), bf16[16,8,1920]{2,1,0:T(8,128)(2,1)S(1)}, u32[]{:S(2)}, u32[]{:S(2)}) async-start(bf16[16,8,1920]{2,1,0:T(8,128)(2,1)} %broadcast_in_dim.33), calls=%async_computation.1 | async-start | bytes 983040 | tf_op jit(solution)/shard_map/all_to_all | solution.py:145
  27.6 0.0 copy-done.2
  27.6 1.1 constant_dynamic-slice_fusion
  28.7 2.8 %collective-permute-start.1 = (bf16[128,1792]{1,0:T(8,128)(2,1)}, bf16[128,1792]{1,0:T(8,128)(2,1)S(1)}, u32[]{:S(2)}, u32[]{:S(2)}) collective-permute-start(bf16[128,1792]{1,0:T(8,128)(2,1)} %get-tuple-element.17), channel_id=1, source_target_pairs={{0,6},{2,4},{4,2},{6,0},{1,7},{3,5},{5,3},{7,1},{8,14},{10,12},{12... | collective-permute-start | bytes 1376264 | tf_op jit(solution)/shard_map/ppermute | solution.py:140
  31.5 1.9 %collective-permute-start = (bf16[128,1792]{1,0:T(8,128)(2,1)}, bf16[128,1792]{1,0:T(8,128)(2,1)S(1)}, u32[]{:S(2)}, u32[]{:S(2)}) collective-permute-start(bf16[128,1792]{1,0:T(8,128)(2,1)} %get-tuple-element.18), channel_id=1, source_target_pairs={{0,2},{2,0},{4,6},{6,4},{1,3},{3,1},{5,7},{7,5},{8,10},{10,8},{12,... | collective-permute-start | bytes 1376264 | tf_op jit(solution)/shard_map/ppermute | solution.py:140
  33.4 12.9 %all-to-all-done.1 = bf16[16,8,1920]{2,1,0:T(8,128)(2,1)S(1)} async-done(((bf16[16,8,1920]{2,1,0:T(8,128)(2,1)}), bf16[16,8,1920]{2,1,0:T(8,128)(2,1)S(1)}, u32[]{:S(2)}, u32[]{:S(2)}) %all-to-all-start.1) | async-done | bytes 491552 | tf_op jit(solution)/shard_map/all_to_all | solution.py:145
  46.3 0.1 copy.15
  46.4 0.4 copy.16
  46.7 0.2 reshape.68
  46.9 0.0 collective-permute-done.1.refs_4_
  47.0 0.0 collective-permute-done.refs_2_
  47.0 1.5 %broadcast_in_dim.34 = bf16[4,128,1920]{2,1,0:T(8,128)(2,1)} broadcast(bf16[128,1920]{1,0:T(8,128)(2,1)S(1)} %reshape.68), dimensions={1,2} | broadcast | bytes 2457600 | tf_op jit(solution)/shard_map/broadcast_in_dim | solution.py:149
  48.4 4.4 %all-to-all-start.2 = ((bf16[4,128,1920]{2,1,0:T(8,128)(2,1)}), bf16[4,128,1920]{2,1,0:T(8,128)(2,1)}, u32[]{:S(2)}, u32[]{:S(2)}) async-start(bf16[4,128,1920]{2,1,0:T(8,128)(2,1)} %broadcast_in_dim.34), calls=%async_computation.2 | async-start | bytes 3932160 | tf_op jit(solution)/shard_map/all_to_all | solution.py:150
  52.9 2.7 %collective-permute-start.2 = (bf16[128,1792]{1,0:T(8,128)(2,1)S(1)}, bf16[128,1792]{1,0:T(8,128)(2,1)S(1)}, u32[]{:S(2)}, u32[]{:S(2)}) collective-permute-start(bf16[128,1792]{1,0:T(8,128)(2,1)S(1)} %get-tuple-element.16), channel_id=1, source_target_pairs={{0,4},{2,6},{4,0},{6,2},{1,5},{3,7},{5,1},{7,3},{8,12},{10,14},{12... | collective-permute-start | bytes 1376264 | tf_op jit(solution)/shard_map/ppermute | solution.py:140
  55.6 4.2 %collective-permute-start.3 = (bf16[128,1792]{1,0:T(8,128)(2,1)S(1)}, bf16[128,1792]{1,0:T(8,128)(2,1)S(1)}, u32[]{:S(2)}, u32[]{:S(2)}) collective-permute-start(bf16[128,1792]{1,0:T(8,128)(2,1)S(1)} %get-tuple-element.19.refs_1_), channel_id=1, source_target_pairs={{0,1},{1,0},{2,3},{3,2},{4,5},{5,4},{6,7},{7,6},{8,9},{9,8},{10,11... | collective-permute-start | bytes 1376264 | tf_op jit(solution)/shard_map/ppermute | solution.py:153
  59.8 6.6 %collective-permute-done.2.refs_3_ = bf16[128,1792]{1,0:T(8,128)(2,1)S(1)} collective-permute-done((bf16[128,1792]{1,0:T(8,128)(2,1)S(1)}, bf16[128,1792]{1,0:T(8,128)(2,1)S(1)}, u32[]{:S(2)}, u32[]{:S(2)}) %collective-permute-start.2) | collective-permute-done | bytes 458784 | tf_op jit(solution)/shard_map/ppermute | solution.py:140
  66.4 4.7 %collective-permute-start.5 = (bf16[128,1792]{1,0:T(8,128)(2,1)S(1)}, bf16[128,1792]{1,0:T(8,128)(2,1)S(1)}, u32[]{:S(2)}, u32[]{:S(2)}) collective-permute-start(bf16[128,1792]{1,0:T(8,128)(2,1)S(1)} %collective-permute-done.2.refs_3_), channel_id=1, source_target_pairs={{0,1},{1,0},{2,3},{3,2},{4,5},{5,4},{6,7},{7,6},{8,9},{9,8},{10,11... | collective-permute-start | bytes 1376264 | tf_op jit(solution)/shard_map/ppermute | solution.py:153
  71.1 1.9 %collective-permute-start.4 = (bf16[128,1792]{1,0:T(8,128)(2,1)S(1)}, bf16[128,1792]{1,0:T(8,128)(2,1)S(1)}, u32[]{:S(2)}, u32[]{:S(2)}) collective-permute-start(bf16[128,1792]{1,0:T(8,128)(2,1)S(1)} %collective-permute-done.refs_2_), channel_id=1, source_target_pairs={{0,1},{1,0},{2,3},{3,2},{4,5},{5,4},{6,7},{7,6},{8,9},{9,8},{10,11... | collective-permute-start | bytes 1376264 | tf_op jit(solution)/shard_map/ppermute | solution.py:153
  73.0 2.4 %collective-permute-start.6 = (bf16[128,1792]{1,0:T(8,128)(2,1)S(1)}, bf16[128,1792]{1,0:T(8,128)(2,1)S(1)}, u32[]{:S(2)}, u32[]{:S(2)}) collective-permute-start(bf16[128,1792]{1,0:T(8,128)(2,1)S(1)} %collective-permute-done.1.refs_4_), channel_id=1, source_target_pairs={{0,1},{1,0},{2,3},{3,2},{4,5},{5,4},{6,7},{7,6},{8,9},{9,8},{10,11... | collective-permute-start | bytes 1376264 | tf_op jit(solution)/shard_map/ppermute | solution.py:153
  75.4 0.0 collective-permute-done.3.refs_5_
  75.4 0.0 collective-permute-done.5.refs_7_
  75.5 0.0 collective-permute-done.4.refs_6_
  75.5 1.4 %collective-permute-done.6.refs_8_ = bf16[128,1792]{1,0:T(8,128)(2,1)S(1)} collective-permute-done((bf16[128,1792]{1,0:T(8,128)(2,1)S(1)}, bf16[128,1792]{1,0:T(8,128)(2,1)S(1)}, u32[]{:S(2)}, u32[]{:S(2)}) %collective-permute-start.6) | collective-permute-done | bytes 458784 | tf_op jit(solution)/shard_map/ppermute | solution.py:153
  76.9 0.0 copy-start
  76.9 0.8 copy-done
  77.6 0.0 all-to-all-done.2
  77.6 0.0 copy-start.1
  77.6 1.0 copy-done.1
  78.7 6.9 %shard_map.59 = (f32[4,8,128,128]{3,2,1,0:T(8,128)}, s32[1,128]{1,0:T(1,128)S(1)}) custom-call(s32[1]{0:T(128)} %bitcast.8.x_ref, bf16[4,4,32,1920]{3,2,1,0:T(8,128)(2,1)} %bitcast.21.refs_0_, bf16[128,1792]{1,0:T(8,128)(2,1)S(1)} %get-tuple-element.19.refs_1_, bf16[128,1792]{1,0:T(8,128)(2,1)S(1)} %collective-permute-done.refs_2_, ...), custom_call_target="tpu_custom_call" | custom-call | tf_op jit(solution)/shard_map/pallas_call | solution.py:69
  85.5 3.6 %all-to-all-start.3 = ((f32[4,8,128,128]{3,2,1,0:T(8,128)}), f32[4,8,128,128]{3,2,1,0:T(8,128)S(1)}, u32[]{:S(2)}, u32[]{:S(2)}) async-start(f32[4,8,128,128]{3,2,1,0:T(8,128)} %get-tuple-element.10), calls=%async_computation.3 | async-start | bytes 4194304 | tf_op jit(solution)/shard_map/all_to_all | solution.py:156
  89.2 0.0 copy-start.3
  89.2 0.1 stack.50.first_ref
  89.3 25.9 %all-to-all-done.3.parts_ref = f32[4,8,128,128]{3,2,1,0:T(8,128)S(1)} async-done(((f32[4,8,128,128]{3,2,1,0:T(8,128)}), f32[4,8,128,128]{3,2,1,0:T(8,128)S(1)}, u32[]{:S(2)}, u32[]{:S(2)}) %all-to-all-start.3) | async-done | bytes 2097184 | tf_op jit(solution)/shard_map/all_to_all | solution.py:156
  115.2 1.0 shard_map.60
  116.2 18.6 %all_to_all.26 = f32[64,2,8]{2,1,0:T(2,128)S(1)} all-to-all(f32[64,2,8]{2,1,0:T(2,128)S(1)} %bitcast.48), channel_id=1, replica_groups=mesh['s1'=2,'s0'=2,'zh'=2,'y1'=4,'y0'=2,'x1'=2,'x0'=2,'core'=2] {'s0','y..., dimensions={0} | all-to-all | bytes 8192 | tf_op jit(solution)/shard_map/all_to_all | solution.py:169
  134.8 0.4 fusion.5
  135.2 0.1 copy.17
  135.3 0.1 copy.18
  135.4 0.2 fusion.2
  135.6 0.0 copy-done.3
  135.6 0.5 fusion.4
  (3 shorter events, 0.1 us)
Async XLA Ops:
  0.6 27.0 %copy-start.2 = (bf16[128,7168]{1,0:T(8,128)(2,1)S(1)}, bf16[128,7168]{1,0:T(8,128)(2,1)}, u32[]{:S(2)}) copy-start(bf16[128,7168]{1,0:T(8,128)(2,1)} %param.5) | copy-start | bytes 5505028
  12.2 34.1 %all-to-all-start.1 = ((bf16[16,8,1920]{2,1,0:T(8,128)(2,1)}), bf16[16,8,1920]{2,1,0:T(8,128)(2,1)S(1)}, u32[]{:S(2)}, u32[]{:S(2)}) async-start(bf16[16,8,1920]{2,1,0:T(8,128)(2,1)} %broadcast_in_dim.33), calls=%async_computation.1 | async-start | bytes 983040 | tf_op jit(solution)/shard_map/all_to_all | solution.py:145
  28.7 18.2 %collective-permute-start.1 = (bf16[128,1792]{1,0:T(8,128)(2,1)}, bf16[128,1792]{1,0:T(8,128)(2,1)S(1)}, u32[]{:S(2)}, u32[]{:S(2)}) collective-permute-start(bf16[128,1792]{1,0:T(8,128)(2,1)} %get-tuple-element.17), channel_id=1, source_target_pairs={{0,6},{2,4},{4,2},{6,0},{1,7},{3,5},{5,3},{7,1},{8,14},{10,12},{12... | collective-permute-start | bytes 1376264 | tf_op jit(solution)/shard_map/ppermute | solution.py:140
  31.5 15.5 %collective-permute-start = (bf16[128,1792]{1,0:T(8,128)(2,1)}, bf16[128,1792]{1,0:T(8,128)(2,1)S(1)}, u32[]{:S(2)}, u32[]{:S(2)}) collective-permute-start(bf16[128,1792]{1,0:T(8,128)(2,1)} %get-tuple-element.18), channel_id=1, source_target_pairs={{0,2},{2,0},{4,6},{6,4},{1,3},{3,1},{5,7},{7,5},{8,10},{10,8},{12,... | collective-permute-start | bytes 1376264 | tf_op jit(solution)/shard_map/ppermute | solution.py:140
  48.4 29.2 %all-to-all-start.2 = ((bf16[4,128,1920]{2,1,0:T(8,128)(2,1)}), bf16[4,128,1920]{2,1,0:T(8,128)(2,1)}, u32[]{:S(2)}, u32[]{:S(2)}) async-start(bf16[4,128,1920]{2,1,0:T(8,128)(2,1)} %broadcast_in_dim.34), calls=%async_computation.2 | async-start | bytes 3932160 | tf_op jit(solution)/shard_map/all_to_all | solution.py:150
  52.9 13.6 %collective-permute-start.2 = (bf16[128,1792]{1,0:T(8,128)(2,1)S(1)}, bf16[128,1792]{1,0:T(8,128)(2,1)S(1)}, u32[]{:S(2)}, u32[]{:S(2)}) collective-permute-start(bf16[128,1792]{1,0:T(8,128)(2,1)S(1)} %get-tuple-element.16), channel_id=1, source_target_pairs={{0,4},{2,6},{4,0},{6,2},{1,5},{3,7},{5,1},{7,3},{8,12},{10,14},{12... | collective-permute-start | bytes 1376264 | tf_op jit(solution)/shard_map/ppermute | solution.py:140
  55.6 19.8 %collective-permute-start.3 = (bf16[128,1792]{1,0:T(8,128)(2,1)S(1)}, bf16[128,1792]{1,0:T(8,128)(2,1)S(1)}, u32[]{:S(2)}, u32[]{:S(2)}) collective-permute-start(bf16[128,1792]{1,0:T(8,128)(2,1)S(1)} %get-tuple-element.19.refs_1_), channel_id=1, source_target_pairs={{0,1},{1,0},{2,3},{3,2},{4,5},{5,4},{6,7},{7,6},{8,9},{9,8},{10,11... | collective-permute-start | bytes 1376264 | tf_op jit(solution)/shard_map/ppermute | solution.py:153
  66.4 9.0 %collective-permute-start.5 = (bf16[128,1792]{1,0:T(8,128)(2,1)S(1)}, bf16[128,1792]{1,0:T(8,128)(2,1)S(1)}, u32[]{:S(2)}, u32[]{:S(2)}) collective-permute-start(bf16[128,1792]{1,0:T(8,128)(2,1)S(1)} %collective-permute-done.2.refs_3_), channel_id=1, source_target_pairs={{0,1},{1,0},{2,3},{3,2},{4,5},{5,4},{6,7},{7,6},{8,9},{9,8},{10,11... | collective-permute-start | bytes 1376264 | tf_op jit(solution)/shard_map/ppermute | solution.py:153
  71.1 4.4 %collective-permute-start.4 = (bf16[128,1792]{1,0:T(8,128)(2,1)S(1)}, bf16[128,1792]{1,0:T(8,128)(2,1)S(1)}, u32[]{:S(2)}, u32[]{:S(2)}) collective-permute-start(bf16[128,1792]{1,0:T(8,128)(2,1)S(1)} %collective-permute-done.refs_2_), channel_id=1, source_target_pairs={{0,1},{1,0},{2,3},{3,2},{4,5},{5,4},{6,7},{7,6},{8,9},{9,8},{10,11... | collective-permute-start | bytes 1376264 | tf_op jit(solution)/shard_map/ppermute | solution.py:153
  73.0 3.8 %collective-permute-start.6 = (bf16[128,1792]{1,0:T(8,128)(2,1)S(1)}, bf16[128,1792]{1,0:T(8,128)(2,1)S(1)}, u32[]{:S(2)}, u32[]{:S(2)}) collective-permute-start(bf16[128,1792]{1,0:T(8,128)(2,1)S(1)} %collective-permute-done.1.refs_4_), channel_id=1, source_target_pairs={{0,1},{1,0},{2,3},{3,2},{4,5},{5,4},{6,7},{7,6},{8,9},{9,8},{10,11... | collective-permute-start | bytes 1376264 | tf_op jit(solution)/shard_map/ppermute | solution.py:153
  76.9 0.8 copy-start
  77.6 1.0 copy-start.1
  85.5 29.7 %all-to-all-start.3 = ((f32[4,8,128,128]{3,2,1,0:T(8,128)}), f32[4,8,128,128]{3,2,1,0:T(8,128)S(1)}, u32[]{:S(2)}, u32[]{:S(2)}) async-start(f32[4,8,128,128]{3,2,1,0:T(8,128)} %get-tuple-element.10), calls=%async_computation.3 | async-start | bytes 4194304 | tf_op jit(solution)/shard_map/all_to_all | solution.py:156
  89.2 46.4 %copy-start.3 = (f32[1,2]{1,0:T(1,128)S(1)}, f32[1,2]{1,0:T(1,128)}, u32[]{:S(2)}) copy-start(f32[1,2]{1,0:T(1,128)} %param.7) | copy-start | bytes 28

commit v5 on v2

--- a/solution.py
+++ b/solution.py
@@ -6,12 +6,12 @@
 from jax.experimental.pallas import tpu as pltpu
 from jax.sharding import Mesh, PartitionSpec as P
 
-NAMES = ("s1", "s0", "zh", "y1", "y0", "x", "core")
-SIZES = (2, 2, 2, 4, 2, 4, 2)
+NAMES = ("s1", "s0", "zh", "y1", "y0", "x1", "x0", "core")
+SIZES = (2, 2, 2, 4, 2, 2, 2, 2)
 SEG = ("s1", "s0")
-DP = ("zh", "y1", "y0", "x", "core")
+DP = ("zh", "y1", "y0", "x1", "x0", "core")
 GA = ("s1", "zh", "y1")
-GB = ("x",)
+GB = ("s0", "y0")
 IDS = 128
 SWAP = [(0, 1), (1, 0)]
 
@@ -20,29 +20,27 @@
     return int(np.prod([SIZES[NAMES.index(a)] for a in axes]))
 
 
-def matmul_kernel(s0_ref, h_ref, *refs):
-    pieces, (keep_ref, send_ref, id_ref) = refs[:-3], refs[-3:]
-    voc, depth = pieces[0].shape
-    mine = s0_ref[0]
+def matmul_kernel(k_ref, h_ref, *refs):
+    pieces, (keep_ref, send_ref, id_ref, turned) = refs[:-4], refs[-4:]
+    depth = pieces[0].shape[1]
     wide = h_ref.shape[-1]
+    mine = k_ref[0]
     kept = h_ref[:, mine].reshape(-1, wide)
     sent = h_ref[:, 1 - mine].reshape(-1, wide)
-    rows = jnp.concatenate([kept[:, :depth], sent[:, :depth]], axis=0)
     half = kept.shape[0]
+    turned[:, :half] = kept[:, :depth].T
+    turned[:, half:] = sent[:, :depth].T
     code = kept[:, depth:].astype(jnp.float32).T
     id_ref[...] = (code[0:1] * 256.0 + code[1:2]).astype(jnp.int32)
     for j, piece in enumerate(pieces):
-        out = lax.dot_general(
-            piece[...], rows, (((1,), (1,)), ((), ())),
-            preferred_element_type=jnp.float32,
-        )
+        out = jnp.dot(piece[...], turned[...], preferred_element_type=jnp.float32)
         keep_ref[j] = out[:, :half]
         send_ref[j ^ 1] = out[:, half:]
 
 
-def partial_logits(s0, gathered, pieces):
+def partial_logits(k, gathered, pieces):
     nb, _, rows, _ = gathered.shape
-    voc = pieces[0].shape[0]
+    voc, depth = pieces[0].shape
     block = jax.ShapeDtypeStruct((len(pieces), voc, nb * rows), jnp.float32)
     vmem = pl.BlockSpec(memory_space=pltpu.VMEM)
     return pl.pallas_call(
@@ -50,8 +48,9 @@
         in_specs=[pl.BlockSpec(memory_space=pltpu.SMEM)] + [vmem] * (1 + len(pieces)),
         out_specs=[vmem] * 3,
         out_shape=[block, block, jax.ShapeDtypeStruct((1, nb * rows), jnp.int32)],
-        compiler_params=pltpu.CompilerParams(vmem_limit_bytes=48 * 1024 * 1024),
-    )(s0, gathered, *pieces)
+        scratch_shapes=[pltpu.VMEM((depth, 2 * nb * rows), gathered.dtype)],
+        compiler_params=pltpu.CompilerParams(vmem_limit_bytes=50 * 1024 * 1024),
+    )(k, gathered, *pieces)
 
 
 def stats_kernel(first_ref, mine_ref, theirs_ref, ids_ref, out_ref):
@@ -76,7 +75,7 @@
         in_specs=[pl.BlockSpec(memory_space=pltpu.SMEM)] + [vmem] * 3,
         out_specs=vmem,
         out_shape=jax.ShapeDtypeStruct((mine.shape[2], 128), jnp.float32),
-        compiler_params=pltpu.CompilerParams(vmem_limit_bytes=32 * 1024 * 1024),
+        compiler_params=pltpu.CompilerParams(vmem_limit_bytes=8 * 1024 * 1024),
     )(first, mine, theirs, ids)
 
 
@@ -86,15 +85,15 @@
     voc = head_weight.shape[0]
     depth = width // 2
     at = {a: lax.axis_index(a) for a in NAMES}
-    s0 = at["s0"]
+    k = at["x0"]
 
-    kept = lax.dynamic_slice_in_dim(head_weight, s0 * depth, depth, 1)
-    given = lax.dynamic_slice_in_dim(head_weight, (1 - s0) * depth, depth, 1)
+    kept = lax.dynamic_slice_in_dim(head_weight, k * depth, depth, 1)
+    given = lax.dynamic_slice_in_dim(head_weight, (1 - k) * depth, depth, 1)
     pieces = [
         kept,
-        lax.ppermute(given, "s0", SWAP),
-        lax.ppermute(kept, "y0", SWAP),
-        lax.ppermute(given, ("s0", "y0"), [(i, i ^ 3) for i in range(4)]),
+        lax.ppermute(given, "x0", SWAP),
+        lax.ppermute(kept, "x1", SWAP),
+        lax.ppermute(given, ("x1", "x0"), [(i, i ^ 3) for i in range(4)]),
     ]
 
     ids = target_ids.reshape(rows, 1)
@@ -106,7 +105,7 @@
     ]
     message = jnp.broadcast_to(jnp.stack(halves)[:, None], (2, na, rows, depth + IDS))
     message = message.reshape(2 * na, rows, depth + IDS)
-    column = lax.all_to_all(message, ("s0",) + GA, 0, 0, tiled=True)
+    column = lax.all_to_all(message, ("x0",) + GA, 0, 0, tiled=True)
     column = column.reshape(2 * na * rows, depth + IDS)
     copies = jnp.broadcast_to(column[None], (nb,) + column.shape)
     gathered = lax.all_to_all(copies, GB, 0, 0, tiled=True)
@@ -114,14 +113,14 @@
 
     pieces += [lax.ppermute(piece, "core", SWAP) for piece in pieces]
 
-    mine, send, ids = partial_logits(s0.reshape(1), gathered, pieces)
-    theirs = lax.ppermute(send, "s0", SWAP)
+    mine, send, ids = partial_logits(k.reshape(1), gathered, pieces)
+    theirs = lax.ppermute(send, "x0", SWAP)
 
     firsts = []
     for j in range(len(pieces)):
         place = dict(at)
-        place["s0"] = at["s0"] ^ (j & 1)
-        place["y0"] = at["y0"] ^ ((j >> 1) & 1)
+        place["x0"] = at["x0"] ^ (j & 1)
+        place["x1"] = at["x1"] ^ ((j >> 1) & 1)
         place["core"] = at["core"] ^ (j >> 2)
         flat = 0
         for a, n in zip(NAMES, SIZES):

time: 134 us -> 140 us (1.045)
  blocking collectives: 24.4 us -> 53.4 us
  starting transfers between devices: 46 us -> 37.5 us
  waiting for transfers between devices: 39.5 us -> 32.7 us
  local copies, waits for them, and re-layouts: 11.1 us -> 5.16 us
  Pallas kernels: 9.06 us -> 6.86 us
    all_to_all x0 -> x1, blocking collectives: none -> 36 us  [per_device(): column = lax.all_to_all(message, ('x0',) + GA, 0, 0, tiled=True)]
    all_to_all x1 -> x0, starting transfers between devices: 16.6 us -> none  [per_device(): column = lax.all_to_all(message, ('s0',) + GA, 0, 0, tiled=True)]
    all_to_all x1 -> x0, waiting for transfers between devices: 9.2 us -> none  [per_device(): column = lax.all_to_all(message, ('s0',) + GA, 0, 0, tiled=True)]
    ppermute x4, starting transfers between devices: 14.1 us -> 21.5 us  [per_device(): pieces += [lax.ppermute(piece, 'core', SWAP) for piece in pieces]]
    all_to_all x1, blocking collectives: 24.4 us -> 17.4 us  [per_device(): stats = lax.all_to_all(stats, GB + GA, 0, 0, tiled=True)]
    ppermute x4, waiting for transfers between devices: 30.3 us -> 32.7 us  [the longest x1 13.3 us: per_device(): theirs = lax.ppermute(send, 'x0', SWAP)]
    dynamic_slice x1, local copies, waits for them, and re-layouts: 2.52 us -> 0.13 us  [per_device(): given = lax.dynamic_slice_in_dim(head_weight, (1 - k) * depth, depth, 1)]
    pallas_call x1, Pallas kernels: 8.17 us -> 5.98 us  [partial_logits(): pl.pallas_call(matmul_kernel, in_specs=[pl.BlockSpec(memory_space=pltpu.S...]
  transfers between devices with their start and end apart: 10 -> 9, of which waited for: 4 -> 3; matrix products, arithmetic and copies ran while one was open for 4% -> 0% of each run, Pallas kernels for 0% -> 0%
where the time goes in v5:
time: 140 us; the launch traced here: 138 us
  blocking collectives  53.4 us (38%)
  starting transfers between devices  37.5 us (27%)
  waiting for transfers between devices  32.7 us (23%)
  Pallas kernels  6.86 us (5%)
  local copies, waits for them, and re-layouts  5.16 us (4%)
  other arithmetic  1.91 us (1%)
    all_to_all x1, blocking collectives, per_device(): column = lax.all_to_all(message, ('x0',) + GA, 0, 0, tiled=True)  36 us
    ppermute x4, starting transfers between devices, per_device(): pieces += [lax.ppermute(piece, 'core', SWAP) for piece in pieces]  21.5 us
    all_to_all x1, blocking collectives, per_device(): stats = lax.all_to_all(stats, GB + GA, 0, 0, tiled=True)  17.4 us
    ppermute x1, waiting for transfers between devices, per_device(): theirs = lax.ppermute(send, 'x0', SWAP)  13.3 us
    ppermute x1, waiting for transfers between devices, per_device(): lax.ppermute(kept, 'x1', SWAP)  11.3 us
    ppermute x1, waiting for transfers between devices, per_device(): lax.ppermute(given, ('x1', 'x0'), [(i, i ^ 3) for i in range(4)])  8.09 us
    pallas_call x1, Pallas kernels, partial_logits(): pl.pallas_call(matmul_kernel, in_specs=[pl.BlockSpec(memory_space=pltpu.S...  5.98 us
    all_to_all x1, starting transfers between devices, per_device(): gathered = lax.all_to_all(copies, GB, 0, 0, tiled=True)  4.53 us
  transfers between devices with their start and end apart: 9, of which 3 were waited for; matrix products, arithmetic and copies ran while one was open for 0% of the time, Pallas kernels for 0%

profile of v5, /device:TPU:1, one launch (start us, length us, event | category | flops | bytes accessed | tf_op | source)
XLA Modules:
  0.0 138.4 jit_solution(13026069229584297520)
XLA Ops:
  0.6 0.7 shift-right-arithmetic_bitcast_fusion
  1.3 0.8 slice_bitcast_fusion.1
  2.1 0.1 select_convert_fusion
  2.2 0.2 broadcast_in_dim.32
  2.5 36.0 %all_to_all.15 = bf16[32,2,3712]{2,1,0:T(2,128)(2,1)S(1)} all-to-all(bf16[32,2,3712]{2,1,0:T(2,128)(2,1)S(1)} %bitcast.39), channel_id=1, replica_groups=mesh['s1'=2,'s0'=2,'zh'=2,'y1'=4,'y0'=2,'x1'=2,'x0'=2,'core'=2] {'x0','s..., dimensions={0} | all-to-all | bytes 950272 | tf_op jit(solution)/shard_map/all_to_all | solution.py:108
  38.5 0.2 broadcast_in_dim.33
  38.7 1.4 broadcast_in_dim.34
  40.0 0.0 copy-start
  40.0 4.5 %all-to-all-start.1 = ((bf16[4,64,3712]{2,1,0:T(8,128)(2,1)}), bf16[4,64,3712]{2,1,0:T(8,128)(2,1)}, u32[]{:S(2)}, u32[]{:S(2)}) async-start(bf16[4,64,3712]{2,1,0:T(8,128)(2,1)} %broadcast_in_dim.34), calls=%async_computation.1 | async-start | bytes 3801088 | tf_op jit(solution)/shard_map/all_to_all | solution.py:111
  44.6 0.0 copy-done
  44.6 0.1 constant_dynamic-slice_fusion
  44.7 4.3 %collective-permute-start.2 = (bf16[128,3584]{1,0:T(8,128)(2,1)S(1)}, bf16[128,3584]{1,0:T(8,128)(2,1)S(1)}, u32[]{:S(2)}, u32[]{:S(2)}) collective-permute-start(bf16[128,3584]{1,0:T(8,128)(2,1)S(1)} %get-tuple-element.12), channel_id=1, source_target_pairs={{0,6},{2,4},{4,2},{6,0},{1,7},{3,5},{5,3},{7,1},{8,14},{10,12},{12... | collective-permute-start | bytes 2752520 | tf_op jit(solution)/shard_map/ppermute | solution.py:96
  49.0 1.9 %collective-permute-start = (bf16[128,3584]{1,0:T(8,128)(2,1)S(1)}, bf16[128,3584]{1,0:T(8,128)(2,1)S(1)}, u32[]{:S(2)}, u32[]{:S(2)}) collective-permute-start(bf16[128,3584]{1,0:T(8,128)(2,1)S(1)} %get-tuple-element.12), channel_id=1, source_target_pairs={{0,2},{2,0},{1,3},{3,1},{4,6},{6,4},{5,7},{7,5},{8,10},{10,8},{9,1... | collective-permute-start | bytes 2752520 | tf_op jit(solution)/shard_map/ppermute | solution.py:94
  50.9 3.4 %collective-permute-start.1 = (bf16[128,3584]{1,0:T(8,128)(2,1)S(1)}, bf16[128,3584]{1,0:T(8,128)(2,1)S(1)}, u32[]{:S(2)}, u32[]{:S(2)}) collective-permute-start(bf16[128,3584]{1,0:T(8,128)(2,1)S(1)} %get-tuple-element.13.refs_0_), channel_id=1, source_target_pairs={{0,4},{4,0},{1,5},{5,1},{2,6},{6,2},{3,7},{7,3},{8,12},{12,8},{9,1... | collective-permute-start | bytes 2752520 | tf_op jit(solution)/shard_map/ppermute | solution.py:95
  54.3 5.0 %collective-permute-start.3 = (bf16[128,3584]{1,0:T(8,128)(2,1)S(1)}, bf16[128,3584]{1,0:T(8,128)(2,1)S(1)}, u32[]{:S(2)}, u32[]{:S(2)}) collective-permute-start(bf16[128,3584]{1,0:T(8,128)(2,1)S(1)} %get-tuple-element.13.refs_0_), channel_id=1, source_target_pairs={{0,1},{1,0},{2,3},{3,2},{4,5},{5,4},{6,7},{7,6},{8,9},{9,8},{10,11... | collective-permute-start | bytes 2752520 | tf_op jit(solution)/shard_map/ppermute | solution.py:114
  59.3 8.1 %collective-permute-done.2.refs_3_ = bf16[128,3584]{1,0:T(8,128)(2,1)S(1)} collective-permute-done((bf16[128,3584]{1,0:T(8,128)(2,1)S(1)}, bf16[128,3584]{1,0:T(8,128)(2,1)S(1)}, u32[]{:S(2)}, u32[]{:S(2)}) %collective-permute-start.2) | collective-permute-done | bytes 917536 | tf_op jit(solution)/shard_map/ppermute | solution.py:96
  67.4 0.0 copy-start.1
  67.4 5.1 %collective-permute-start.6 = (bf16[128,3584]{1,0:T(8,128)(2,1)S(1)}, bf16[128,3584]{1,0:T(8,128)(2,1)S(1)}, u32[]{:S(2)}, u32[]{:S(2)}) collective-permute-start(bf16[128,3584]{1,0:T(8,128)(2,1)S(1)} %collective-permute-done.2.refs_3_), channel_id=1, source_target_pairs={{0,1},{1,0},{2,3},{3,2},{4,5},{5,4},{6,7},{7,6},{8,9},{9,8},{10,11... | collective-permute-start | bytes 2752520 | tf_op jit(solution)/shard_map/ppermute | solution.py:114
  72.5 0.0 collective-permute-done.refs_1_
  72.5 6.0 %collective-permute-start.4 = (bf16[128,3584]{1,0:T(8,128)(2,1)S(1)}, bf16[128,3584]{1,0:T(8,128)(2,1)S(1)}, u32[]{:S(2)}, u32[]{:S(2)}) collective-permute-start(bf16[128,3584]{1,0:T(8,128)(2,1)S(1)} %collective-permute-done.refs_1_), channel_id=1, source_target_pairs={{0,1},{1,0},{2,3},{3,2},{4,5},{5,4},{6,7},{7,6},{8,9},{9,8},{10,11... | collective-permute-start | bytes 2752520 | tf_op jit(solution)/shard_map/ppermute | solution.py:114
  78.6 11.3 %collective-permute-done.1.refs_2_ = bf16[128,3584]{1,0:T(8,128)(2,1)S(1)} collective-permute-done((bf16[128,3584]{1,0:T(8,128)(2,1)S(1)}, bf16[128,3584]{1,0:T(8,128)(2,1)S(1)}, u32[]{:S(2)}, u32[]{:S(2)}) %collective-permute-start.1) | collective-permute-done | bytes 917536 | tf_op jit(solution)/shard_map/ppermute | solution.py:95
  89.9 5.3 %collective-permute-start.5 = (bf16[128,3584]{1,0:T(8,128)(2,1)S(1)}, bf16[128,3584]{1,0:T(8,128)(2,1)}, u32[]{:S(2)}, u32[]{:S(2)}) collective-permute-start(bf16[128,3584]{1,0:T(8,128)(2,1)S(1)} %collective-permute-done.1.refs_2_), channel_id=1, source_target_pairs={{0,1},{1,0},{2,3},{3,2},{4,5},{5,4},{6,7},{7,6},{8,9},{9,8},{10,11... | collective-permute-start | bytes 2752520 | tf_op jit(solution)/shard_map/ppermute | solution.py:114
  95.3 0.0 collective-permute-done.3.refs_4_
  95.3 0.0 copy-start.2
  95.3 0.0 collective-permute-done.6.refs_7_
  95.3 0.0 copy-start.3
  95.3 0.0 collective-permute-done.4.refs_5_
  95.3 0.0 copy-done.1
  95.3 0.9 copy-done.2
  96.2 0.4 copy-done.3
  96.6 0.0 copy-start.4
  96.6 0.9 copy-done.4
  97.5 0.0 collective-permute-done.5.refs_6_
  97.5 0.0 all-to-all-done.1
  97.5 0.0 copy-start.5
  97.5 6.0 %shard_map.59 = (f32[8,128,128]{2,1,0:T(8,128)S(1)}, f32[8,128,128]{2,1,0:T(8,128)}, s32[1,128]{1,0:T(1,128)S(1)}) custom-call(s32[1]{0:T(128)} %bitcast.8.k_ref, bf16[4,2,32,3712]{3,2,1,0:T(8,128)(2,1)} %bitcast.16.h_ref, bf16[128,3584]{1,0:T(8,128)(2,1)S(1)} %get-tuple-element.13.refs_0_, bf16[128,3584]{1,0:T(8,128)(2,1)S(1)} %collective-permute-done.refs_1_, ...), custom_call_target="tpu_custom_call" | custom-call | tf_op jit(solution)/shard_map/pallas_call | solution.py:46
  103.5 1.9 %collective-permute-start.7 = (f32[8,128,128]{2,1,0:T(8,128)}, f32[8,128,128]{2,1,0:T(8,128)S(1)}, u32[]{:S(2)}, u32[]{:S(2)}) collective-permute-start(f32[8,128,128]{2,1,0:T(8,128)} %get-tuple-element.6), channel_id=1, source_target_pairs={{0,2},{2,0},{1,3},{3,1},{4,6},{6,4},{5,7},{7,5},{8,10},{10,8},{9,1... | collective-permute-start | bytes 1572872 | tf_op jit(solution)/shard_map/ppermute | solution.py:117
  105.5 0.1 stack.44.first_ref
  105.6 13.3 %collective-permute-done.7.theirs_ref = f32[8,128,128]{2,1,0:T(8,128)S(1)} collective-permute-done((f32[8,128,128]{2,1,0:T(8,128)}, f32[8,128,128]{2,1,0:T(8,128)S(1)}, u32[]{:S(2)}, u32[]{:S(2)}) %collective-permute-start.7) | collective-permute-done | bytes 524320 | tf_op jit(solution)/shard_map/ppermute | solution.py:117
  118.8 0.9 shard_map.60
  119.7 17.4 %all_to_all.16 = f32[64,2,8]{2,1,0:T(2,128)S(1)} all-to-all(f32[64,2,8]{2,1,0:T(2,128)S(1)} %bitcast.38), channel_id=1, replica_groups=mesh['s1'=2,'s0'=2,'zh'=2,'y1'=4,'y0'=2,'x1'=2,'x0'=2,'core'=2] {'s0','y..., dimensions={0} | all-to-all | bytes 8192 | tf_op jit(solution)/shard_map/all_to_all | solution.py:131
  137.1 0.4 fusion.7
  137.5 0.1 copy.10
  137.6 0.1 copy.11
  137.7 0.2 fusion.4
  137.9 0.0 copy-done.5
  137.9 0.5 fusion.6
  (3 shorter events, 0.1 us)
Async XLA Ops:
  40.0 4.6 %copy-start = (bf16[128,7168]{1,0:T(8,128)(2,1)S(1)}, bf16[128,7168]{1,0:T(8,128)(2,1)}, u32[]{:S(2)}) copy-start(bf16[128,7168]{1,0:T(8,128)(2,1)} %param.5) | copy-start | bytes 5505028
  40.0 57.5 %all-to-all-start.1 = ((bf16[4,64,3712]{2,1,0:T(8,128)(2,1)}), bf16[4,64,3712]{2,1,0:T(8,128)(2,1)}, u32[]{:S(2)}, u32[]{:S(2)}) async-start(bf16[4,64,3712]{2,1,0:T(8,128)(2,1)} %broadcast_in_dim.34), calls=%async_computation.1 | async-start | bytes 3801088 | tf_op jit(solution)/shard_map/all_to_all | solution.py:111
  44.7 22.7 %collective-permute-start.2 = (bf16[128,3584]{1,0:T(8,128)(2,1)S(1)}, bf16[128,3584]{1,0:T(8,128)(2,1)S(1)}, u32[]{:S(2)}, u32[]{:S(2)}) collective-permute-start(bf16[128,3584]{1,0:T(8,128)(2,1)S(1)} %get-tuple-element.12), channel_id=1, source_target_pairs={{0,6},{2,4},{4,2},{6,0},{1,7},{3,5},{5,3},{7,1},{8,14},{10,12},{12... | collective-permute-start | bytes 2752520 | tf_op jit(solution)/shard_map/ppermute | solution.py:96
  49.0 23.5 %collective-permute-start = (bf16[128,3584]{1,0:T(8,128)(2,1)S(1)}, bf16[128,3584]{1,0:T(8,128)(2,1)S(1)}, u32[]{:S(2)}, u32[]{:S(2)}) collective-permute-start(bf16[128,3584]{1,0:T(8,128)(2,1)S(1)} %get-tuple-element.12), channel_id=1, source_target_pairs={{0,2},{2,0},{1,3},{3,1},{4,6},{6,4},{5,7},{7,5},{8,10},{10,8},{9,1... | collective-permute-start | bytes 2752520 | tf_op jit(solution)/shard_map/ppermute | solution.py:94
  50.9 39.0 %collective-permute-start.1 = (bf16[128,3584]{1,0:T(8,128)(2,1)S(1)}, bf16[128,3584]{1,0:T(8,128)(2,1)S(1)}, u32[]{:S(2)}, u32[]{:S(2)}) collective-permute-start(bf16[128,3584]{1,0:T(8,128)(2,1)S(1)} %get-tuple-element.13.refs_0_), channel_id=1, source_target_pairs={{0,4},{4,0},{1,5},{5,1},{2,6},{6,2},{3,7},{7,3},{8,12},{12,8},{9,1... | collective-permute-start | bytes 2752520 | tf_op jit(solution)/shard_map/ppermute | solution.py:95
  54.3 40.9 %collective-permute-start.3 = (bf16[128,3584]{1,0:T(8,128)(2,1)S(1)}, bf16[128,3584]{1,0:T(8,128)(2,1)S(1)}, u32[]{:S(2)}, u32[]{:S(2)}) collective-permute-start(bf16[128,3584]{1,0:T(8,128)(2,1)S(1)} %get-tuple-element.13.refs_0_), channel_id=1, source_target_pairs={{0,1},{1,0},{2,3},{3,2},{4,5},{5,4},{6,7},{7,6},{8,9},{9,8},{10,11... | collective-permute-start | bytes 2752520 | tf_op jit(solution)/shard_map/ppermute | solution.py:114
  67.4 27.9 %copy-start.1 = (bf16[128,3584]{1,0:T(8,128)(2,1)}, bf16[128,3584]{1,0:T(8,128)(2,1)S(1)}, u32[]{:S(2)}) copy-start(bf16[128,3584]{1,0:T(8,128)(2,1)S(1)} %collective-permute-done.2.refs_3_) | copy-start | bytes 2752516
  67.4 27.9 %collective-permute-start.6 = (bf16[128,3584]{1,0:T(8,128)(2,1)S(1)}, bf16[128,3584]{1,0:T(8,128)(2,1)S(1)}, u32[]{:S(2)}, u32[]{:S(2)}) collective-permute-start(bf16[128,3584]{1,0:T(8,128)(2,1)S(1)} %collective-permute-done.2.refs_3_), channel_id=1, source_target_pairs={{0,1},{1,0},{2,3},{3,2},{4,5},{5,4},{6,7},{7,6},{8,9},{9,8},{10,11... | collective-permute-start | bytes 2752520 | tf_op jit(solution)/shard_map/ppermute | solution.py:114
  72.5 22.8 %collective-permute-start.4 = (bf16[128,3584]{1,0:T(8,128)(2,1)S(1)}, bf16[128,3584]{1,0:T(8,128)(2,1)S(1)}, u32[]{:S(2)}, u32[]{:S(2)}) collective-permute-start(bf16[128,3584]{1,0:T(8,128)(2,1)S(1)} %collective-permute-done.refs_1_), channel_id=1, source_target_pairs={{0,1},{1,0},{2,3},{3,2},{4,5},{5,4},{6,7},{7,6},{8,9},{9,8},{10,11... | collective-permute-start | bytes 2752520 | tf_op jit(solution)/shard_map/ppermute | solution.py:114
  89.9 7.6 %collective-permute-start.5 = (bf16[128,3584]{1,0:T(8,128)(2,1)S(1)}, bf16[128,3584]{1,0:T(8,128)(2,1)}, u32[]{:S(2)}, u32[]{:S(2)}) collective-permute-start(bf16[128,3584]{1,0:T(8,128)(2,1)S(1)} %collective-permute-done.1.refs_2_), channel_id=1, source_target_pairs={{0,1},{1,0},{2,3},{3,2},{4,5},{5,4},{6,7},{7,6},{8,9},{9,8},{10,11... | collective-permute-start | bytes 2752520 | tf_op jit(solution)/shard_map/ppermute | solution.py:114
  95.3 1.0 copy-start.2
  95.3 1.3 copy-start.3
  96.6 0.9 copy-start.4
  97.5 40.3 %copy-start.5 = (f32[1,2]{1,0:T(1,128)S(1)}, f32[1,2]{1,0:T(1,128)}, u32[]{:S(2)}) copy-start(f32[1,2]{1,0:T(1,128)} %param.7) | copy-start | bytes 28
  103.5 15.3 %collective-permute-start.7 = (f32[8,128,128]{2,1,0:T(8,128)}, f32[8,128,128]{2,1,0:T(8,128)S(1)}, u32[]{:S(2)}, u32[]{:S(2)}) collective-permute-start(f32[8,128,128]{2,1,0:T(8,128)} %get-tuple-element.6), channel_id=1, source_target_pairs={{0,2},{2,0},{1,3},{3,1},{4,6},{6,4},{5,7},{7,5},{8,10},{10,8},{9,1... | collective-permute-start | bytes 1572872 | tf_op jit(solution)/shard_map/ppermute | solution.py:117

commit v6 on v5

--- a/solution.py
+++ b/solution.py
@@ -107,11 +107,14 @@
     message = message.reshape(2 * na, rows, depth + IDS)
     column = lax.all_to_all(message, ("x0",) + GA, 0, 0, tiled=True)
     column = column.reshape(2 * na * rows, depth + IDS)
+    column, pieces[1], pieces[3] = lax.optimization_barrier((column, pieces[1], pieces[3]))
     copies = jnp.broadcast_to(column[None], (nb,) + column.shape)
     gathered = lax.all_to_all(copies, GB, 0, 0, tiled=True)
     gathered = gathered.reshape(nb, 2, na * rows, depth + IDS)
 
-    pieces += [lax.ppermute(piece, "core", SWAP) for piece in pieces]
+    near = [lax.ppermute(pieces[j], "core", SWAP) for j in (0, 1, 3)]
+    pieces[2], *near = lax.optimization_barrier((pieces[2], *near))
+    pieces += [near[0], near[1], lax.ppermute(pieces[2], "core", SWAP), near[2]]
 
     mine, send, ids = partial_logits(k.reshape(1), gathered, pieces)
     theirs = lax.ppermute(send, "x0", SWAP)

time: 140 us -> 135 us (0.964)
  blocking collectives: 53.4 us -> 22.1 us
  waiting for transfers between devices: 32.7 us -> 46.5 us
  starting transfers between devices: 37.5 us -> 48 us
  local copies, waits for them, and re-layouts: 5.16 us -> 8.01 us
    all_to_all x1 -> x0, blocking collectives: 36 us -> none  [per_device(): column = lax.all_to_all(message, ('x0',) + GA, 0, 0, tiled=True)]
    all_to_all x0 -> x1, starting transfers between devices: none -> 17.4 us  [per_device(): column = lax.all_to_all(message, ('x0',) + GA, 0, 0, tiled=True)]
    ppermute x1, waiting for transfers between devices: 0.01 us -> 11.1 us  [per_device(): lax.ppermute(given, 'x0', SWAP)]
    all_to_all x0 -> x1, waiting for transfers between devices: none -> 9.69 us  [per_device(): column = lax.all_to_all(message, ('x0',) + GA, 0, 0, tiled=True)]
    ppermute x4, starting transfers between devices: 21.5 us -> 12.5 us  [the longest x3 7.96 us: per_device(): near = [lax.ppermute(pieces[j], 'core', SWAP) for j in (0, 1, 3)]]
    ppermute x1, waiting for transfers between devices: 8.09 us -> 0.01 us  [per_device(): lax.ppermute(given, ('x1', 'x0'), [(i, i ^ 3) for i in range(4)])]
    all_to_all x1, blocking collectives: 17.4 us -> 22.1 us  [per_device(): stats = lax.all_to_all(stats, GB + GA, 0, 0, tiled=True)]
    dynamic_slice x1, local copies, waits for them, and re-layouts: 0.13 us -> 2.51 us  [per_device(): kept = lax.dynamic_slice_in_dim(head_weight, k * depth, depth, 1)]
  transfers between devices with their start and end apart: 9 -> 10, of which waited for: 3 -> 5; matrix products, arithmetic and copies ran while one was open for 0% -> 2% of each run, Pallas kernels for 0% -> 0%
where the time goes in v6:
time: 135 us; the launch traced here: 134 us
  starting transfers between devices  48 us (36%)
  waiting for transfers between devices  46.5 us (34%)
  blocking collectives  22.1 us (16%)
  local copies, waits for them, and re-layouts  8.01 us (6%)
  Pallas kernels  6.89 us (5%)
  other arithmetic  1.91 us (1%)
    all_to_all x1, blocking collectives, per_device(): stats = lax.all_to_all(stats, GB + GA, 0, 0, tiled=True)  22.1 us
    all_to_all x1, starting transfers between devices, per_device(): column = lax.all_to_all(message, ('x0',) + GA, 0, 0, tiled=True)  17.4 us
    ppermute x1, waiting for transfers between devices, per_device(): theirs = lax.ppermute(send, 'x0', SWAP)  12.4 us
    ppermute x1, waiting for transfers between devices, per_device(): lax.ppermute(given, 'x0', SWAP)  11.1 us
    ppermute x1, waiting for transfers between devices, per_device(): lax.ppermute(kept, 'x1', SWAP)  11.1 us
    all_to_all x1, waiting for transfers between devices, per_device(): column = lax.all_to_all(message, ('x0',) + GA, 0, 0, tiled=True)  9.69 us
    ppermute x3, starting transfers between devices, per_device(): near = [lax.ppermute(pieces[j], 'core', SWAP) for j in (0, 1, 3)]  7.96 us
    pallas_call x1, Pallas kernels, partial_logits(): pl.pallas_call(matmul_kernel, in_specs=[pl.BlockSpec(memory_space=pltpu.S...  6 us
  transfers between devices with their start and end apart: 10, of which 5 were waited for; matrix products, arithmetic and copies ran while one was open for 2% of the time, Pallas kernels for 0%

profile of v6, /device:TPU:1, one launch (start us, length us, event | category | flops | bytes accessed | tf_op | source)
XLA Modules:
  0.0 134.3 jit_solution(2051503136538117540)
XLA Ops:
  0.6 0.7 shift-right-arithmetic_bitcast_fusion
  1.3 0.8 slice_bitcast_fusion.1
  2.1 0.1 select_convert_fusion
  2.2 1.0 broadcast_in_dim.31
  3.3 17.4 %all-to-all-start = ((bf16[32,2,3712]{2,1,0:T(2,128)(2,1)}), bf16[32,2,3712]{2,1,0:T(2,128)(2,1)S(1)}, u32[]{:S(2)}, u32[]{:S(2)}) async-start(bf16[32,2,3712]{2,1,0:T(2,128)(2,1)} %bitcast.15), calls=%async_computation | async-start | bytes 950272 | tf_op jit(solution)/shard_map/all_to_all | solution.py:108
  20.7 2.5 %constant_dynamic-slice_fusion = (bf16[128,3584]{1,0:T(8,128)(2,1)S(1)}, bf16[128,3584]{1,0:T(8,128)(2,1)}) fusion(bf16[128,7168]{1,0:T(8,128)(2,1)} %param.5, s32[]{:T(128)S(6)} %select_n.12, s32[]{:T(128)S(6)} %select_n.11), kind=kLoop, calls=%fused_computation.19 | loop fusion | bytes 3670024 | tf_op jit(solution)/shard_map/dynamic_slice | solution.py:90
  23.2 3.1 %collective-permute-start = (bf16[128,3584]{1,0:T(8,128)(2,1)}, bf16[128,3584]{1,0:T(8,128)(2,1)S(1)}, u32[]{:S(2)}, u32[]{:S(2)}) collective-permute-start(bf16[128,3584]{1,0:T(8,128)(2,1)} %get-tuple-element.27), channel_id=1, source_target_pairs={{0,2},{2,0},{1,3},{3,1},{4,6},{6,4},{5,7},{7,5},{8,10},{10,8},{9,1... | collective-permute-start | bytes 2752520 | tf_op jit(solution)/shard_map/ppermute | solution.py:94
  26.4 3.4 %collective-permute-start.1 = (bf16[128,3584]{1,0:T(8,128)(2,1)}, bf16[128,3584]{1,0:T(8,128)(2,1)}, u32[]{:S(2)}, u32[]{:S(2)}) collective-permute-start(bf16[128,3584]{1,0:T(8,128)(2,1)} %get-tuple-element.27), channel_id=1, source_target_pairs={{0,6},{2,4},{4,2},{6,0},{1,7},{3,5},{5,3},{7,1},{8,14},{10,12},{12... | collective-permute-start | bytes 2752520 | tf_op jit(solution)/shard_map/ppermute | solution.py:96
  29.8 9.7 %all-to-all-done = bf16[32,2,3712]{2,1,0:T(2,128)(2,1)S(1)} async-done(((bf16[32,2,3712]{2,1,0:T(2,128)(2,1)}), bf16[32,2,3712]{2,1,0:T(2,128)(2,1)S(1)}, u32[]{:S(2)}, u32[]{:S(2)}) %all-to-all-start) | async-done | bytes 475168 | tf_op jit(solution)/shard_map/all_to_all | solution.py:108
  39.5 0.2 reshape.68
  39.6 11.1 %collective-permute-done.refs_1_ = bf16[128,3584]{1,0:T(8,128)(2,1)S(1)} collective-permute-done((bf16[128,3584]{1,0:T(8,128)(2,1)}, bf16[128,3584]{1,0:T(8,128)(2,1)S(1)}, u32[]{:S(2)}, u32[]{:S(2)}) %collective-permute-start) | collective-permute-done | bytes 917536 | tf_op jit(solution)/shard_map/ppermute | solution.py:94
  50.8 0.0 collective-permute-done.1.refs_3_
  50.8 1.4 %broadcast_in_dim.32 = bf16[4,64,3712]{2,1,0:T(8,128)(2,1)} broadcast(bf16[64,3712]{1,0:T(8,128)(2,1)S(1)} %reshape.68), dimensions={1,2} | broadcast | bytes 2375680 | tf_op jit(solution)/shard_map/broadcast_in_dim | solution.py:111
  52.1 4.4 %all-to-all-start.1 = ((bf16[4,64,3712]{2,1,0:T(8,128)(2,1)}), bf16[4,64,3712]{2,1,0:T(8,128)(2,1)}, u32[]{:S(2)}, u32[]{:S(2)}) async-start(bf16[4,64,3712]{2,1,0:T(8,128)(2,1)} %broadcast_in_dim.32), calls=%async_computation.1 | async-start | bytes 3801088 | tf_op jit(solution)/shard_map/all_to_all | solution.py:112
  56.6 4.4 %collective-permute-start.2 = (bf16[128,3584]{1,0:T(8,128)(2,1)S(1)}, bf16[128,3584]{1,0:T(8,128)(2,1)S(1)}, u32[]{:S(2)}, u32[]{:S(2)}) collective-permute-start(bf16[128,3584]{1,0:T(8,128)(2,1)S(1)} %get-tuple-element.26.refs_0_), channel_id=1, source_target_pairs={{0,4},{4,0},{1,5},{5,1},{2,6},{6,2},{3,7},{7,3},{8,12},{12,8},{9,1... | collective-permute-start | bytes 2752520 | tf_op jit(solution)/shard_map/ppermute | solution.py:95
  60.9 3.6 %collective-permute-start.3 = (bf16[128,3584]{1,0:T(8,128)(2,1)S(1)}, bf16[128,3584]{1,0:T(8,128)(2,1)S(1)}, u32[]{:S(2)}, u32[]{:S(2)}) collective-permute-start(bf16[128,3584]{1,0:T(8,128)(2,1)S(1)} %get-tuple-element.26.refs_0_), channel_id=1, source_target_pairs={{0,1},{1,0},{2,3},{3,2},{4,5},{5,4},{6,7},{7,6},{8,9},{9,8},{10,11... | collective-permute-start | bytes 2752520 | tf_op jit(solution)/shard_map/ppermute | solution.py:115
  64.6 1.9 %collective-permute-start.4 = (bf16[128,3584]{1,0:T(8,128)(2,1)S(1)}, bf16[128,3584]{1,0:T(8,128)(2,1)S(1)}, u32[]{:S(2)}, u32[]{:S(2)}) collective-permute-start(bf16[128,3584]{1,0:T(8,128)(2,1)S(1)} %collective-permute-done.refs_1_), channel_id=1, source_target_pairs={{0,1},{1,0},{2,3},{3,2},{4,5},{5,4},{6,7},{7,6},{8,9},{9,8},{10,11... | collective-permute-start | bytes 2752520 | tf_op jit(solution)/shard_map/ppermute | solution.py:115
  66.5 2.4 %collective-permute-start.5 = (bf16[128,3584]{1,0:T(8,128)(2,1)}, bf16[128,3584]{1,0:T(8,128)(2,1)S(1)}, u32[]{:S(2)}, u32[]{:S(2)}) collective-permute-start(bf16[128,3584]{1,0:T(8,128)(2,1)} %collective-permute-done.1.refs_3_), channel_id=1, source_target_pairs={{0,1},{1,0},{2,3},{3,2},{4,5},{5,4},{6,7},{7,6},{8,9},{9,8},{10,11... | collective-permute-start | bytes 2752520 | tf_op jit(solution)/shard_map/ppermute | solution.py:115
  68.9 11.1 %collective-permute-done.2.refs_2_ = bf16[128,3584]{1,0:T(8,128)(2,1)S(1)} collective-permute-done((bf16[128,3584]{1,0:T(8,128)(2,1)S(1)}, bf16[128,3584]{1,0:T(8,128)(2,1)S(1)}, u32[]{:S(2)}, u32[]{:S(2)}) %collective-permute-start.2) | collective-permute-done | bytes 917536 | tf_op jit(solution)/shard_map/ppermute | solution.py:95
  80.0 0.0 collective-permute-done.3.refs_4_
  80.0 0.0 copy-start
  80.0 0.0 collective-permute-done.4.refs_5_
  80.0 1.0 copy-done
  81.0 0.0 copy-start.1
  81.0 0.0 collective-permute-done.5.refs_7_
  81.0 0.9 copy-done.1
  81.9 0.0 copy-start.2
  81.9 4.6 %collective-permute-start.6 = (bf16[128,3584]{1,0:T(8,128)(2,1)S(1)}, bf16[128,3584]{1,0:T(8,128)(2,1)}, u32[]{:S(2)}, u32[]{:S(2)}) collective-permute-start(bf16[128,3584]{1,0:T(8,128)(2,1)S(1)} %collective-permute-done.2.refs_2_), channel_id=1, source_target_pairs={{0,1},{1,0},{2,3},{3,2},{4,5},{5,4},{6,7},{7,6},{8,9},{9,8},{10,11... | collective-permute-start | bytes 2752520 | tf_op jit(solution)/shard_map/ppermute | solution.py:117
  86.5 0.0 copy-done.2
  86.5 2.2 %collective-permute-done.6.refs_6_ = bf16[128,3584]{1,0:T(8,128)(2,1)} collective-permute-done((bf16[128,3584]{1,0:T(8,128)(2,1)S(1)}, bf16[128,3584]{1,0:T(8,128)(2,1)}, u32[]{:S(2)}, u32[]{:S(2)}) %collective-permute-start.6) | collective-permute-done | bytes 917536 | tf_op jit(solution)/shard_map/ppermute | solution.py:117
  88.7 0.0 all-to-all-done.1
  88.7 0.0 copy-start.3
  88.7 6.0 %shard_map.59 = (f32[8,128,128]{2,1,0:T(8,128)S(1)}, f32[8,128,128]{2,1,0:T(8,128)}, s32[1,128]{1,0:T(1,128)S(1)}) custom-call(s32[1]{0:T(128)} %bitcast.8.k_ref, bf16[4,2,32,3712]{3,2,1,0:T(8,128)(2,1)} %bitcast.16.h_ref, bf16[128,3584]{1,0:T(8,128)(2,1)S(1)} %get-tuple-element.26.refs_0_, bf16[128,3584]{1,0:T(8,128)(2,1)S(1)} %collective-permute-done.refs_1_, ...), custom_call_target="tpu_custom_call" | custom-call | tf_op jit(solution)/shard_map/pallas_call | solution.py:46
  94.7 2.7 %collective-permute-start.7 = (f32[8,128,128]{2,1,0:T(8,128)}, f32[8,128,128]{2,1,0:T(8,128)S(1)}, u32[]{:S(2)}, u32[]{:S(2)}) collective-permute-start(f32[8,128,128]{2,1,0:T(8,128)} %get-tuple-element.20), channel_id=1, source_target_pairs={{0,2},{2,0},{1,3},{3,1},{4,6},{6,4},{5,7},{7,5},{8,10},{10,8},{9,1... | collective-permute-start | bytes 1572872 | tf_op jit(solution)/shard_map/ppermute | solution.py:120
  97.5 0.1 stack.44.first_ref
  97.6 12.4 %collective-permute-done.7.theirs_ref = f32[8,128,128]{2,1,0:T(8,128)S(1)} collective-permute-done((f32[8,128,128]{2,1,0:T(8,128)}, f32[8,128,128]{2,1,0:T(8,128)S(1)}, u32[]{:S(2)}, u32[]{:S(2)}) %collective-permute-start.7) | collective-permute-done | bytes 524320 | tf_op jit(solution)/shard_map/ppermute | solution.py:120
  110.0 0.9 shard_map.60
  110.9 22.1 %all_to_all.15 = f32[64,2,8]{2,1,0:T(2,128)S(1)} all-to-all(f32[64,2,8]{2,1,0:T(2,128)S(1)} %bitcast.38), channel_id=1, replica_groups=mesh['s1'=2,'s0'=2,'zh'=2,'y1'=4,'y0'=2,'x1'=2,'x0'=2,'core'=2] {'s0','y..., dimensions={0} | all-to-all | bytes 8192 | tf_op jit(solution)/shard_map/all_to_all | solution.py:134
  133.0 0.4 fusion.7
  133.4 0.1 copy.11
  133.4 0.1 copy.10
  133.5 0.2 fusion.4
  133.7 0.0 copy-done.3
  133.7 0.5 fusion.6
  (3 shorter events, 0.1 us)
Async XLA Ops:
  3.3 36.2 %all-to-all-start = ((bf16[32,2,3712]{2,1,0:T(2,128)(2,1)}), bf16[32,2,3712]{2,1,0:T(2,128)(2,1)S(1)}, u32[]{:S(2)}, u32[]{:S(2)}) async-start(bf16[32,2,3712]{2,1,0:T(2,128)(2,1)} %bitcast.15), calls=%async_computation | async-start | bytes 950272 | tf_op jit(solution)/shard_map/all_to_all | solution.py:108
  23.2 27.6 %collective-permute-start = (bf16[128,3584]{1,0:T(8,128)(2,1)}, bf16[128,3584]{1,0:T(8,128)(2,1)S(1)}, u32[]{:S(2)}, u32[]{:S(2)}) collective-permute-start(bf16[128,3584]{1,0:T(8,128)(2,1)} %get-tuple-element.27), channel_id=1, source_target_pairs={{0,2},{2,0},{1,3},{3,1},{4,6},{6,4},{5,7},{7,5},{8,10},{10,8},{9,1... | collective-permute-start | bytes 2752520 | tf_op jit(solution)/shard_map/ppermute | solution.py:94
  26.4 24.4 %collective-permute-start.1 = (bf16[128,3584]{1,0:T(8,128)(2,1)}, bf16[128,3584]{1,0:T(8,128)(2,1)}, u32[]{:S(2)}, u32[]{:S(2)}) collective-permute-start(bf16[128,3584]{1,0:T(8,128)(2,1)} %get-tuple-element.27), channel_id=1, source_target_pairs={{0,6},{2,4},{4,2},{6,0},{1,7},{3,5},{5,3},{7,1},{8,14},{10,12},{12... | collective-permute-start | bytes 2752520 | tf_op jit(solution)/shard_map/ppermute | solution.py:96
  52.1 36.6 %all-to-all-start.1 = ((bf16[4,64,3712]{2,1,0:T(8,128)(2,1)}), bf16[4,64,3712]{2,1,0:T(8,128)(2,1)}, u32[]{:S(2)}, u32[]{:S(2)}) async-start(bf16[4,64,3712]{2,1,0:T(8,128)(2,1)} %broadcast_in_dim.32), calls=%async_computation.1 | async-start | bytes 3801088 | tf_op jit(solution)/shard_map/all_to_all | solution.py:112
  56.6 23.5 %collective-permute-start.2 = (bf16[128,3584]{1,0:T(8,128)(2,1)S(1)}, bf16[128,3584]{1,0:T(8,128)(2,1)S(1)}, u32[]{:S(2)}, u32[]{:S(2)}) collective-permute-start(bf16[128,3584]{1,0:T(8,128)(2,1)S(1)} %get-tuple-element.26.refs_0_), channel_id=1, source_target_pairs={{0,4},{4,0},{1,5},{5,1},{2,6},{6,2},{3,7},{7,3},{8,12},{12,8},{9,1... | collective-permute-start | bytes 2752520 | tf_op jit(solution)/shard_map/ppermute | solution.py:95
  60.9 19.1 %collective-permute-start.3 = (bf16[128,3584]{1,0:T(8,128)(2,1)S(1)}, bf16[128,3584]{1,0:T(8,128)(2,1)S(1)}, u32[]{:S(2)}, u32[]{:S(2)}) collective-permute-start(bf16[128,3584]{1,0:T(8,128)(2,1)S(1)} %get-tuple-element.26.refs_0_), channel_id=1, source_target_pairs={{0,1},{1,0},{2,3},{3,2},{4,5},{5,4},{6,7},{7,6},{8,9},{9,8},{10,11... | collective-permute-start | bytes 2752520 | tf_op jit(solution)/shard_map/ppermute | solution.py:115
  64.6 15.5 %collective-permute-start.4 = (bf16[128,3584]{1,0:T(8,128)(2,1)S(1)}, bf16[128,3584]{1,0:T(8,128)(2,1)S(1)}, u32[]{:S(2)}, u32[]{:S(2)}) collective-permute-start(bf16[128,3584]{1,0:T(8,128)(2,1)S(1)} %collective-permute-done.refs_1_), channel_id=1, source_target_pairs={{0,1},{1,0},{2,3},{3,2},{4,5},{5,4},{6,7},{7,6},{8,9},{9,8},{10,11... | collective-permute-start | bytes 2752520 | tf_op jit(solution)/shard_map/ppermute | solution.py:115
  66.5 14.5 %collective-permute-start.5 = (bf16[128,3584]{1,0:T(8,128)(2,1)}, bf16[128,3584]{1,0:T(8,128)(2,1)S(1)}, u32[]{:S(2)}, u32[]{:S(2)}) collective-permute-start(bf16[128,3584]{1,0:T(8,128)(2,1)} %collective-permute-done.1.refs_3_), channel_id=1, source_target_pairs={{0,1},{1,0},{2,3},{3,2},{4,5},{5,4},{6,7},{7,6},{8,9},{9,8},{10,11... | collective-permute-start | bytes 2752520 | tf_op jit(solution)/shard_map/ppermute | solution.py:115
  80.0 1.0 copy-start
  81.0 0.9 copy-start.1
  81.9 4.6 %copy-start.2 = (bf16[128,3584]{1,0:T(8,128)(2,1)}, bf16[128,3584]{1,0:T(8,128)(2,1)S(1)}, u32[]{:S(2)}) copy-start(bf16[128,3584]{1,0:T(8,128)(2,1)S(1)} %collective-permute-done.5.refs_7_) | copy-start | bytes 2752516
  81.9 6.8 %collective-permute-start.6 = (bf16[128,3584]{1,0:T(8,128)(2,1)S(1)}, bf16[128,3584]{1,0:T(8,128)(2,1)}, u32[]{:S(2)}, u32[]{:S(2)}) collective-permute-start(bf16[128,3584]{1,0:T(8,128)(2,1)S(1)} %collective-permute-done.2.refs_2_), channel_id=1, source_target_pairs={{0,1},{1,0},{2,3},{3,2},{4,5},{5,4},{6,7},{7,6},{8,9},{9,8},{10,11... | collective-permute-start | bytes 2752520 | tf_op jit(solution)/shard_map/ppermute | solution.py:117
  88.7 45.0 %copy-start.3 = (f32[1,2]{1,0:T(1,128)S(1)}, f32[1,2]{1,0:T(1,128)}, u32[]{:S(2)}) copy-start(f32[1,2]{1,0:T(1,128)} %param.7) | copy-start | bytes 28
  94.7 15.2 %collective-permute-start.7 = (f32[8,128,128]{2,1,0:T(8,128)}, f32[8,128,128]{2,1,0:T(8,128)S(1)}, u32[]{:S(2)}, u32[]{:S(2)}) collective-permute-start(f32[8,128,128]{2,1,0:T(8,128)} %get-tuple-element.20), channel_id=1, source_target_pairs={{0,2},{2,0},{1,3},{3,1},{4,6},{6,4},{5,7},{7,5},{8,10},{10,8},{9,1... | collective-permute-start | bytes 1572872 | tf_op jit(solution)/shard_map/ppermute | solution.py:120

commit v7 on v5

v7 whole, which is shorter than its diff:
```python
import jax
import jax.numpy as jnp
import numpy as np
from jax import lax
from jax.experimental import pallas as pl
from jax.experimental.pallas import tpu as pltpu
from jax.sharding import Mesh, PartitionSpec as P

NAMES = ("s1", "s0", "zh", "y1", "y0", "x1", "x0", "core")
SIZES = (2, 2, 2, 4, 2, 2, 2, 2)
SEG = ("s1", "s0")
DP = ("zh", "y1", "y0", "x1", "x0", "core")
GA = ("s1", "zh", "y1")
GB = ("s0", "y0")
IDS = 128
SWAP = [(0, 1), (1, 0)]
SOON, FAR = [0, 1, 3, 4, 5, 7], [2, 6]


def size_of(axes):
    return int(np.prod([SIZES[NAMES.index(a)] for a in axes]))


def matmul_kernel(h_ref, *refs):
    pieces, (keep_ref, send_ref, id_ref, turned) = refs[:-4], refs[-4:]
    depth = pieces[0].shape[1]
    wide = h_ref.shape[-1]
    kept = h_ref[:, 0].reshape(-1, wide)
    sent = h_ref[:, 1].reshape(-1, wide)
    half = kept.shape[0]
    turned[:, :half] = kept[:, :depth].T
    turned[:, half:] = sent[:, :depth].T
    code = kept[:, depth:].astype(jnp.float32).T
    id_ref[...] = (code[0:1] * 256.0 + code[1:2]).astype(jnp.int32)
    for j, piece in enumerate(pieces):
        out = jnp.dot(piece[...], turned[...], preferred_element_type=jnp.float32)
        keep_ref[j] = out[:, :half]
        send_ref[j] = out[:, half:]


def partial_logits(gathered, pieces):
    nb, _, rows, _ = gathered.shape
    voc, depth = pieces[0].shape
    block = jax.ShapeDtypeStruct((len(pieces), voc, nb * rows), jnp.float32)
    vmem = pl.BlockSpec(memory_space=pltpu.VMEM)
    return pl.pallas_call(
        matmul_kernel,
        in_specs=[vmem] * (1 + len(pieces)),
        out_specs=[vmem] * 3,
        out_shape=[block, block, jax.ShapeDtypeStruct((1, nb * rows), jnp.int32)],
        scratch_shapes=[pltpu.VMEM((depth, 2 * nb * rows), gathered.dtype)],
        compiler_params=pltpu.CompilerParams(vmem_limit_bytes=51 * 1024 * 1024),
    )(gathered, *pieces)


def stats_kernel(first_ref, mine_ref, mine_far_ref, theirs_ref, theirs_far_ref, ids_ref, out_ref):
    voc, rows = mine_ref.shape[1:]
    mine = [mine_ref[SOON.index(j)] if j in SOON else mine_far_ref[FAR.index(j)] for j in range(8)]
    theirs = [
        theirs_ref[SOON.index(j ^ 1)] if j ^ 1 in SOON else theirs_far_ref[FAR.index(j ^ 1)]
        for j in range(8)
    ]
    logits = [m + t for m, t in zip(mine, theirs)]
    top = logits[0]
    for piece in logits[1:]:
        top = jnp.maximum(top, piece)
    top = jnp.max(top, axis=0, keepdims=True)
    ids = ids_ref[...]
    entry = lax.broadcasted_iota(jnp.int32, (voc, rows), 0)
    total = jnp.zeros((voc, rows), jnp.float32)
    picked = jnp.zeros((voc, rows), jnp.float32)
    for j, piece in enumerate(logits):
        total += jnp.exp(piece - top)
        picked += jnp.where(entry + first_ref[j] == ids, piece, 0.0)
    total = jnp.sum(total, axis=0, keepdims=True)
    picked = jnp.sum(picked, axis=0, keepdims=True)
    line = lax.broadcasted_iota(jnp.int32, (128, rows), 0)
    out_ref[...] = jnp.where(line == 0, top, jnp.where(line == 1, total, picked)).T


def local_stats(first, *arrays):
    vmem = pl.BlockSpec(memory_space=pltpu.VMEM)
    return pl.pallas_call(
        stats_kernel,
        in_specs=[pl.BlockSpec(memory_space=pltpu.SMEM)] + [vmem] * len(arrays),
        out_specs=vmem,
        out_shape=jax.ShapeDtypeStruct((arrays[0].shape[2], 128), jnp.float32),
        compiler_params=pltpu.CompilerParams(vmem_limit_bytes=8 * 1024 * 1024),
    )(first, *arrays)


def per_device(hidden, head_weight, target_ids, policy_logp):
    na, nb = size_of(GA), size_of(GB)
    rows, width = hidden.shape[1:]
    voc = head_weight.shape[0]
    depth = width // 2
    at = {a: lax.axis_index(a) for a in NAMES}
    k = at["x0"]

    ids = target_ids.reshape(rows, 1)
    lane = lax.broadcasted_iota(jnp.int32, (rows, IDS), 1)
    code = jnp.where(lane == 0, ids >> 8, ids & 255).astype(hidden.dtype)
    low, high = hidden[0, :, :depth], hidden[0, :, depth:]
    own = jnp.concatenate([jnp.where(k == 0, low, high), code], axis=1)
    other = jnp.concatenate([jnp.where(k == 0, high, low), code], axis=1)
    other = lax.ppermute(other, "x0", SWAP)

    kept = lax.dynamic_slice_in_dim(head_weight, k * depth, depth, 1)
    given = lax.dynamic_slice_in_dim(head_weight, (1 - k) * depth, depth, 1)
    near = lax.ppermute(given, "x0", SWAP)
    back = lax.ppermute(given, ("x1", "x0"), [(i, i ^ 3) for i in range(4)])

    message = jnp.broadcast_to(jnp.stack([own, other])[None], (na, 2, rows, depth + IDS))
    column = lax.all_to_all(message, GA, 0, 0, tiled=True)
    column = column.transpose(1, 0, 2, 3).reshape(2 * na * rows, depth + IDS)
    column, near, back = lax.optimization_barrier((column, near, back))
    copies = jnp.broadcast_to(column[None], (nb,) + column.shape)
    gathered = lax.all_to_all(copies, GB, 0, 0, tiled=True)
    gathered = gathered.reshape(nb, 2, na * rows, depth + IDS)
    far = lax.ppermute(kept, "x1", SWAP)

    soon = [kept, near, back]
    soon += [lax.ppermute(piece, "core", SWAP) for piece in soon]
    mine, send, ids = partial_logits(gathered, soon)
    theirs = lax.ppermute(send, "x0", SWAP)
    far, mine = lax.optimization_barrier((far, mine))
    late = [far, lax.ppermute(far, "core", SWAP)]
    mine_far, send_far, _ = partial_logits(gathered, late)
    theirs_far = lax.ppermute(send_far, "x0", SWAP)

    firsts = []
    for j in range(8):
        place = dict(at)
        place["x0"] = at["x0"] ^ (j & 1)
        place["x1"] = at["x1"] ^ ((j >> 1) & 1)
        place["core"] = at["core"] ^ (j >> 2)
        flat = 0
        for a, n in zip(NAMES, SIZES):
            flat = flat * n + place[a]
        firsts.append(flat * voc)
    stats = local_stats(
        jnp.stack(firsts), mine, mine_far, theirs, theirs_far, ids
    )[:, :8]
    stats = stats.reshape(nb * na, rows, 8)
    stats = lax.all_to_all(stats, GB + GA, 0, 0, tiled=True)
    tops, totals, picks = stats[..., 0], stats[..., 1], stats[..., 2]
    highest = jnp.max(tops, axis=0)
    total = jnp.sum(totals * jnp.exp(tops - highest), axis=0)
    picked = jnp.sum(picks, axis=0)
    ref_logp = (picked - (highest + jnp.log(total))).reshape(1, rows)
    log_ratio = ref_logp - policy_logp
    kl_term = jnp.minimum(jnp.exp(log_ratio) - log_ratio - 1.0, 10.0)
    return (ref_logp, kl_term)


def solution(mesh):
    fine = Mesh(mesh.devices.reshape(SIZES), NAMES)
    return jax.shard_map(
        per_device,
        mesh=fine,
        in_specs=(P(SEG, DP, None), P(SEG + DP, None), P(SEG, DP), P(SEG, DP)),
        out_specs=(P(SEG, DP), P(SEG, DP)),
        check_vma=False,
    )
```

time: 140 us -> 129 us (0.921)
  waiting for transfers between devices: 32.7 us -> 23.9 us
  starting transfers between devices: 37.5 us -> 33.4 us
  local copies, waits for them, and re-layouts: 5.16 us -> 8.6 us
  blocking collectives: 53.4 us -> 50.7 us
    all_to_all x1, waiting for transfers between devices: 0.01 us -> 9.61 us  [per_device(): gathered = lax.all_to_all(copies, GB, 0, 0, tiled=True)]
    ppermute x7 -> x9, waiting for transfers between devices: 19.4 us -> 9.93 us  [the longest x1 6.97 us: per_device(): far = lax.ppermute(kept, 'x1', SWAP)]
    ppermute x1, waiting for transfers between devices: 13.3 us -> 4.35 us  [per_device(): theirs = lax.ppermute(send, 'x0', SWAP)]
    ppermute x7 -> x9, starting transfers between devices: 31 us -> 27.1 us  [the longest x3 8.28 us: per_device(): soon += [lax.ppermute(piece, 'core', SWAP) for piece in soon]]
    all_to_all x1, blocking collectives: 36 us -> 33.3 us  [per_device(): column = lax.all_to_all(message, GA, 0, 0, tiled=True)]
    dynamic_slice x1, local copies, waits for them, and re-layouts: 0.13 us -> 2.51 us  [per_device(): given = lax.dynamic_slice_in_dim(head_weight, (1 - k) * depth, depth, 1)]
    pallas_call x1 -> x2, Pallas kernels: 5.98 us -> 7.28 us  [partial_logits(): pl.pallas_call(matmul_kernel, in_specs=[vmem] * (1 + len(pieces)), out_sp...]
  transfers between devices with their start and end apart: 9 -> 11, of which waited for: 3 -> 5; matrix products, arithmetic and copies ran while one was open for 0% -> 4% of each run, Pallas kernels for 0% -> 6%
where the time goes in v7:
time: 129 us; the launch traced here: 128 us
  blocking collectives  50.7 us (39%)
  starting transfers between devices  33.4 us (26%)
  waiting for transfers between devices  23.9 us (19%)
  local copies, waits for them, and re-layouts  8.6 us (7%)
  Pallas kernels  8.17 us (6%)
  other arithmetic  2.67 us (2%)
    all_to_all x1, blocking collectives, per_device(): column = lax.all_to_all(message, GA, 0, 0, tiled=True)  33.3 us
    all_to_all x1, blocking collectives, per_device(): stats = lax.all_to_all(stats, GB + GA, 0, 0, tiled=True)  17.4 us
    all_to_all x1, waiting for transfers between devices, per_device(): gathered = lax.all_to_all(copies, GB, 0, 0, tiled=True)  9.61 us
    ppermute x3, starting transfers between devices, per_device(): soon += [lax.ppermute(piece, 'core', SWAP) for piece in soon]  8.28 us
    pallas_call x2, Pallas kernels, partial_logits(): pl.pallas_call(matmul_kernel, in_specs=[vmem] * (1 + len(pieces)), out_sp...  7.28 us
    ppermute x1, waiting for transfers between devices, per_device(): far = lax.ppermute(kept, 'x1', SWAP)  6.97 us
    ppermute x1, starting transfers between devices, per_device(): back = lax.ppermute(given, ('x1', 'x0'), [(i, i ^ 3) for i in range(4)])  4.63 us
    all_to_all x1, starting transfers between devices, per_device(): gathered = lax.all_to_all(copies, GB, 0, 0, tiled=True)  4.4 us
  transfers between devices with their start and end apart: 11, of which 5 were waited for; matrix products, arithmetic and copies ran while one was open for 4% of the time, Pallas kernels for 6%

profile of v7, /device:TPU:1, one launch (start us, length us, event | category | flops | bytes accessed | tf_op | source)
XLA Modules:
  0.0 128.4 jit_solution(9778451416707507852)
XLA Ops:
  0.6 0.7 shift-right-arithmetic_bitcast_fusion
  1.3 0.8 fusion.1
  2.1 0.1 select_convert_fusion
  2.2 3.9 %collective-permute-start.1 = (bf16[2,3712]{1,0:T(2,128)(2,1)S(1)}, bf16[2,3712]{1,0:T(2,128)(2,1)S(1)}, u32[]{:S(2)}, u32[]{:S(2)}) collective-permute-start(bf16[2,3712]{1,0:T(2,128)(2,1)S(1)} %get-tuple-element.35), channel_id=1, source_target_pairs={{0,2},{2,0},{1,3},{3,1},{4,6},{6,4},{5,7},{7,5},{8,10},{10,8},{9,1... | collective-permute-start | bytes 44552 | tf_op jit(solution)/shard_map/ppermute | solution.py:106
  6.1 2.5 %constant_dynamic-slice_fusion = (bf16[128,3584]{1,0:T(8,128)(2,1)}, bf16[128,3584]{1,0:T(8,128)(2,1)S(1)}) fusion(bf16[128,7168]{1,0:T(8,128)(2,1)} %param.5, s32[]{:T(128)S(6)} %select_n.35, s32[]{:T(128)S(6)} %select_n.28), kind=kLoop, calls=%fused_computation.21 | loop fusion | bytes 3670024 | tf_op jit(solution)/shard_map/dynamic_slice | solution.py:109
  8.7 1.9 %collective-permute-start.2 = (bf16[128,3584]{1,0:T(8,128)(2,1)}, bf16[128,3584]{1,0:T(8,128)(2,1)S(1)}, u32[]{:S(2)}, u32[]{:S(2)}) collective-permute-start(bf16[128,3584]{1,0:T(8,128)(2,1)} %get-tuple-element.26), channel_id=1, source_target_pairs={{0,2},{2,0},{1,3},{3,1},{4,6},{6,4},{5,7},{7,5},{8,10},{10,8},{9,1... | collective-permute-start | bytes 2752520 | tf_op jit(solution)/shard_map/ppermute | solution.py:110
  10.6 4.6 %collective-permute-start.3 = (bf16[128,3584]{1,0:T(8,128)(2,1)}, bf16[128,3584]{1,0:T(8,128)(2,1)}, u32[]{:S(2)}, u32[]{:S(2)}) collective-permute-start(bf16[128,3584]{1,0:T(8,128)(2,1)} %get-tuple-element.26), channel_id=1, source_target_pairs={{0,6},{2,4},{4,2},{6,0},{1,7},{3,5},{5,3},{7,1},{8,14},{10,12},{12... | collective-permute-start | bytes 2752520 | tf_op jit(solution)/shard_map/ppermute | solution.py:111
  15.2 0.0 collective-permute-done.1
  15.3 0.2 broadcast_in_dim.31
  15.5 33.3 %all_to_all.15 = bf16[16,2,2,3712]{3,2,1,0:T(2,128)(2,1)S(1)} all-to-all(bf16[16,2,2,3712]{3,2,1,0:T(2,128)(2,1)S(1)} %broadcast_in_dim.31), channel_id=1, replica_groups=mesh['s1'=2,'s0'=2,'zh'=2,'y1'=4,'y0'=2,'x1'=2,'x0'=2,'core'=2] {'s1','z..., dimensions={0} | all-to-all | bytes 950272 | tf_op jit(solution)/shard_map/all_to_all | solution.py:114
  48.8 1.1 copy.14
  49.9 1.2 reshape.64
  51.1 0.0 collective-permute-done.2.refs_1_
  51.1 0.0 collective-permute-done.3.refs_2_
  51.1 1.4 %broadcast_in_dim.32 = bf16[4,64,3712]{2,1,0:T(8,128)(2,1)} broadcast(bf16[64,3712]{1,0:T(8,128)(2,1)S(1)} %reshape.64), dimensions={1,2} | broadcast | bytes 2375680 | tf_op jit(solution)/shard_map/broadcast_in_dim | solution.py:117
  52.5 4.4 %all-to-all-start.1 = ((bf16[4,64,3712]{2,1,0:T(8,128)(2,1)}), bf16[4,64,3712]{2,1,0:T(8,128)(2,1)}, u32[]{:S(2)}, u32[]{:S(2)}) async-start(bf16[4,64,3712]{2,1,0:T(8,128)(2,1)} %broadcast_in_dim.32), calls=%async_computation.1 | async-start | bytes 3801088 | tf_op jit(solution)/shard_map/all_to_all | solution.py:118
  56.9 4.0 %collective-permute-start.4 = (bf16[128,3584]{1,0:T(8,128)(2,1)S(1)}, bf16[128,3584]{1,0:T(8,128)(2,1)S(1)}, u32[]{:S(2)}, u32[]{:S(2)}) collective-permute-start(bf16[128,3584]{1,0:T(8,128)(2,1)S(1)} %get-tuple-element.27.refs_0_), channel_id=1, source_target_pairs={{0,1},{1,0},{2,3},{3,2},{4,5},{5,4},{6,7},{7,6},{8,9},{9,8},{10,11... | collective-permute-start | bytes 2752520 | tf_op jit(solution)/shard_map/ppermute | solution.py:123
  60.9 1.9 %collective-permute-start.5 = (bf16[128,3584]{1,0:T(8,128)(2,1)S(1)}, bf16[128,3584]{1,0:T(8,128)(2,1)S(1)}, u32[]{:S(2)}, u32[]{:S(2)}) collective-permute-start(bf16[128,3584]{1,0:T(8,128)(2,1)S(1)} %collective-permute-done.2.refs_1_), channel_id=1, source_target_pairs={{0,1},{1,0},{2,3},{3,2},{4,5},{5,4},{6,7},{7,6},{8,9},{9,8},{10,11... | collective-permute-start | bytes 2752520 | tf_op jit(solution)/shard_map/ppermute | solution.py:123
  62.8 2.4 %collective-permute-start.6 = (bf16[128,3584]{1,0:T(8,128)(2,1)}, bf16[128,3584]{1,0:T(8,128)(2,1)}, u32[]{:S(2)}, u32[]{:S(2)}) collective-permute-start(bf16[128,3584]{1,0:T(8,128)(2,1)} %collective-permute-done.3.refs_2_), channel_id=1, source_target_pairs={{0,1},{1,0},{2,3},{3,2},{4,5},{5,4},{6,7},{7,6},{8,9},{9,8},{10,11... | collective-permute-start | bytes 2752520 | tf_op jit(solution)/shard_map/ppermute | solution.py:123
  65.2 2.4 %collective-permute-start = (bf16[128,3584]{1,0:T(8,128)(2,1)S(1)}, bf16[128,3584]{1,0:T(8,128)(2,1)S(1)}, u32[]{:S(2)}, u32[]{:S(2)}) collective-permute-start(bf16[128,3584]{1,0:T(8,128)(2,1)S(1)} %get-tuple-element.27.refs_0_), channel_id=1, source_target_pairs={{0,4},{4,0},{1,5},{5,1},{2,6},{6,2},{3,7},{7,3},{8,12},{12,8},{9,1... | collective-permute-start | bytes 2752520 | tf_op jit(solution)/shard_map/ppermute | solution.py:120
  67.7 0.0 collective-permute-done.4.refs_3_
  67.7 0.0 copy-start
  67.7 0.0 collective-permute-done.5.refs_4_
  67.7 0.9 copy-done
  68.6 0.0 copy-start.1
  68.6 0.9 copy-done.1
  69.6 0.0 collective-permute-done.6.refs_5_
  69.6 9.6 %all-to-all-done.1 = bf16[4,64,3712]{2,1,0:T(8,128)(2,1)} async-done(((bf16[4,64,3712]{2,1,0:T(8,128)(2,1)}), bf16[4,64,3712]{2,1,0:T(8,128)(2,1)}, u32[]{:S(2)}, u32[]{:S(2)}) %all-to-all-start.1) | async-done | bytes 1900576 | tf_op jit(solution)/shard_map/all_to_all | solution.py:118
  79.2 4.4 %shard_map.59 = (f32[6,128,128]{2,1,0:T(8,128)S(1)}, f32[6,128,128]{2,1,0:T(8,128)S(1)}, s32[1,128]{1,0:T(1,128)S(1)}) custom-call(bf16[4,2,32,3712]{3,2,1,0:T(8,128)(2,1)} %bitcast.15.h_ref, bf16[128,3584]{1,0:T(8,128)(2,1)S(1)} %get-tuple-element.27.refs_0_, bf16[128,3584]{1,0:T(8,128)(2,1)S(1)} %collective-permute-done.2.refs_1_, ...), custom_call_target="tpu_custom_call" | custom-call | tf_op jit(solution)/shard_map/pallas_call | solution.py:46
  83.6 7.0 %collective-permute-done.refs_0_ = bf16[128,3584]{1,0:T(8,128)(2,1)S(1)} collective-permute-done((bf16[128,3584]{1,0:T(8,128)(2,1)S(1)}, bf16[128,3584]{1,0:T(8,128)(2,1)S(1)}, u32[]{:S(2)}, u32[]{:S(2)}) %collective-permute-start) | collective-permute-done | bytes 917536 | tf_op jit(solution)/shard_map/ppermute | solution.py:120
  90.6 2.7 %collective-permute-start.7 = (bf16[128,3584]{1,0:T(8,128)(2,1)S(1)}, bf16[128,3584]{1,0:T(8,128)(2,1)S(1)}, u32[]{:S(2)}, u32[]{:S(2)}) collective-permute-start(bf16[128,3584]{1,0:T(8,128)(2,1)S(1)} %collective-permute-done.refs_0_), channel_id=1, source_target_pairs={{0,1},{1,0},{2,3},{3,2},{4,5},{5,4},{6,7},{7,6},{8,9},{9,8},{10,11... | collective-permute-start | bytes 2752520 | tf_op jit(solution)/shard_map/ppermute | solution.py:127
  93.3 0.0 copy-start.2
  93.3 1.9 %collective-permute-start.8 = (f32[6,128,128]{2,1,0:T(8,128)S(1)}, f32[6,128,128]{2,1,0:T(8,128)S(1)}, u32[]{:S(2)}, u32[]{:S(2)}) collective-permute-start(f32[6,128,128]{2,1,0:T(8,128)S(1)} %get-tuple-element.19), channel_id=1, source_target_pairs={{0,2},{2,0},{1,3},{3,1},{4,6},{6,4},{5,7},{7,5},{8,10},{10,8},{9,1... | collective-permute-start | bytes 1179656 | tf_op jit(solution)/shard_map/ppermute | solution.py:125
  95.2 0.1 collective-permute-done.7.refs_1_
  95.4 2.9 %shard_map.60 = (f32[2,128,128]{2,1,0:T(8,128)S(1)}, f32[2,128,128]{2,1,0:T(8,128)S(1)}, s32[1,128]{1,0:T(1,128)}) custom-call(bf16[4,2,32,3712]{3,2,1,0:T(8,128)(2,1)} %bitcast.15.h_ref, bf16[128,3584]{1,0:T(8,128)(2,1)S(1)} %collective-permute-done.refs_0_, bf16[128,3584]{1,0:T(8,128)(2,1)S(1)} %collective-permute-done.7.refs_1_), custom_call_target="tpu_custom_call" | custom-call | tf_op jit(solution)/shard_map/pallas_call | solution.py:46
  98.2 3.2 %collective-permute-start.9 = (f32[2,128,128]{2,1,0:T(8,128)S(1)}, f32[2,128,128]{2,1,0:T(8,128)S(1)}, u32[]{:S(2)}, u32[]{:S(2)}) collective-permute-start(f32[2,128,128]{2,1,0:T(8,128)S(1)} %get-tuple-element.20), channel_id=1, source_target_pairs={{0,2},{2,0},{1,3},{3,1},{4,6},{6,4},{5,7},{7,5},{8,10},{10,8},{9,1... | collective-permute-start | bytes 393224 | tf_op jit(solution)/shard_map/ppermute | solution.py:129
  101.5 0.1 stack.44.first_ref
  101.6 4.4 %collective-permute-done.8.theirs_ref = f32[6,128,128]{2,1,0:T(8,128)S(1)} collective-permute-done((f32[6,128,128]{2,1,0:T(8,128)S(1)}, f32[6,128,128]{2,1,0:T(8,128)S(1)}, u32[]{:S(2)}, u32[]{:S(2)}) %collective-permute-start.8) | collective-permute-done | bytes 393248 | tf_op jit(solution)/shard_map/ppermute | solution.py:125
  105.9 2.8 %collective-permute-done.9.theirs_far_ref = f32[2,128,128]{2,1,0:T(8,128)S(1)} collective-permute-done((f32[2,128,128]{2,1,0:T(8,128)S(1)}, f32[2,128,128]{2,1,0:T(8,128)S(1)}, u32[]{:S(2)}, u32[]{:S(2)}) %collective-permute-start.9) | collective-permute-done | bytes 131104 | tf_op jit(solution)/shard_map/ppermute | solution.py:129
  108.7 0.9 shard_map.61
  109.6 17.4 %all_to_all.16 = f32[64,2,8]{2,1,0:T(2,128)S(1)} all-to-all(f32[64,2,8]{2,1,0:T(2,128)S(1)} %bitcast.36), channel_id=1, replica_groups=mesh['s1'=2,'s0'=2,'zh'=2,'y1'=4,'y0'=2,'x1'=2,'x0'=2,'core'=2] {'s0','y..., dimensions={0} | all-to-all | bytes 8192 | tf_op jit(solution)/shard_map/all_to_all | solution.py:145
  127.1 0.4 fusion.8
  127.4 0.1 copy.15
  127.5 0.1 copy.16
  127.6 0.2 fusion.5
  127.8 0.0 copy-done.2
  127.8 0.5 fusion.7
  (3 shorter events, 0.1 us)
Async XLA Ops:
  2.2 13.0 %collective-permute-start.1 = (bf16[2,3712]{1,0:T(2,128)(2,1)S(1)}, bf16[2,3712]{1,0:T(2,128)(2,1)S(1)}, u32[]{:S(2)}, u32[]{:S(2)}) collective-permute-start(bf16[2,3712]{1,0:T(2,128)(2,1)S(1)} %get-tuple-element.35), channel_id=1, source_target_pairs={{0,2},{2,0},{1,3},{3,1},{4,6},{6,4},{5,7},{7,5},{8,10},{10,8},{9,1... | collective-permute-start | bytes 44552 | tf_op jit(solution)/shard_map/ppermute | solution.py:106
  8.7 42.5 %collective-permute-start.2 = (bf16[128,3584]{1,0:T(8,128)(2,1)}, bf16[128,3584]{1,0:T(8,128)(2,1)S(1)}, u32[]{:S(2)}, u32[]{:S(2)}) collective-permute-start(bf16[128,3584]{1,0:T(8,128)(2,1)} %get-tuple-element.26), channel_id=1, source_target_pairs={{0,2},{2,0},{1,3},{3,1},{4,6},{6,4},{5,7},{7,5},{8,10},{10,8},{9,1... | collective-permute-start | bytes 2752520 | tf_op jit(solution)/shard_map/ppermute | solution.py:110
  10.6 40.6 %collective-permute-start.3 = (bf16[128,3584]{1,0:T(8,128)(2,1)}, bf16[128,3584]{1,0:T(8,128)(2,1)}, u32[]{:S(2)}, u32[]{:S(2)}) collective-permute-start(bf16[128,3584]{1,0:T(8,128)(2,1)} %get-tuple-element.26), channel_id=1, source_target_pairs={{0,6},{2,4},{4,2},{6,0},{1,7},{3,5},{5,3},{7,1},{8,14},{10,12},{12... | collective-permute-start | bytes 2752520 | tf_op jit(solution)/shard_map/ppermute | solution.py:111
  52.5 26.7 %all-to-all-start.1 = ((bf16[4,64,3712]{2,1,0:T(8,128)(2,1)}), bf16[4,64,3712]{2,1,0:T(8,128)(2,1)}, u32[]{:S(2)}, u32[]{:S(2)}) async-start(bf16[4,64,3712]{2,1,0:T(8,128)(2,1)} %broadcast_in_dim.32), calls=%async_computation.1 | async-start | bytes 3801088 | tf_op jit(solution)/shard_map/all_to_all | solution.py:118
  56.9 10.7 %collective-permute-start.4 = (bf16[128,3584]{1,0:T(8,128)(2,1)S(1)}, bf16[128,3584]{1,0:T(8,128)(2,1)S(1)}, u32[]{:S(2)}, u32[]{:S(2)}) collective-permute-start(bf16[128,3584]{1,0:T(8,128)(2,1)S(1)} %get-tuple-element.27.refs_0_), channel_id=1, source_target_pairs={{0,1},{1,0},{2,3},{3,2},{4,5},{5,4},{6,7},{7,6},{8,9},{9,8},{10,11... | collective-permute-start | bytes 2752520 | tf_op jit(solution)/shard_map/ppermute | solution.py:123
  60.9 6.8 %collective-permute-start.5 = (bf16[128,3584]{1,0:T(8,128)(2,1)S(1)}, bf16[128,3584]{1,0:T(8,128)(2,1)S(1)}, u32[]{:S(2)}, u32[]{:S(2)}) collective-permute-start(bf16[128,3584]{1,0:T(8,128)(2,1)S(1)} %collective-permute-done.2.refs_1_), channel_id=1, source_target_pairs={{0,1},{1,0},{2,3},{3,2},{4,5},{5,4},{6,7},{7,6},{8,9},{9,8},{10,11... | collective-permute-start | bytes 2752520 | tf_op jit(solution)/shard_map/ppermute | solution.py:123
  62.8 6.8 %collective-permute-start.6 = (bf16[128,3584]{1,0:T(8,128)(2,1)}, bf16[128,3584]{1,0:T(8,128)(2,1)}, u32[]{:S(2)}, u32[]{:S(2)}) collective-permute-start(bf16[128,3584]{1,0:T(8,128)(2,1)} %collective-permute-done.3.refs_2_), channel_id=1, source_target_pairs={{0,1},{1,0},{2,3},{3,2},{4,5},{5,4},{6,7},{7,6},{8,9},{9,8},{10,11... | collective-permute-start | bytes 2752520 | tf_op jit(solution)/shard_map/ppermute | solution.py:123
  65.2 25.4 %collective-permute-start = (bf16[128,3584]{1,0:T(8,128)(2,1)S(1)}, bf16[128,3584]{1,0:T(8,128)(2,1)S(1)}, u32[]{:S(2)}, u32[]{:S(2)}) collective-permute-start(bf16[128,3584]{1,0:T(8,128)(2,1)S(1)} %get-tuple-element.27.refs_0_), channel_id=1, source_target_pairs={{0,4},{4,0},{1,5},{5,1},{2,6},{6,2},{3,7},{7,3},{8,12},{12,8},{9,1... | collective-permute-start | bytes 2752520 | tf_op jit(solution)/shard_map/ppermute | solution.py:120
  67.7 1.0 copy-start
  68.6 0.9 copy-start.1
  90.6 4.8 %collective-permute-start.7 = (bf16[128,3584]{1,0:T(8,128)(2,1)S(1)}, bf16[128,3584]{1,0:T(8,128)(2,1)S(1)}, u32[]{:S(2)}, u32[]{:S(2)}) collective-permute-start(bf16[128,3584]{1,0:T(8,128)(2,1)S(1)} %collective-permute-done.refs_0_), channel_id=1, source_target_pairs={{0,1},{1,0},{2,3},{3,2},{4,5},{5,4},{6,7},{7,6},{8,9},{9,8},{10,11... | collective-permute-start | bytes 2752520 | tf_op jit(solution)/shard_map/ppermute | solution.py:127
  93.3 34.5 %copy-start.2 = (f32[1,2]{1,0:T(1,128)S(1)}, f32[1,2]{1,0:T(1,128)}, u32[]{:S(2)}) copy-start(f32[1,2]{1,0:T(1,128)} %param.7) | copy-start | bytes 28
  93.3 12.6 %collective-permute-start.8 = (f32[6,128,128]{2,1,0:T(8,128)S(1)}, f32[6,128,128]{2,1,0:T(8,128)S(1)}, u32[]{:S(2)}, u32[]{:S(2)}) collective-permute-start(f32[6,128,128]{2,1,0:T(8,128)S(1)} %get-tuple-element.19), channel_id=1, source_target_pairs={{0,2},{2,0},{1,3},{3,1},{4,6},{6,4},{5,7},{7,5},{8,10},{10,8},{9,1... | collective-permute-start | bytes 1179656 | tf_op jit(solution)/shard_map/ppermute | solution.py:125
  98.2 10.5 %collective-permute-start.9 = (f32[2,128,128]{2,1,0:T(8,128)S(1)}, f32[2,128,128]{2,1,0:T(8,128)S(1)}, u32[]{:S(2)}, u32[]{:S(2)}) collective-permute-start(f32[2,128,128]{2,1,0:T(8,128)S(1)} %get-tuple-element.20), channel_id=1, source_target_pairs={{0,2},{2,0},{1,3},{3,1},{4,6},{6,4},{5,7},{7,5},{8,10},{10,8},{9,1... | collective-permute-start | bytes 393224 | tf_op jit(solution)/shard_map/ppermute | solution.py:129

commit v8 on v7

--- a/solution.py
+++ b/solution.py
@@ -89,6 +89,33 @@
     )(first, *arrays)
 
 
+def finish_kernel(stats_ref, policy_ref, logp_ref, kl_ref):
+    rows = stats_ref.shape[1]
+    lane = lax.broadcasted_iota(jnp.int32, (1, rows), 1)
+    ref_logp = jnp.zeros((1, rows), jnp.float32)
+    for r in range(rows):
+        tops, totals, picks = (stats_ref[:, r, c : c + 1] for c in range(3))
+        highest = jnp.max(tops, axis=0, keepdims=True)
+        total = jnp.sum(totals * jnp.exp(tops - highest), axis=0, keepdims=True)
+        picked = jnp.sum(picks, axis=0, keepdims=True)
+        ref_logp = jnp.where(lane == r, picked - (highest + jnp.log(total)), ref_logp)
+    log_ratio = ref_logp - policy_ref[...]
+    logp_ref[...] = ref_logp
+    kl_ref[...] = jnp.minimum(jnp.exp(log_ratio) - log_ratio - 1.0, 10.0)
+
+
+def finish(stats, policy_logp):
+    vmem = pl.BlockSpec(memory_space=pltpu.VMEM)
+    out = jax.ShapeDtypeStruct(policy_logp.shape, jnp.float32)
+    return pl.pallas_call(
+        finish_kernel,
+        in_specs=[vmem] * 2,
+        out_specs=[vmem] * 2,
+        out_shape=[out, out],
+        compiler_params=pltpu.CompilerParams(vmem_limit_bytes=2 * 1024 * 1024),
+    )(stats, policy_logp)
+
+
 def per_device(hidden, head_weight, target_ids, policy_logp):
     na, nb = size_of(GA), size_of(GB)
     rows, width = hidden.shape[1:]
@@ -119,6 +146,7 @@
     gathered = gathered.reshape(nb, 2, na * rows, depth + IDS)
     far = lax.ppermute(kept, "x1", SWAP)
 
+    gathered, far = lax.optimization_barrier((gathered, far))
     soon = [kept, near, back]
     soon += [lax.ppermute(piece, "core", SWAP) for piece in soon]
     mine, send, ids = partial_logits(gathered, soon)
@@ -143,14 +171,7 @@
     )[:, :8]
     stats = stats.reshape(nb * na, rows, 8)
     stats = lax.all_to_all(stats, GB + GA, 0, 0, tiled=True)
-    tops, totals, picks = stats[..., 0], stats[..., 1], stats[..., 2]
-    highest = jnp.max(tops, axis=0)
-    total = jnp.sum(totals * jnp.exp(tops - highest), axis=0)
-    picked = jnp.sum(picks, axis=0)
-    ref_logp = (picked - (highest + jnp.log(total))).reshape(1, rows)
-    log_ratio = ref_logp - policy_logp
-    kl_term = jnp.minimum(jnp.exp(log_ratio) - log_ratio - 1.0, 10.0)
-    return (ref_logp, kl_term)
+    return tuple(finish(stats, policy_logp))
 
 
 def solution(mesh):

time: 129 us -> 123 us (0.953)
  waiting for transfers between devices: 23.9 us -> 19.5 us
  local copies, waits for them, and re-layouts: 8.6 us -> 4.73 us
  starting transfers between devices: 33.4 us -> 35.9 us
    all_to_all x1, waiting for transfers between devices: 9.61 us -> 0.01 us  [per_device(): gathered = lax.all_to_all(copies, GB, 0, 0, tiled=True)]
    ppermute x1, waiting for transfers between devices: 6.97 us -> 12.2 us  [per_device(): far = lax.ppermute(kept, 'x1', SWAP)]
    ppermute x1, starting transfers between devices: 2.69 us -> 4.88 us  [per_device(): late = [far, lax.ppermute(far, 'core', SWAP)]]
    unnamed x6 -> x2, local copies, waits for them, and re-layouts: 1.88 us -> 0.01 us
  transfers between devices with their start and end apart: 11 -> 11, of which waited for: 5 -> 4; matrix products, arithmetic and copies ran while one was open for 4% -> 3% of each run, Pallas kernels for 6% -> 2%
where the time goes in v8:
time: 123 us; the launch traced here: 122 us
  blocking collectives  50.9 us (41%)
  starting transfers between devices  35.9 us (29%)
  waiting for transfers between devices  19.5 us (16%)
  Pallas kernels  8.95 us (7%)
  local copies, waits for them, and re-layouts  4.73 us (4%)
  other arithmetic  1.57 us (1%)
    all_to_all x1, blocking collectives, per_device(): column = lax.all_to_all(message, GA, 0, 0, tiled=True)  33.3 us
    all_to_all x1, blocking collectives, per_device(): stats = lax.all_to_all(stats, GB + GA, 0, 0, tiled=True)  17.6 us
    ppermute x1, waiting for transfers between devices, per_device(): far = lax.ppermute(kept, 'x1', SWAP)  12.2 us
    ppermute x3, starting transfers between devices, per_device(): soon += [lax.ppermute(piece, 'core', SWAP) for piece in soon]  8.57 us
    pallas_call x2, Pallas kernels, partial_logits(): pl.pallas_call(matmul_kernel, in_specs=[vmem] * (1 + len(pieces)), out_sp...  7.25 us
    ppermute x1, starting transfers between devices, per_device(): late = [far, lax.ppermute(far, 'core', SWAP)]  4.88 us
    ppermute x1, starting transfers between devices, per_device(): back = lax.ppermute(given, ('x1', 'x0'), [(i, i ^ 3) for i in range(4)])  4.63 us
    all_to_all x1, starting transfers between devices, per_device(): gathered = lax.all_to_all(copies, GB, 0, 0, tiled=True)  4.4 us
  transfers between devices with their start and end apart: 11, of which 4 were waited for; matrix products, arithmetic and copies ran while one was open for 3% of the time, Pallas kernels for 2%

profile of v8, /device:TPU:1, one launch (start us, length us, event | category | flops | bytes accessed | tf_op | source)
XLA Modules:
  0.0 122.4 jit_solution(3158432991480645461)
XLA Ops:
  0.6 0.7 shift-right-arithmetic_bitcast_fusion
  1.3 0.8 fusion.1
  2.1 0.1 select_convert_fusion
  2.2 3.9 %collective-permute-start = (bf16[2,3712]{1,0:T(2,128)(2,1)S(1)}, bf16[2,3712]{1,0:T(2,128)(2,1)S(1)}, u32[]{:S(2)}, u32[]{:S(2)}) collective-permute-start(bf16[2,3712]{1,0:T(2,128)(2,1)S(1)} %get-tuple-element.31), channel_id=1, source_target_pairs={{0,2},{2,0},{1,3},{3,1},{4,6},{6,4},{5,7},{7,5},{8,10},{10,8},{9,1... | collective-permute-start | bytes 44552 | tf_op jit(solution)/shard_map/ppermute | solution.py:133
  6.1 2.5 %constant_dynamic-slice_fusion = (bf16[128,3584]{1,0:T(8,128)(2,1)S(1)}, bf16[128,3584]{1,0:T(8,128)(2,1)}) fusion(bf16[128,7168]{1,0:T(8,128)(2,1)} %param.5, s32[]{:T(128)S(6)} %select_n.35, s32[]{:T(128)S(6)} %select_n.34), kind=kLoop, calls=%fused_computation.12 | loop fusion | bytes 3670024 | tf_op jit(solution)/shard_map/dynamic_slice | solution.py:135
  8.7 1.9 %collective-permute-start.1 = (bf16[128,3584]{1,0:T(8,128)(2,1)}, bf16[128,3584]{1,0:T(8,128)(2,1)S(1)}, u32[]{:S(2)}, u32[]{:S(2)}) collective-permute-start(bf16[128,3584]{1,0:T(8,128)(2,1)} %get-tuple-element.27), channel_id=1, source_target_pairs={{0,2},{2,0},{1,3},{3,1},{4,6},{6,4},{5,7},{7,5},{8,10},{10,8},{9,1... | collective-permute-start | bytes 2752520 | tf_op jit(solution)/shard_map/ppermute | solution.py:137
  10.6 4.6 %collective-permute-start.2 = (bf16[128,3584]{1,0:T(8,128)(2,1)}, bf16[128,3584]{1,0:T(8,128)(2,1)}, u32[]{:S(2)}, u32[]{:S(2)}) collective-permute-start(bf16[128,3584]{1,0:T(8,128)(2,1)} %get-tuple-element.27), channel_id=1, source_target_pairs={{0,6},{2,4},{4,2},{6,0},{1,7},{3,5},{5,3},{7,1},{8,14},{10,12},{12... | collective-permute-start | bytes 2752520 | tf_op jit(solution)/shard_map/ppermute | solution.py:138
  15.2 0.0 collective-permute-done
  15.3 0.2 broadcast_in_dim.30
  15.5 33.3 %all_to_all.15 = bf16[16,2,2,3712]{3,2,1,0:T(2,128)(2,1)S(1)} all-to-all(bf16[16,2,2,3712]{3,2,1,0:T(2,128)(2,1)S(1)} %broadcast_in_dim.30), channel_id=1, replica_groups=mesh['s1'=2,'s0'=2,'zh'=2,'y1'=4,'y0'=2,'x1'=2,'x0'=2,'core'=2] {'s1','z..., dimensions={0} | all-to-all | bytes 950272 | tf_op jit(solution)/shard_map/all_to_all | solution.py:141
  48.8 0.3 copy.6
  49.1 0.2 reshape.38
  49.3 0.0 collective-permute-done.1.refs_1_
  49.3 0.0 collective-permute-done.2.refs_2_
  49.3 1.4 %broadcast_in_dim.31 = bf16[4,64,3712]{2,1,0:T(8,128)(2,1)} broadcast(bf16[64,3712]{1,0:T(8,128)(2,1)S(1)} %reshape.38), dimensions={1,2} | broadcast | bytes 2375680 | tf_op jit(solution)/shard_map/broadcast_in_dim | solution.py:144
  50.7 4.4 %all-to-all-start.1 = ((bf16[4,64,3712]{2,1,0:T(8,128)(2,1)}), bf16[4,64,3712]{2,1,0:T(8,128)(2,1)}, u32[]{:S(2)}, u32[]{:S(2)}) async-start(bf16[4,64,3712]{2,1,0:T(8,128)(2,1)} %broadcast_in_dim.31), calls=%async_computation.1 | async-start | bytes 3801088 | tf_op jit(solution)/shard_map/all_to_all | solution.py:145
  55.1 2.4 %collective-permute-start.3 = (bf16[128,3584]{1,0:T(8,128)(2,1)S(1)}, bf16[128,3584]{1,0:T(8,128)(2,1)S(1)}, u32[]{:S(2)}, u32[]{:S(2)}) collective-permute-start(bf16[128,3584]{1,0:T(8,128)(2,1)S(1)} %get-tuple-element.26.refs_0_), channel_id=1, source_target_pairs={{0,4},{4,0},{1,5},{5,1},{2,6},{6,2},{3,7},{7,3},{8,12},{12,8},{9,1... | collective-permute-start | bytes 2752520 | tf_op jit(solution)/shard_map/ppermute | solution.py:147
  57.5 4.2 %collective-permute-start.4 = (bf16[128,3584]{1,0:T(8,128)(2,1)S(1)}, bf16[128,3584]{1,0:T(8,128)(2,1)}, u32[]{:S(2)}, u32[]{:S(2)}) collective-permute-start(bf16[128,3584]{1,0:T(8,128)(2,1)S(1)} %get-tuple-element.26.refs_0_), channel_id=1, source_target_pairs={{0,1},{1,0},{2,3},{3,2},{4,5},{5,4},{6,7},{7,6},{8,9},{9,8},{10,11... | collective-permute-start | bytes 2752520 | tf_op jit(solution)/shard_map/ppermute | solution.py:151
  61.8 1.9 %collective-permute-start.5 = (bf16[128,3584]{1,0:T(8,128)(2,1)S(1)}, bf16[128,3584]{1,0:T(8,128)(2,1)}, u32[]{:S(2)}, u32[]{:S(2)}) collective-permute-start(bf16[128,3584]{1,0:T(8,128)(2,1)S(1)} %collective-permute-done.1.refs_1_), channel_id=1, source_target_pairs={{0,1},{1,0},{2,3},{3,2},{4,5},{5,4},{6,7},{7,6},{8,9},{9,8},{10,11... | collective-permute-start | bytes 2752520 | tf_op jit(solution)/shard_map/ppermute | solution.py:151
  63.7 2.4 %collective-permute-start.6 = (bf16[128,3584]{1,0:T(8,128)(2,1)}, bf16[128,3584]{1,0:T(8,128)(2,1)}, u32[]{:S(2)}, u32[]{:S(2)}) collective-permute-start(bf16[128,3584]{1,0:T(8,128)(2,1)} %collective-permute-done.2.refs_2_), channel_id=1, source_target_pairs={{0,1},{1,0},{2,3},{3,2},{4,5},{5,4},{6,7},{7,6},{8,9},{9,8},{10,11... | collective-permute-start | bytes 2752520 | tf_op jit(solution)/shard_map/ppermute | solution.py:151
  66.1 12.2 %collective-permute-done.3.refs_0_ = bf16[128,3584]{1,0:T(8,128)(2,1)S(1)} collective-permute-done((bf16[128,3584]{1,0:T(8,128)(2,1)S(1)}, bf16[128,3584]{1,0:T(8,128)(2,1)S(1)}, u32[]{:S(2)}, u32[]{:S(2)}) %collective-permute-start.3) | collective-permute-done | bytes 917536 | tf_op jit(solution)/shard_map/ppermute | solution.py:147
  78.3 0.0 all-to-all-done.1
  78.3 0.0 collective-permute-done.4.refs_3_
  78.3 0.0 collective-permute-done.5.refs_4_
  78.3 0.0 collective-permute-done.6.refs_5_
  78.3 4.4 %shard_map.59 = (f32[6,128,128]{2,1,0:T(8,128)S(1)}, f32[6,128,128]{2,1,0:T(8,128)S(1)}, s32[1,128]{1,0:T(1,128)S(1)}) custom-call(bf16[4,2,32,3712]{3,2,1,0:T(8,128)(2,1)} %bitcast.15.h_ref, bf16[128,3584]{1,0:T(8,128)(2,1)S(1)} %get-tuple-element.26.refs_0_, bf16[128,3584]{1,0:T(8,128)(2,1)S(1)} %collective-permute-done.1.refs_1_, ...), custom_call_target="tpu_custom_call" | custom-call | tf_op jit(solution)/shard_map/pallas_call | solution.py:46
  82.7 4.9 %collective-permute-start.7 = (bf16[128,3584]{1,0:T(8,128)(2,1)S(1)}, bf16[128,3584]{1,0:T(8,128)(2,1)S(1)}, u32[]{:S(2)}, u32[]{:S(2)}) collective-permute-start(bf16[128,3584]{1,0:T(8,128)(2,1)S(1)} %collective-permute-done.3.refs_0_), channel_id=1, source_target_pairs={{0,1},{1,0},{2,3},{3,2},{4,5},{5,4},{6,7},{7,6},{8,9},{9,8},{10,11... | collective-permute-start | bytes 2752520 | tf_op jit(solution)/shard_map/ppermute | solution.py:155
  87.6 0.0 copy-start
  87.7 1.9 %collective-permute-start.8 = (f32[6,128,128]{2,1,0:T(8,128)S(1)}, f32[6,128,128]{2,1,0:T(8,128)S(1)}, u32[]{:S(2)}, u32[]{:S(2)}) collective-permute-start(f32[6,128,128]{2,1,0:T(8,128)S(1)} %get-tuple-element.23), channel_id=1, source_target_pairs={{0,2},{2,0},{1,3},{3,1},{4,6},{6,4},{5,7},{7,5},{8,10},{10,8},{9,1... | collective-permute-start | bytes 1179656 | tf_op jit(solution)/shard_map/ppermute | solution.py:153
  89.6 0.1 collective-permute-done.7.refs_1_
  89.7 2.8 %shard_map.60 = (f32[2,128,128]{2,1,0:T(8,128)S(1)}, f32[2,128,128]{2,1,0:T(8,128)S(1)}, s32[1,128]{1,0:T(1,128)}) custom-call(bf16[4,2,32,3712]{3,2,1,0:T(8,128)(2,1)} %bitcast.15.h_ref, bf16[128,3584]{1,0:T(8,128)(2,1)S(1)} %collective-permute-done.3.refs_0_, bf16[128,3584]{1,0:T(8,128)(2,1)S(1)} %collective-permute-done.7.refs_1_), custom_call_target="tpu_custom_call" | custom-call | tf_op jit(solution)/shard_map/pallas_call | solution.py:46
  92.5 3.2 %collective-permute-start.9 = (f32[2,128,128]{2,1,0:T(8,128)S(1)}, f32[2,128,128]{2,1,0:T(8,128)S(1)}, u32[]{:S(2)}, u32[]{:S(2)}) collective-permute-start(f32[2,128,128]{2,1,0:T(8,128)S(1)} %get-tuple-element.24), channel_id=1, source_target_pairs={{0,2},{2,0},{1,3},{3,1},{4,6},{6,4},{5,7},{7,5},{8,10},{10,8},{9,1... | collective-permute-start | bytes 393224 | tf_op jit(solution)/shard_map/ppermute | solution.py:157
  95.8 0.1 stack.44.first_ref
  95.9 4.4 %collective-permute-done.8.theirs_ref = f32[6,128,128]{2,1,0:T(8,128)S(1)} collective-permute-done((f32[6,128,128]{2,1,0:T(8,128)S(1)}, f32[6,128,128]{2,1,0:T(8,128)S(1)}, u32[]{:S(2)}, u32[]{:S(2)}) %collective-permute-start.8) | collective-permute-done | bytes 393248 | tf_op jit(solution)/shard_map/ppermute | solution.py:153
  100.3 2.8 %collective-permute-done.9.theirs_far_ref = f32[2,128,128]{2,1,0:T(8,128)S(1)} collective-permute-done((f32[2,128,128]{2,1,0:T(8,128)S(1)}, f32[2,128,128]{2,1,0:T(8,128)S(1)}, u32[]{:S(2)}, u32[]{:S(2)}) %collective-permute-start.9) | collective-permute-done | bytes 131104 | tf_op jit(solution)/shard_map/ppermute | solution.py:157
  103.1 0.9 shard_map.61
  104.0 17.6 %all_to_all.16.stats_ref = f32[64,2,8]{2,1,0:T(2,128)S(1)} all-to-all(f32[64,2,8]{2,1,0:T(2,128)S(1)} %bitcast.23), channel_id=1, replica_groups=mesh['s1'=2,'s0'=2,'zh'=2,'y1'=4,'y0'=2,'x1'=2,'x0'=2,'core'=2] {'s0','y..., dimensions={0} | all-to-all | bytes 8192 | tf_op jit(solution)/shard_map/all_to_all | solution.py:173
  121.6 0.0 copy-done
  121.6 0.8 shard_map.62
  (3 shorter events, 0.1 us)
Async XLA Ops:
  2.2 13.0 %collective-permute-start = (bf16[2,3712]{1,0:T(2,128)(2,1)S(1)}, bf16[2,3712]{1,0:T(2,128)(2,1)S(1)}, u32[]{:S(2)}, u32[]{:S(2)}) collective-permute-start(bf16[2,3712]{1,0:T(2,128)(2,1)S(1)} %get-tuple-element.31), channel_id=1, source_target_pairs={{0,2},{2,0},{1,3},{3,1},{4,6},{6,4},{5,7},{7,5},{8,10},{10,8},{9,1... | collective-permute-start | bytes 44552 | tf_op jit(solution)/shard_map/ppermute | solution.py:133
  8.7 40.7 %collective-permute-start.1 = (bf16[128,3584]{1,0:T(8,128)(2,1)}, bf16[128,3584]{1,0:T(8,128)(2,1)S(1)}, u32[]{:S(2)}, u32[]{:S(2)}) collective-permute-start(bf16[128,3584]{1,0:T(8,128)(2,1)} %get-tuple-element.27), channel_id=1, source_target_pairs={{0,2},{2,0},{1,3},{3,1},{4,6},{6,4},{5,7},{7,5},{8,10},{10,8},{9,1... | collective-permute-start | bytes 2752520 | tf_op jit(solution)/shard_map/ppermute | solution.py:137
  10.6 38.7 %collective-permute-start.2 = (bf16[128,3584]{1,0:T(8,128)(2,1)}, bf16[128,3584]{1,0:T(8,128)(2,1)}, u32[]{:S(2)}, u32[]{:S(2)}) collective-permute-start(bf16[128,3584]{1,0:T(8,128)(2,1)} %get-tuple-element.27), channel_id=1, source_target_pairs={{0,6},{2,4},{4,2},{6,0},{1,7},{3,5},{5,3},{7,1},{8,14},{10,12},{12... | collective-permute-start | bytes 2752520 | tf_op jit(solution)/shard_map/ppermute | solution.py:138
  50.7 27.6 %all-to-all-start.1 = ((bf16[4,64,3712]{2,1,0:T(8,128)(2,1)}), bf16[4,64,3712]{2,1,0:T(8,128)(2,1)}, u32[]{:S(2)}, u32[]{:S(2)}) async-start(bf16[4,64,3712]{2,1,0:T(8,128)(2,1)} %broadcast_in_dim.31), calls=%async_computation.1 | async-start | bytes 3801088 | tf_op jit(solution)/shard_map/all_to_all | solution.py:145
  55.1 23.2 %collective-permute-start.3 = (bf16[128,3584]{1,0:T(8,128)(2,1)S(1)}, bf16[128,3584]{1,0:T(8,128)(2,1)S(1)}, u32[]{:S(2)}, u32[]{:S(2)}) collective-permute-start(bf16[128,3584]{1,0:T(8,128)(2,1)S(1)} %get-tuple-element.26.refs_0_), channel_id=1, source_target_pairs={{0,4},{4,0},{1,5},{5,1},{2,6},{6,2},{3,7},{7,3},{8,12},{12,8},{9,1... | collective-permute-start | bytes 2752520 | tf_op jit(solution)/shard_map/ppermute | solution.py:147
  57.5 20.8 %collective-permute-start.4 = (bf16[128,3584]{1,0:T(8,128)(2,1)S(1)}, bf16[128,3584]{1,0:T(8,128)(2,1)}, u32[]{:S(2)}, u32[]{:S(2)}) collective-permute-start(bf16[128,3584]{1,0:T(8,128)(2,1)S(1)} %get-tuple-element.26.refs_0_), channel_id=1, source_target_pairs={{0,1},{1,0},{2,3},{3,2},{4,5},{5,4},{6,7},{7,6},{8,9},{9,8},{10,11... | collective-permute-start | bytes 2752520 | tf_op jit(solution)/shard_map/ppermute | solution.py:151
  61.8 16.5 %collective-permute-start.5 = (bf16[128,3584]{1,0:T(8,128)(2,1)S(1)}, bf16[128,3584]{1,0:T(8,128)(2,1)}, u32[]{:S(2)}, u32[]{:S(2)}) collective-permute-start(bf16[128,3584]{1,0:T(8,128)(2,1)S(1)} %collective-permute-done.1.refs_1_), channel_id=1, source_target_pairs={{0,1},{1,0},{2,3},{3,2},{4,5},{5,4},{6,7},{7,6},{8,9},{9,8},{10,11... | collective-permute-start | bytes 2752520 | tf_op jit(solution)/shard_map/ppermute | solution.py:151
  63.7 14.6 %collective-permute-start.6 = (bf16[128,3584]{1,0:T(8,128)(2,1)}, bf16[128,3584]{1,0:T(8,128)(2,1)}, u32[]{:S(2)}, u32[]{:S(2)}) collective-permute-start(bf16[128,3584]{1,0:T(8,128)(2,1)} %collective-permute-done.2.refs_2_), channel_id=1, source_target_pairs={{0,1},{1,0},{2,3},{3,2},{4,5},{5,4},{6,7},{7,6},{8,9},{9,8},{10,11... | collective-permute-start | bytes 2752520 | tf_op jit(solution)/shard_map/ppermute | solution.py:151
  82.7 7.0 %collective-permute-start.7 = (bf16[128,3584]{1,0:T(8,128)(2,1)S(1)}, bf16[128,3584]{1,0:T(8,128)(2,1)S(1)}, u32[]{:S(2)}, u32[]{:S(2)}) collective-permute-start(bf16[128,3584]{1,0:T(8,128)(2,1)S(1)} %collective-permute-done.3.refs_0_), channel_id=1, source_target_pairs={{0,1},{1,0},{2,3},{3,2},{4,5},{5,4},{6,7},{7,6},{8,9},{9,8},{10,11... | collective-permute-start | bytes 2752520 | tf_op jit(solution)/shard_map/ppermute | solution.py:155
  87.6 34.0 %copy-start = (f32[1,2]{1,0:T(1,128)S(1)}, f32[1,2]{1,0:T(1,128)}, u32[]{:S(2)}) copy-start(f32[1,2]{1,0:T(1,128)} %policy_ref.1) | copy-start | bytes 28
  87.7 12.6 %collective-permute-start.8 = (f32[6,128,128]{2,1,0:T(8,128)S(1)}, f32[6,128,128]{2,1,0:T(8,128)S(1)}, u32[]{:S(2)}, u32[]{:S(2)}) collective-permute-start(f32[6,128,128]{2,1,0:T(8,128)S(1)} %get-tuple-element.23), channel_id=1, source_target_pairs={{0,2},{2,0},{1,3},{3,1},{4,6},{6,4},{5,7},{7,5},{8,10},{10,8},{9,1... | collective-permute-start | bytes 1179656 | tf_op jit(solution)/shard_map/ppermute | solution.py:153
  92.5 10.5 %collective-permute-start.9 = (f32[2,128,128]{2,1,0:T(8,128)S(1)}, f32[2,128,128]{2,1,0:T(8,128)S(1)}, u32[]{:S(2)}, u32[]{:S(2)}) collective-permute-start(f32[2,128,128]{2,1,0:T(8,128)S(1)} %get-tuple-element.24), channel_id=1, source_target_pairs={{0,2},{2,0},{1,3},{3,1},{4,6},{6,4},{5,7},{7,5},{8,10},{10,8},{9,1... | collective-permute-start | bytes 393224 | tf_op jit(solution)/shard_map/ppermute | solution.py:157

commit v9 on v8

--- a/solution.py
+++ b/solution.py
@@ -124,12 +124,13 @@
     at = {a: lax.axis_index(a) for a in NAMES}
     k = at["x0"]
 
-    ids = target_ids.reshape(rows, 1)
     lane = lax.broadcasted_iota(jnp.int32, (rows, IDS), 1)
+    ids = jnp.broadcast_to(target_ids.reshape(rows, 1), (rows, IDS))
     code = jnp.where(lane == 0, ids >> 8, ids & 255).astype(hidden.dtype)
-    low, high = hidden[0, :, :depth], hidden[0, :, depth:]
-    own = jnp.concatenate([jnp.where(k == 0, low, high), code], axis=1)
-    other = jnp.concatenate([jnp.where(k == 0, high, low), code], axis=1)
+    own = lax.dynamic_slice_in_dim(hidden[0], k * depth, depth, 1)
+    other = lax.dynamic_slice_in_dim(hidden[0], (1 - k) * depth, depth, 1)
+    own = jnp.concatenate([own, code], axis=1)
+    other = jnp.concatenate([other, code], axis=1)
     other = lax.ppermute(other, "x0", SWAP)
 
     kept = lax.dynamic_slice_in_dim(head_weight, k * depth, depth, 1)
@@ -151,7 +152,6 @@
     soon += [lax.ppermute(piece, "core", SWAP) for piece in soon]
     mine, send, ids = partial_logits(gathered, soon)
     theirs = lax.ppermute(send, "x0", SWAP)
-    far, mine = lax.optimization_barrier((far, mine))
     late = [far, lax.ppermute(far, "core", SWAP)]
     mine_far, send_far, _ = partial_logits(gathered, late)
     theirs_far = lax.ppermute(send_far, "x0", SWAP)

time: 123 us -> 123 us (level)
  transfers between devices with their start and end apart: 11 -> 11, of which waited for: 4 -> 3; matrix products, arithmetic and copies ran while one was open for 3% -> 3% of each run, Pallas kernels for 2% -> 6%
where the time goes in v9:
time: 123 us; the launch traced here: 122 us
  blocking collectives  50.9 us (41%)
  starting transfers between devices  36 us (29%)
  waiting for transfers between devices  19.4 us (16%)
  Pallas kernels  8.95 us (7%)
  local copies, waits for them, and re-layouts  5.48 us (4%)
    all_to_all x1, blocking collectives, per_device(): column = lax.all_to_all(message, GA, 0, 0, tiled=True)  33.3 us
    all_to_all x1, blocking collectives, per_device(): stats = lax.all_to_all(stats, GB + GA, 0, 0, tiled=True)  17.6 us
    ppermute x1, waiting for transfers between devices, per_device(): far = lax.ppermute(kept, 'x1', SWAP)  12.2 us
    ppermute x3, starting transfers between devices, per_device(): soon += [lax.ppermute(piece, 'core', SWAP) for piece in soon]  8.57 us
    pallas_call x2, Pallas kernels, partial_logits(): pl.pallas_call(matmul_kernel, in_specs=[vmem] * (1 + len(pieces)), out_sp...  7.25 us
    ppermute x1, starting transfers between devices, per_device(): late = [far, lax.ppermute(far, 'core', SWAP)]  4.87 us
    ppermute x1, starting transfers between devices, per_device(): back = lax.ppermute(given, ('x1', 'x0'), [(i, i ^ 3) for i in range(4)])  4.63 us
    all_to_all x1, starting transfers between devices, per_device(): gathered = lax.all_to_all(copies, GB, 0, 0, tiled=True)  4.4 us
  transfers between devices with their start and end apart: 11, of which 3 were waited for; matrix products, arithmetic and copies ran while one was open for 3% of the time, Pallas kernels for 6%

profile of v9, /device:TPU:1, one launch (start us, length us, event | category | flops | bytes accessed | tf_op | source)
XLA Modules:
  0.0 122.4 jit_solution(17624187465582683378)
XLA Ops:
  0.6 0.7 shift-right-arithmetic_bitcast_fusion
  1.3 0.8 dynamic-slice_bitcast_fusion.1
  2.1 0.1 select_convert_fusion
  2.2 3.9 %collective-permute-start = (bf16[2,3712]{1,0:T(2,128)(2,1)S(1)}, bf16[2,3712]{1,0:T(2,128)(2,1)S(1)}, u32[]{:S(2)}, u32[]{:S(2)}) collective-permute-start(bf16[2,3712]{1,0:T(2,128)(2,1)S(1)} %get-tuple-element.27), channel_id=1, source_target_pairs={{0,2},{2,0},{1,3},{3,1},{4,6},{6,4},{5,7},{7,5},{8,10},{10,8},{9,1... | collective-permute-start | bytes 44552 | tf_op jit(solution)/shard_map/ppermute | solution.py:134
  6.1 2.5 %constant_dynamic-slice_fusion = (bf16[128,3584]{1,0:T(8,128)(2,1)S(1)}, bf16[128,3584]{1,0:T(8,128)(2,1)}) fusion(bf16[128,7168]{1,0:T(8,128)(2,1)} %param.5, s32[]{:T(128)S(6)} %select_n.12, s32[]{:T(128)S(6)} %select_n.14), kind=kLoop, calls=%fused_computation.7 | loop fusion | bytes 3670024 | tf_op jit(solution)/shard_map/dynamic_slice | solution.py:136
  8.6 1.9 %collective-permute-start.1 = (bf16[128,3584]{1,0:T(8,128)(2,1)}, bf16[128,3584]{1,0:T(8,128)(2,1)S(1)}, u32[]{:S(2)}, u32[]{:S(2)}) collective-permute-start(bf16[128,3584]{1,0:T(8,128)(2,1)} %get-tuple-element.23), channel_id=1, source_target_pairs={{0,2},{2,0},{1,3},{3,1},{4,6},{6,4},{5,7},{7,5},{8,10},{10,8},{9,1... | collective-permute-start | bytes 2752520 | tf_op jit(solution)/shard_map/ppermute | solution.py:138
  10.6 4.6 %collective-permute-start.2 = (bf16[128,3584]{1,0:T(8,128)(2,1)}, bf16[128,3584]{1,0:T(8,128)(2,1)}, u32[]{:S(2)}, u32[]{:S(2)}) collective-permute-start(bf16[128,3584]{1,0:T(8,128)(2,1)} %get-tuple-element.23), channel_id=1, source_target_pairs={{0,6},{2,4},{4,2},{6,0},{1,7},{3,5},{5,3},{7,1},{8,14},{10,12},{12... | collective-permute-start | bytes 2752520 | tf_op jit(solution)/shard_map/ppermute | solution.py:139
  15.2 0.0 collective-permute-done
  15.3 0.2 broadcast_in_dim.10
  15.5 33.3 %all_to_all.15 = bf16[16,2,2,3712]{3,2,1,0:T(2,128)(2,1)S(1)} all-to-all(bf16[16,2,2,3712]{3,2,1,0:T(2,128)(2,1)S(1)} %broadcast_in_dim.10), channel_id=1, replica_groups=mesh['s1'=2,'s0'=2,'zh'=2,'y1'=4,'y0'=2,'x1'=2,'x0'=2,'core'=2] {'s1','z..., dimensions={0} | all-to-all | bytes 950272 | tf_op jit(solution)/shard_map/all_to_all | solution.py:142
  48.8 0.3 copy.6
  49.1 0.2 reshape.23
  49.3 0.0 collective-permute-done.1.refs_1_
  49.3 0.0 collective-permute-done.2.refs_2_
  49.3 1.4 %broadcast_in_dim.22 = bf16[4,64,3712]{2,1,0:T(8,128)(2,1)} broadcast(bf16[64,3712]{1,0:T(8,128)(2,1)S(1)} %reshape.23), dimensions={1,2} | broadcast | bytes 2375680 | tf_op jit(solution)/shard_map/broadcast_in_dim | solution.py:145
  50.7 4.4 %all-to-all-start.1 = ((bf16[4,64,3712]{2,1,0:T(8,128)(2,1)}), bf16[4,64,3712]{2,1,0:T(8,128)(2,1)}, u32[]{:S(2)}, u32[]{:S(2)}) async-start(bf16[4,64,3712]{2,1,0:T(8,128)(2,1)} %broadcast_in_dim.22), calls=%async_computation.1 | async-start | bytes 3801088 | tf_op jit(solution)/shard_map/all_to_all | solution.py:146
  55.1 2.4 %collective-permute-start.3 = (bf16[128,3584]{1,0:T(8,128)(2,1)S(1)}, bf16[128,3584]{1,0:T(8,128)(2,1)S(1)}, u32[]{:S(2)}, u32[]{:S(2)}) collective-permute-start(bf16[128,3584]{1,0:T(8,128)(2,1)S(1)} %get-tuple-element.22.refs_0_), channel_id=1, source_target_pairs={{0,4},{4,0},{1,5},{5,1},{2,6},{6,2},{3,7},{7,3},{8,12},{12,8},{9,1... | collective-permute-start | bytes 2752520 | tf_op jit(solution)/shard_map/ppermute | solution.py:148
  57.5 4.2 %collective-permute-start.4 = (bf16[128,3584]{1,0:T(8,128)(2,1)S(1)}, bf16[128,3584]{1,0:T(8,128)(2,1)}, u32[]{:S(2)}, u32[]{:S(2)}) collective-permute-start(bf16[128,3584]{1,0:T(8,128)(2,1)S(1)} %get-tuple-element.22.refs_0_), channel_id=1, source_target_pairs={{0,1},{1,0},{2,3},{3,2},{4,5},{5,4},{6,7},{7,6},{8,9},{9,8},{10,11... | collective-permute-start | bytes 2752520 | tf_op jit(solution)/shard_map/ppermute | solution.py:152
  61.8 1.9 %collective-permute-start.5 = (bf16[128,3584]{1,0:T(8,128)(2,1)S(1)}, bf16[128,3584]{1,0:T(8,128)(2,1)}, u32[]{:S(2)}, u32[]{:S(2)}) collective-permute-start(bf16[128,3584]{1,0:T(8,128)(2,1)S(1)} %collective-permute-done.1.refs_1_), channel_id=1, source_target_pairs={{0,1},{1,0},{2,3},{3,2},{4,5},{5,4},{6,7},{7,6},{8,9},{9,8},{10,11... | collective-permute-start | bytes 2752520 | tf_op jit(solution)/shard_map/ppermute | solution.py:152
  63.7 2.4 %collective-permute-start.6 = (bf16[128,3584]{1,0:T(8,128)(2,1)}, bf16[128,3584]{1,0:T(8,128)(2,1)}, u32[]{:S(2)}, u32[]{:S(2)}) collective-permute-start(bf16[128,3584]{1,0:T(8,128)(2,1)} %collective-permute-done.2.refs_2_), channel_id=1, source_target_pairs={{0,1},{1,0},{2,3},{3,2},{4,5},{5,4},{6,7},{7,6},{8,9},{9,8},{10,11... | collective-permute-start | bytes 2752520 | tf_op jit(solution)/shard_map/ppermute | solution.py:152
  66.1 12.2 %collective-permute-done.3.refs_0_ = bf16[128,3584]{1,0:T(8,128)(2,1)S(1)} collective-permute-done((bf16[128,3584]{1,0:T(8,128)(2,1)S(1)}, bf16[128,3584]{1,0:T(8,128)(2,1)S(1)}, u32[]{:S(2)}, u32[]{:S(2)}) %collective-permute-start.3) | collective-permute-done | bytes 917536 | tf_op jit(solution)/shard_map/ppermute | solution.py:148
  78.3 0.0 all-to-all-done.1
  78.3 4.9 %collective-permute-start.7 = (bf16[128,3584]{1,0:T(8,128)(2,1)S(1)}, bf16[128,3584]{1,0:T(8,128)(2,1)S(1)}, u32[]{:S(2)}, u32[]{:S(2)}) collective-permute-start(bf16[128,3584]{1,0:T(8,128)(2,1)S(1)} %collective-permute-done.3.refs_0_), channel_id=1, source_target_pairs={{0,1},{1,0},{2,3},{3,2},{4,5},{5,4},{6,7},{7,6},{8,9},{9,8},{10,11... | collective-permute-start | bytes 2752520 | tf_op jit(solution)/shard_map/ppermute | solution.py:155
  83.2 0.0 collective-permute-done.4.refs_3_
  83.2 0.0 collective-permute-done.5.refs_4_
  83.2 0.0 collective-permute-done.6.refs_5_
  83.2 4.4 %shard_map.59 = (f32[6,128,128]{2,1,0:T(8,128)S(1)}, f32[6,128,128]{2,1,0:T(8,128)S(1)}, s32[1,128]{1,0:T(1,128)S(1)}) custom-call(bf16[4,2,32,3712]{3,2,1,0:T(8,128)(2,1)} %bitcast.15.h_ref, bf16[128,3584]{1,0:T(8,128)(2,1)S(1)} %get-tuple-element.22.refs_0_, bf16[128,3584]{1,0:T(8,128)(2,1)S(1)} %collective-permute-done.1.refs_1_, ...), custom_call_target="tpu_custom_call" | custom-call | tf_op jit(solution)/shard_map/pallas_call | solution.py:46
  87.6 0.0 copy-start
  87.6 1.9 %collective-permute-start.8 = (f32[6,128,128]{2,1,0:T(8,128)S(1)}, f32[6,128,128]{2,1,0:T(8,128)S(1)}, u32[]{:S(2)}, u32[]{:S(2)}) collective-permute-start(f32[6,128,128]{2,1,0:T(8,128)S(1)} %get-tuple-element.19), channel_id=1, source_target_pairs={{0,2},{2,0},{1,3},{3,1},{4,6},{6,4},{5,7},{7,5},{8,10},{10,8},{9,1... | collective-permute-start | bytes 1179656 | tf_op jit(solution)/shard_map/ppermute | solution.py:154
  89.6 0.0 collective-permute-done.7.refs_1_
  89.6 2.8 %shard_map.60 = (f32[2,128,128]{2,1,0:T(8,128)S(1)}, f32[2,128,128]{2,1,0:T(8,128)S(1)}, s32[1,128]{1,0:T(1,128)}) custom-call(bf16[4,2,32,3712]{3,2,1,0:T(8,128)(2,1)} %bitcast.15.h_ref, bf16[128,3584]{1,0:T(8,128)(2,1)S(1)} %collective-permute-done.3.refs_0_, bf16[128,3584]{1,0:T(8,128)(2,1)S(1)} %collective-permute-done.7.refs_1_), custom_call_target="tpu_custom_call" | custom-call | tf_op jit(solution)/shard_map/pallas_call | solution.py:46
  92.4 3.4 %collective-permute-start.9 = (f32[2,128,128]{2,1,0:T(8,128)S(1)}, f32[2,128,128]{2,1,0:T(8,128)S(1)}, u32[]{:S(2)}, u32[]{:S(2)}) collective-permute-start(f32[2,128,128]{2,1,0:T(8,128)S(1)} %get-tuple-element.20), channel_id=1, source_target_pairs={{0,2},{2,0},{1,3},{3,1},{4,6},{6,4},{5,7},{7,5},{8,10},{10,8},{9,1... | collective-permute-start | bytes 393224 | tf_op jit(solution)/shard_map/ppermute | solution.py:157
  95.8 0.1 stack.44.first_ref
  95.9 4.4 %collective-permute-done.8.theirs_ref = f32[6,128,128]{2,1,0:T(8,128)S(1)} collective-permute-done((f32[6,128,128]{2,1,0:T(8,128)S(1)}, f32[6,128,128]{2,1,0:T(8,128)S(1)}, u32[]{:S(2)}, u32[]{:S(2)}) %collective-permute-start.8) | collective-permute-done | bytes 393248 | tf_op jit(solution)/shard_map/ppermute | solution.py:154
  100.3 2.8 %collective-permute-done.9.theirs_far_ref = f32[2,128,128]{2,1,0:T(8,128)S(1)} collective-permute-done((f32[2,128,128]{2,1,0:T(8,128)S(1)}, f32[2,128,128]{2,1,0:T(8,128)S(1)}, u32[]{:S(2)}, u32[]{:S(2)}) %collective-permute-start.9) | collective-permute-done | bytes 131104 | tf_op jit(solution)/shard_map/ppermute | solution.py:157
  103.1 0.9 shard_map.61
  104.0 17.6 %all_to_all.16.stats_ref = f32[64,2,8]{2,1,0:T(2,128)S(1)} all-to-all(f32[64,2,8]{2,1,0:T(2,128)S(1)} %bitcast.23), channel_id=1, replica_groups=mesh['s1'=2,'s0'=2,'zh'=2,'y1'=4,'y0'=2,'x1'=2,'x0'=2,'core'=2] {'s0','y..., dimensions={0} | all-to-all | bytes 8192 | tf_op jit(solution)/shard_map/all_to_all | solution.py:173
  121.6 0.0 copy-done
  121.6 0.8 shard_map.62
  (3 shorter events, 0.1 us)
Async XLA Ops:
  2.2 13.0 %collective-permute-start = (bf16[2,3712]{1,0:T(2,128)(2,1)S(1)}, bf16[2,3712]{1,0:T(2,128)(2,1)S(1)}, u32[]{:S(2)}, u32[]{:S(2)}) collective-permute-start(bf16[2,3712]{1,0:T(2,128)(2,1)S(1)} %get-tuple-element.27), channel_id=1, source_target_pairs={{0,2},{2,0},{1,3},{3,1},{4,6},{6,4},{5,7},{7,5},{8,10},{10,8},{9,1... | collective-permute-start | bytes 44552 | tf_op jit(solution)/shard_map/ppermute | solution.py:134
  8.6 40.7 %collective-permute-start.1 = (bf16[128,3584]{1,0:T(8,128)(2,1)}, bf16[128,3584]{1,0:T(8,128)(2,1)S(1)}, u32[]{:S(2)}, u32[]{:S(2)}) collective-permute-start(bf16[128,3584]{1,0:T(8,128)(2,1)} %get-tuple-element.23), channel_id=1, source_target_pairs={{0,2},{2,0},{1,3},{3,1},{4,6},{6,4},{5,7},{7,5},{8,10},{10,8},{9,1... | collective-permute-start | bytes 2752520 | tf_op jit(solution)/shard_map/ppermute | solution.py:138
  10.6 38.7 %collective-permute-start.2 = (bf16[128,3584]{1,0:T(8,128)(2,1)}, bf16[128,3584]{1,0:T(8,128)(2,1)}, u32[]{:S(2)}, u32[]{:S(2)}) collective-permute-start(bf16[128,3584]{1,0:T(8,128)(2,1)} %get-tuple-element.23), channel_id=1, source_target_pairs={{0,6},{2,4},{4,2},{6,0},{1,7},{3,5},{5,3},{7,1},{8,14},{10,12},{12... | collective-permute-start | bytes 2752520 | tf_op jit(solution)/shard_map/ppermute | solution.py:139
  50.7 27.6 %all-to-all-start.1 = ((bf16[4,64,3712]{2,1,0:T(8,128)(2,1)}), bf16[4,64,3712]{2,1,0:T(8,128)(2,1)}, u32[]{:S(2)}, u32[]{:S(2)}) async-start(bf16[4,64,3712]{2,1,0:T(8,128)(2,1)} %broadcast_in_dim.22), calls=%async_computation.1 | async-start | bytes 3801088 | tf_op jit(solution)/shard_map/all_to_all | solution.py:146
  55.1 23.2 %collective-permute-start.3 = (bf16[128,3584]{1,0:T(8,128)(2,1)S(1)}, bf16[128,3584]{1,0:T(8,128)(2,1)S(1)}, u32[]{:S(2)}, u32[]{:S(2)}) collective-permute-start(bf16[128,3584]{1,0:T(8,128)(2,1)S(1)} %get-tuple-element.22.refs_0_), channel_id=1, source_target_pairs={{0,4},{4,0},{1,5},{5,1},{2,6},{6,2},{3,7},{7,3},{8,12},{12,8},{9,1... | collective-permute-start | bytes 2752520 | tf_op jit(solution)/shard_map/ppermute | solution.py:148
  57.5 25.6 %collective-permute-start.4 = (bf16[128,3584]{1,0:T(8,128)(2,1)S(1)}, bf16[128,3584]{1,0:T(8,128)(2,1)}, u32[]{:S(2)}, u32[]{:S(2)}) collective-permute-start(bf16[128,3584]{1,0:T(8,128)(2,1)S(1)} %get-tuple-element.22.refs_0_), channel_id=1, source_target_pairs={{0,1},{1,0},{2,3},{3,2},{4,5},{5,4},{6,7},{7,6},{8,9},{9,8},{10,11... | collective-permute-start | bytes 2752520 | tf_op jit(solution)/shard_map/ppermute | solution.py:152
  61.8 21.4 %collective-permute-start.5 = (bf16[128,3584]{1,0:T(8,128)(2,1)S(1)}, bf16[128,3584]{1,0:T(8,128)(2,1)}, u32[]{:S(2)}, u32[]{:S(2)}) collective-permute-start(bf16[128,3584]{1,0:T(8,128)(2,1)S(1)} %collective-permute-done.1.refs_1_), channel_id=1, source_target_pairs={{0,1},{1,0},{2,3},{3,2},{4,5},{5,4},{6,7},{7,6},{8,9},{9,8},{10,11... | collective-permute-start | bytes 2752520 | tf_op jit(solution)/shard_map/ppermute | solution.py:152
  63.7 19.5 %collective-permute-start.6 = (bf16[128,3584]{1,0:T(8,128)(2,1)}, bf16[128,3584]{1,0:T(8,128)(2,1)}, u32[]{:S(2)}, u32[]{:S(2)}) collective-permute-start(bf16[128,3584]{1,0:T(8,128)(2,1)} %collective-permute-done.2.refs_2_), channel_id=1, source_target_pairs={{0,1},{1,0},{2,3},{3,2},{4,5},{5,4},{6,7},{7,6},{8,9},{9,8},{10,11... | collective-permute-start | bytes 2752520 | tf_op jit(solution)/shard_map/ppermute | solution.py:152
  78.3 11.3 %collective-permute-start.7 = (bf16[128,3584]{1,0:T(8,128)(2,1)S(1)}, bf16[128,3584]{1,0:T(8,128)(2,1)S(1)}, u32[]{:S(2)}, u32[]{:S(2)}) collective-permute-start(bf16[128,3584]{1,0:T(8,128)(2,1)S(1)} %collective-permute-done.3.refs_0_), channel_id=1, source_target_pairs={{0,1},{1,0},{2,3},{3,2},{4,5},{5,4},{6,7},{7,6},{8,9},{9,8},{10,11... | collective-permute-start | bytes 2752520 | tf_op jit(solution)/shard_map/ppermute | solution.py:155
  87.6 34.0 %copy-start = (f32[1,2]{1,0:T(1,128)S(1)}, f32[1,2]{1,0:T(1,128)}, u32[]{:S(2)}) copy-start(f32[1,2]{1,0:T(1,128)} %policy_ref.1) | copy-start | bytes 28
  87.6 12.6 %collective-permute-start.8 = (f32[6,128,128]{2,1,0:T(8,128)S(1)}, f32[6,128,128]{2,1,0:T(8,128)S(1)}, u32[]{:S(2)}, u32[]{:S(2)}) collective-permute-start(f32[6,128,128]{2,1,0:T(8,128)S(1)} %get-tuple-element.19), channel_id=1, source_target_pairs={{0,2},{2,0},{1,3},{3,1},{4,6},{6,4},{5,7},{7,5},{8,10},{10,8},{9,1... | collective-permute-start | bytes 1179656 | tf_op jit(solution)/shard_map/ppermute | solution.py:154
  92.4 10.7 %collective-permute-start.9 = (f32[2,128,128]{2,1,0:T(8,128)S(1)}, f32[2,128,128]{2,1,0:T(8,128)S(1)}, u32[]{:S(2)}, u32[]{:S(2)}) collective-permute-start(f32[2,128,128]{2,1,0:T(8,128)S(1)} %get-tuple-element.20), channel_id=1, source_target_pairs={{0,2},{2,0},{1,3},{3,1},{4,6},{6,4},{5,7},{7,5},{8,10},{10,8},{9,1... | collective-permute-start | bytes 393224 | tf_op jit(solution)/shard_map/ppermute | solution.py:157

commit v10 on v8

--- a/solution.py
+++ b/solution.py
@@ -49,6 +49,36 @@
         out_specs=[vmem] * 3,
         out_shape=[block, block, jax.ShapeDtypeStruct((1, nb * rows), jnp.int32)],
         scratch_shapes=[pltpu.VMEM((depth, 2 * nb * rows), gathered.dtype)],
+        compiler_params=pltpu.CompilerParams(vmem_limit_bytes=51 * 1024 * 1024),
+    )(gathered, *pieces)
+
+
+def far_kernel(h_ref, first_ref, second_ref, keep_ref, send_ref):
+    voc, depth = first_ref.shape
+    wide = h_ref.shape[-1]
+    rows = [h_ref[:, i].reshape(-1, wide)[:, :depth] for i in range(2)]
+    half = rows[0].shape[0]
+    weights = jnp.concatenate([first_ref[...], second_ref[...]], axis=0)
+    out = lax.dot_general(
+        jnp.concatenate(rows, axis=0),
+        weights,
+        (((1,), (1,)), ((), ())),
+        preferred_element_type=jnp.float32,
+    ).T
+    for j in range(2):
+        keep_ref[j] = out[j * voc : (j + 1) * voc, :half]
+        send_ref[j] = out[j * voc : (j + 1) * voc, half:]
+
+
+def far_logits(gathered, pieces):
+    nb, _, rows, _ = gathered.shape
+    block = jax.ShapeDtypeStruct((2, pieces[0].shape[0], nb * rows), jnp.float32)
+    vmem = pl.BlockSpec(memory_space=pltpu.VMEM)
+    return pl.pallas_call(
+        far_kernel,
+        in_specs=[vmem] * 3,
+        out_specs=[vmem] * 2,
+        out_shape=[block, block],
         compiler_params=pltpu.CompilerParams(vmem_limit_bytes=51 * 1024 * 1024),
     )(gathered, *pieces)
 
@@ -153,7 +183,7 @@
     theirs = lax.ppermute(send, "x0", SWAP)
     far, mine = lax.optimization_barrier((far, mine))
     late = [far, lax.ppermute(far, "core", SWAP)]
-    mine_far, send_far, _ = partial_logits(gathered, late)
+    mine_far, send_far = far_logits(gathered, late)
     theirs_far = lax.ppermute(send_far, "x0", SWAP)
 
     firsts = []

time: 123 us -> 123 us (level)
    pallas_call x2 -> x1, Pallas kernels: 7.25 us -> 4.42 us  [partial_logits(): pl.pallas_call(matmul_kernel, in_specs=[vmem] * (1 + len(pieces)), out_sp...]
    pallas_call x0 -> x1, Pallas kernels: none -> 2.25 us  [far_logits(): pl.pallas_call(far_kernel, in_specs=[vmem] * 3, out_specs=[vmem] * 2, out...]
where the time goes in v10:
time: 123 us; the launch traced here: 122 us
  blocking collectives  50.9 us (41%)
  starting transfers between devices  35.9 us (29%)
  waiting for transfers between devices  20.1 us (16%)
  Pallas kernels  8.37 us (7%)
  local copies, waits for them, and re-layouts  4.73 us (4%)
  other arithmetic  1.57 us (1%)
    all_to_all x1, blocking collectives, per_device(): column = lax.all_to_all(message, GA, 0, 0, tiled=True)  33.3 us
    all_to_all x1, blocking collectives, per_device(): stats = lax.all_to_all(stats, GB + GA, 0, 0, tiled=True)  17.6 us
    ppermute x1, waiting for transfers between devices, per_device(): far = lax.ppermute(kept, 'x1', SWAP)  12.2 us
    ppermute x3, starting transfers between devices, per_device(): soon += [lax.ppermute(piece, 'core', SWAP) for piece in soon]  8.57 us
    ppermute x1, waiting for transfers between devices, per_device(): theirs = lax.ppermute(send, 'x0', SWAP)  4.93 us
    ppermute x1, starting transfers between devices, per_device(): late = [far, lax.ppermute(far, 'core', SWAP)]  4.88 us
    ppermute x1, starting transfers between devices, per_device(): back = lax.ppermute(given, ('x1', 'x0'), [(i, i ^ 3) for i in range(4)])  4.63 us
    pallas_call x1, Pallas kernels, partial_logits(): pl.pallas_call(matmul_kernel, in_specs=[vmem] * (1 + len(pieces)), out_sp...  4.42 us
  transfers between devices with their start and end apart: 11, of which 4 were waited for; matrix products, arithmetic and copies ran while one was open for 3% of the time, Pallas kernels for 2%

profile of v10, /device:TPU:1, one launch (start us, length us, event | category | flops | bytes accessed | tf_op | source)
XLA Modules:
  0.0 122.4 jit_solution(692404922957885291)
XLA Ops:
  0.6 0.7 shift-right-arithmetic_bitcast_fusion
  1.3 0.8 fusion.1
  2.1 0.1 select_convert_fusion
  2.2 3.9 %collective-permute-start = (bf16[2,3712]{1,0:T(2,128)(2,1)S(1)}, bf16[2,3712]{1,0:T(2,128)(2,1)S(1)}, u32[]{:S(2)}, u32[]{:S(2)}) collective-permute-start(bf16[2,3712]{1,0:T(2,128)(2,1)S(1)} %get-tuple-element.31), channel_id=1, source_target_pairs={{0,2},{2,0},{1,3},{3,1},{4,6},{6,4},{5,7},{7,5},{8,10},{10,8},{9,1... | collective-permute-start | bytes 44552 | tf_op jit(solution)/shard_map/ppermute | solution.py:163
  6.1 2.5 %constant_dynamic-slice_fusion = (bf16[128,3584]{1,0:T(8,128)(2,1)S(1)}, bf16[128,3584]{1,0:T(8,128)(2,1)}) fusion(bf16[128,7168]{1,0:T(8,128)(2,1)} %param.5, s32[]{:T(128)S(6)} %select_n.35, s32[]{:T(128)S(6)} %select_n.34), kind=kLoop, calls=%fused_computation.12 | loop fusion | bytes 3670024 | tf_op jit(solution)/shard_map/dynamic_slice | solution.py:165
  8.7 1.9 %collective-permute-start.1 = (bf16[128,3584]{1,0:T(8,128)(2,1)}, bf16[128,3584]{1,0:T(8,128)(2,1)S(1)}, u32[]{:S(2)}, u32[]{:S(2)}) collective-permute-start(bf16[128,3584]{1,0:T(8,128)(2,1)} %get-tuple-element.27), channel_id=1, source_target_pairs={{0,2},{2,0},{1,3},{3,1},{4,6},{6,4},{5,7},{7,5},{8,10},{10,8},{9,1... | collective-permute-start | bytes 2752520 | tf_op jit(solution)/shard_map/ppermute | solution.py:167
  10.6 4.6 %collective-permute-start.2 = (bf16[128,3584]{1,0:T(8,128)(2,1)}, bf16[128,3584]{1,0:T(8,128)(2,1)}, u32[]{:S(2)}, u32[]{:S(2)}) collective-permute-start(bf16[128,3584]{1,0:T(8,128)(2,1)} %get-tuple-element.27), channel_id=1, source_target_pairs={{0,6},{2,4},{4,2},{6,0},{1,7},{3,5},{5,3},{7,1},{8,14},{10,12},{12... | collective-permute-start | bytes 2752520 | tf_op jit(solution)/shard_map/ppermute | solution.py:168
  15.2 0.0 collective-permute-done
  15.3 0.2 broadcast_in_dim.30
  15.5 33.3 %all_to_all.15 = bf16[16,2,2,3712]{3,2,1,0:T(2,128)(2,1)S(1)} all-to-all(bf16[16,2,2,3712]{3,2,1,0:T(2,128)(2,1)S(1)} %broadcast_in_dim.30), channel_id=1, replica_groups=mesh['s1'=2,'s0'=2,'zh'=2,'y1'=4,'y0'=2,'x1'=2,'x0'=2,'core'=2] {'s1','z..., dimensions={0} | all-to-all | bytes 950272 | tf_op jit(solution)/shard_map/all_to_all | solution.py:171
  48.8 0.3 copy.6
  49.1 0.2 reshape.38
  49.3 0.0 collective-permute-done.1.refs_1_
  49.3 0.0 collective-permute-done.2.refs_2_
  49.3 1.4 %broadcast_in_dim.31 = bf16[4,64,3712]{2,1,0:T(8,128)(2,1)} broadcast(bf16[64,3712]{1,0:T(8,128)(2,1)S(1)} %reshape.38), dimensions={1,2} | broadcast | bytes 2375680 | tf_op jit(solution)/shard_map/broadcast_in_dim | solution.py:174
  50.7 4.4 %all-to-all-start.1 = ((bf16[4,64,3712]{2,1,0:T(8,128)(2,1)}), bf16[4,64,3712]{2,1,0:T(8,128)(2,1)}, u32[]{:S(2)}, u32[]{:S(2)}) async-start(bf16[4,64,3712]{2,1,0:T(8,128)(2,1)} %broadcast_in_dim.31), calls=%async_computation.1 | async-start | bytes 3801088 | tf_op jit(solution)/shard_map/all_to_all | solution.py:175
  55.1 2.4 %collective-permute-start.3 = (bf16[128,3584]{1,0:T(8,128)(2,1)S(1)}, bf16[128,3584]{1,0:T(8,128)(2,1)S(1)}, u32[]{:S(2)}, u32[]{:S(2)}) collective-permute-start(bf16[128,3584]{1,0:T(8,128)(2,1)S(1)} %get-tuple-element.26.refs_0_), channel_id=1, source_target_pairs={{0,4},{4,0},{1,5},{5,1},{2,6},{6,2},{3,7},{7,3},{8,12},{12,8},{9,1... | collective-permute-start | bytes 2752520 | tf_op jit(solution)/shard_map/ppermute | solution.py:177
  57.5 4.2 %collective-permute-start.4 = (bf16[128,3584]{1,0:T(8,128)(2,1)S(1)}, bf16[128,3584]{1,0:T(8,128)(2,1)}, u32[]{:S(2)}, u32[]{:S(2)}) collective-permute-start(bf16[128,3584]{1,0:T(8,128)(2,1)S(1)} %get-tuple-element.26.refs_0_), channel_id=1, source_target_pairs={{0,1},{1,0},{2,3},{3,2},{4,5},{5,4},{6,7},{7,6},{8,9},{9,8},{10,11... | collective-permute-start | bytes 2752520 | tf_op jit(solution)/shard_map/ppermute | solution.py:181
  61.8 1.9 %collective-permute-start.5 = (bf16[128,3584]{1,0:T(8,128)(2,1)S(1)}, bf16[128,3584]{1,0:T(8,128)(2,1)}, u32[]{:S(2)}, u32[]{:S(2)}) collective-permute-start(bf16[128,3584]{1,0:T(8,128)(2,1)S(1)} %collective-permute-done.1.refs_1_), channel_id=1, source_target_pairs={{0,1},{1,0},{2,3},{3,2},{4,5},{5,4},{6,7},{7,6},{8,9},{9,8},{10,11... | collective-permute-start | bytes 2752520 | tf_op jit(solution)/shard_map/ppermute | solution.py:181
  63.7 2.4 %collective-permute-start.6 = (bf16[128,3584]{1,0:T(8,128)(2,1)}, bf16[128,3584]{1,0:T(8,128)(2,1)}, u32[]{:S(2)}, u32[]{:S(2)}) collective-permute-start(bf16[128,3584]{1,0:T(8,128)(2,1)} %collective-permute-done.2.refs_2_), channel_id=1, source_target_pairs={{0,1},{1,0},{2,3},{3,2},{4,5},{5,4},{6,7},{7,6},{8,9},{9,8},{10,11... | collective-permute-start | bytes 2752520 | tf_op jit(solution)/shard_map/ppermute | solution.py:181
  66.1 12.2 %collective-permute-done.3.first_ref = bf16[128,3584]{1,0:T(8,128)(2,1)S(1)} collective-permute-done((bf16[128,3584]{1,0:T(8,128)(2,1)S(1)}, bf16[128,3584]{1,0:T(8,128)(2,1)S(1)}, u32[]{:S(2)}, u32[]{:S(2)}) %collective-permute-start.3) | collective-permute-done | bytes 917536 | tf_op jit(solution)/shard_map/ppermute | solution.py:177
  78.3 0.0 all-to-all-done.1
  78.3 0.0 collective-permute-done.4.refs_3_
  78.3 0.0 collective-permute-done.5.refs_4_
  78.3 0.0 collective-permute-done.6.refs_5_
  78.3 4.4 %shard_map.59 = (f32[6,128,128]{2,1,0:T(8,128)S(1)}, f32[6,128,128]{2,1,0:T(8,128)S(1)}, s32[1,128]{1,0:T(1,128)S(1)}) custom-call(bf16[4,2,32,3712]{3,2,1,0:T(8,128)(2,1)} %bitcast.15.h_ref, bf16[128,3584]{1,0:T(8,128)(2,1)S(1)} %get-tuple-element.26.refs_0_, bf16[128,3584]{1,0:T(8,128)(2,1)S(1)} %collective-permute-done.1.refs_1_, ...), custom_call_target="tpu_custom_call" | custom-call | tf_op jit(solution)/shard_map/pallas_call | solution.py:46
  82.7 4.9 %collective-permute-start.7 = (bf16[128,3584]{1,0:T(8,128)(2,1)S(1)}, bf16[128,3584]{1,0:T(8,128)(2,1)S(1)}, u32[]{:S(2)}, u32[]{:S(2)}) collective-permute-start(bf16[128,3584]{1,0:T(8,128)(2,1)S(1)} %collective-permute-done.3.first_ref), channel_id=1, source_target_pairs={{0,1},{1,0},{2,3},{3,2},{4,5},{5,4},{6,7},{7,6},{8,9},{9,8},{10,11... | collective-permute-start | bytes 2752520 | tf_op jit(solution)/shard_map/ppermute | solution.py:185
  87.6 0.0 copy-start
  87.7 1.9 %collective-permute-start.8 = (f32[6,128,128]{2,1,0:T(8,128)S(1)}, f32[6,128,128]{2,1,0:T(8,128)S(1)}, u32[]{:S(2)}, u32[]{:S(2)}) collective-permute-start(f32[6,128,128]{2,1,0:T(8,128)S(1)} %get-tuple-element.23), channel_id=1, source_target_pairs={{0,2},{2,0},{1,3},{3,1},{4,6},{6,4},{5,7},{7,5},{8,10},{10,8},{9,1... | collective-permute-start | bytes 1179656 | tf_op jit(solution)/shard_map/ppermute | solution.py:183
  89.6 0.1 collective-permute-done.7.second_ref
  89.7 2.2 %shard_map.60 = (f32[2,128,128]{2,1,0:T(8,128)S(1)}, f32[2,128,128]{2,1,0:T(8,128)S(1)}) custom-call(bf16[4,2,32,3712]{3,2,1,0:T(8,128)(2,1)} %bitcast.15.h_ref, bf16[128,3584]{1,0:T(8,128)(2,1)S(1)} %collective-permute-done.3.first_ref, bf16[128,3584]{1,0:T(8,128)(2,1)S(1)} %collective-permute-done.7.second_ref), custom_call_target="tpu_custom_call" | custom-call | tf_op jit(solution)/shard_map/pallas_call | solution.py:77
  92.0 3.2 %collective-permute-start.9 = (f32[2,128,128]{2,1,0:T(8,128)S(1)}, f32[2,128,128]{2,1,0:T(8,128)S(1)}, u32[]{:S(2)}, u32[]{:S(2)}) collective-permute-start(f32[2,128,128]{2,1,0:T(8,128)S(1)} %get-tuple-element.24), channel_id=1, source_target_pairs={{0,2},{2,0},{1,3},{3,1},{4,6},{6,4},{5,7},{7,5},{8,10},{10,8},{9,1... | collective-permute-start | bytes 393224 | tf_op jit(solution)/shard_map/ppermute | solution.py:187
  95.3 0.1 stack.44.first_ref
  95.3 4.9 %collective-permute-done.8.theirs_ref = f32[6,128,128]{2,1,0:T(8,128)S(1)} collective-permute-done((f32[6,128,128]{2,1,0:T(8,128)S(1)}, f32[6,128,128]{2,1,0:T(8,128)S(1)}, u32[]{:S(2)}, u32[]{:S(2)}) %collective-permute-start.8) | collective-permute-done | bytes 393248 | tf_op jit(solution)/shard_map/ppermute | solution.py:183
  100.3 2.8 %collective-permute-done.9.theirs_far_ref = f32[2,128,128]{2,1,0:T(8,128)S(1)} collective-permute-done((f32[2,128,128]{2,1,0:T(8,128)S(1)}, f32[2,128,128]{2,1,0:T(8,128)S(1)}, u32[]{:S(2)}, u32[]{:S(2)}) %collective-permute-start.9) | collective-permute-done | bytes 131104 | tf_op jit(solution)/shard_map/ppermute | solution.py:187
  103.1 0.9 shard_map.61
  104.0 17.6 %all_to_all.16.stats_ref = f32[64,2,8]{2,1,0:T(2,128)S(1)} all-to-all(f32[64,2,8]{2,1,0:T(2,128)S(1)} %bitcast.23), channel_id=1, replica_groups=mesh['s1'=2,'s0'=2,'zh'=2,'y1'=4,'y0'=2,'x1'=2,'x0'=2,'core'=2] {'s0','y..., dimensions={0} | all-to-all | bytes 8192 | tf_op jit(solution)/shard_map/all_to_all | solution.py:203
  121.6 0.0 copy-done
  121.6 0.8 shard_map.62
  (3 shorter events, 0.1 us)
Async XLA Ops:
  2.2 13.0 %collective-permute-start = (bf16[2,3712]{1,0:T(2,128)(2,1)S(1)}, bf16[2,3712]{1,0:T(2,128)(2,1)S(1)}, u32[]{:S(2)}, u32[]{:S(2)}) collective-permute-start(bf16[2,3712]{1,0:T(2,128)(2,1)S(1)} %get-tuple-element.31), channel_id=1, source_target_pairs={{0,2},{2,0},{1,3},{3,1},{4,6},{6,4},{5,7},{7,5},{8,10},{10,8},{9,1... | collective-permute-start | bytes 44552 | tf_op jit(solution)/shard_map/ppermute | solution.py:163
  8.7 40.7 %collective-permute-start.1 = (bf16[128,3584]{1,0:T(8,128)(2,1)}, bf16[128,3584]{1,0:T(8,128)(2,1)S(1)}, u32[]{:S(2)}, u32[]{:S(2)}) collective-permute-start(bf16[128,3584]{1,0:T(8,128)(2,1)} %get-tuple-element.27), channel_id=1, source_target_pairs={{0,2},{2,0},{1,3},{3,1},{4,6},{6,4},{5,7},{7,5},{8,10},{10,8},{9,1... | collective-permute-start | bytes 2752520 | tf_op jit(solution)/shard_map/ppermute | solution.py:167
  10.6 38.7 %collective-permute-start.2 = (bf16[128,3584]{1,0:T(8,128)(2,1)}, bf16[128,3584]{1,0:T(8,128)(2,1)}, u32[]{:S(2)}, u32[]{:S(2)}) collective-permute-start(bf16[128,3584]{1,0:T(8,128)(2,1)} %get-tuple-element.27), channel_id=1, source_target_pairs={{0,6},{2,4},{4,2},{6,0},{1,7},{3,5},{5,3},{7,1},{8,14},{10,12},{12... | collective-permute-start | bytes 2752520 | tf_op jit(solution)/shard_map/ppermute | solution.py:168
  50.7 27.6 %all-to-all-start.1 = ((bf16[4,64,3712]{2,1,0:T(8,128)(2,1)}), bf16[4,64,3712]{2,1,0:T(8,128)(2,1)}, u32[]{:S(2)}, u32[]{:S(2)}) async-start(bf16[4,64,3712]{2,1,0:T(8,128)(2,1)} %broadcast_in_dim.31), calls=%async_computation.1 | async-start | bytes 3801088 | tf_op jit(solution)/shard_map/all_to_all | solution.py:175
  55.1 23.2 %collective-permute-start.3 = (bf16[128,3584]{1,0:T(8,128)(2,1)S(1)}, bf16[128,3584]{1,0:T(8,128)(2,1)S(1)}, u32[]{:S(2)}, u32[]{:S(2)}) collective-permute-start(bf16[128,3584]{1,0:T(8,128)(2,1)S(1)} %get-tuple-element.26.refs_0_), channel_id=1, source_target_pairs={{0,4},{4,0},{1,5},{5,1},{2,6},{6,2},{3,7},{7,3},{8,12},{12,8},{9,1... | collective-permute-start | bytes 2752520 | tf_op jit(solution)/shard_map/ppermute | solution.py:177
  57.5 20.8 %collective-permute-start.4 = (bf16[128,3584]{1,0:T(8,128)(2,1)S(1)}, bf16[128,3584]{1,0:T(8,128)(2,1)}, u32[]{:S(2)}, u32[]{:S(2)}) collective-permute-start(bf16[128,3584]{1,0:T(8,128)(2,1)S(1)} %get-tuple-element.26.refs_0_), channel_id=1, source_target_pairs={{0,1},{1,0},{2,3},{3,2},{4,5},{5,4},{6,7},{7,6},{8,9},{9,8},{10,11... | collective-permute-start | bytes 2752520 | tf_op jit(solution)/shard_map/ppermute | solution.py:181
  61.8 16.5 %collective-permute-start.5 = (bf16[128,3584]{1,0:T(8,128)(2,1)S(1)}, bf16[128,3584]{1,0:T(8,128)(2,1)}, u32[]{:S(2)}, u32[]{:S(2)}) collective-permute-start(bf16[128,3584]{1,0:T(8,128)(2,1)S(1)} %collective-permute-done.1.refs_1_), channel_id=1, source_target_pairs={{0,1},{1,0},{2,3},{3,2},{4,5},{5,4},{6,7},{7,6},{8,9},{9,8},{10,11... | collective-permute-start | bytes 2752520 | tf_op jit(solution)/shard_map/ppermute | solution.py:181
  63.7 14.6 %collective-permute-start.6 = (bf16[128,3584]{1,0:T(8,128)(2,1)}, bf16[128,3584]{1,0:T(8,128)(2,1)}, u32[]{:S(2)}, u32[]{:S(2)}) collective-permute-start(bf16[128,3584]{1,0:T(8,128)(2,1)} %collective-permute-done.2.refs_2_), channel_id=1, source_target_pairs={{0,1},{1,0},{2,3},{3,2},{4,5},{5,4},{6,7},{7,6},{8,9},{9,8},{10,11... | collective-permute-start | bytes 2752520 | tf_op jit(solution)/shard_map/ppermute | solution.py:181
  82.7 7.0 %collective-permute-start.7 = (bf16[128,3584]{1,0:T(8,128)(2,1)S(1)}, bf16[128,3584]{1,0:T(8,128)(2,1)S(1)}, u32[]{:S(2)}, u32[]{:S(2)}) collective-permute-start(bf16[128,3584]{1,0:T(8,128)(2,1)S(1)} %collective-permute-done.3.first_ref), channel_id=1, source_target_pairs={{0,1},{1,0},{2,3},{3,2},{4,5},{5,4},{6,7},{7,6},{8,9},{9,8},{10,11... | collective-permute-start | bytes 2752520 | tf_op jit(solution)/shard_map/ppermute | solution.py:185
  87.6 34.0 %copy-start = (f32[1,2]{1,0:T(1,128)S(1)}, f32[1,2]{1,0:T(1,128)}, u32[]{:S(2)}) copy-start(f32[1,2]{1,0:T(1,128)} %policy_ref.1) | copy-start | bytes 28
  87.7 12.6 %collective-permute-start.8 = (f32[6,128,128]{2,1,0:T(8,128)S(1)}, f32[6,128,128]{2,1,0:T(8,128)S(1)}, u32[]{:S(2)}, u32[]{:S(2)}) collective-permute-start(f32[6,128,128]{2,1,0:T(8,128)S(1)} %get-tuple-element.23), channel_id=1, source_target_pairs={{0,2},{2,0},{1,3},{3,1},{4,6},{6,4},{5,7},{7,5},{8,10},{10,8},{9,1... | collective-permute-start | bytes 1179656 | tf_op jit(solution)/shard_map/ppermute | solution.py:183
  92.0 11.1 %collective-permute-start.9 = (f32[2,128,128]{2,1,0:T(8,128)S(1)}, f32[2,128,128]{2,1,0:T(8,128)S(1)}, u32[]{:S(2)}, u32[]{:S(2)}) collective-permute-start(f32[2,128,128]{2,1,0:T(8,128)S(1)} %get-tuple-element.24), channel_id=1, source_target_pairs={{0,2},{2,0},{1,3},{3,1},{4,6},{6,4},{5,7},{7,5},{8,10},{10,8},{9,1... | collective-permute-start | bytes 393224 | tf_op jit(solution)/shard_map/ppermute | solution.py:187
